TPU v7x, 32 devices: a whole 2x2x4 slice. The times are simulated.
32 devices in a mesh: dp: 8 (over z, x), tm: 4 (over y, core).
Axes of the slice: x: 2, y: 2, z: 4, core: 2. Of those that a mesh axis runs over, the one named last changes fastest.
Arguments:
- frames: bfloat16 [8, 3072, 1024], P('dp', 'tm'), may hold values from -18 to 18
- lengths: int32 [8], P('dp'), may hold values from 1 to 3072, 14745 in all
- w_in: bfloat16 [1024, 2048], replicated, may hold values from -4 to 4
- w_dw: float32 [31, 1024], replicated, may hold values from -1 to 1
- bn_gain: float32 [1024], replicated, may hold values from 0.25 to 1.75
- bn_bias: float32 [1024], replicated, may hold values from -1 to 1
- w_out: bfloat16 [1024, 1024], replicated, may hold values from -0.1875 to 0.1875
- cotangent: bfloat16 [8, 3072, 1024], P('dp', 'tm'), may hold values from -6 to 6
Outputs:
- output: bfloat16 [8, 3072, 1024], P('dp', 'tm')
- grad_frames: bfloat16 [8, 3072, 1024], P('dp', 'tm')
- grad_w_in: float32 [1024, 2048], P(('dp', 'tm'))
- grad_w_out: float32 [1024, 1024], P(('dp', 'tm'))
- grad_kernel: float32 [31, 1024], replicated
- grad_gain: float32 [1024], replicated
- grad_bias: float32 [1024], replicated
Inputs may be any that keep to these rules, and one draw needn't show every extreme that they name: Frame slots at or after a recording's length are padding; the lengths sum to 14745 and the longest is exactly 3072.
All inputs are finite; a program needn't handle non-finite values. No bound on the sum of `lengths` on one device may be relied on, other than what follows from the above.
Results may differ from a plain program's by a relative error of at most 0.015.
Values may be sent and summed in bfloat16 or wider, within the bound.
No kernel may reach another device: no remote copies, remote signals or barrier semaphores. Data moves between devices by JAX's collectives and lax.ppermute only.
A program may use at most 128 MiB of HBM per device.

v0:
```python
import math

import jax
import jax.numpy as jnp
from jax import lax
from jax.sharding import PartitionSpec as P


def padded_2(cells, sides, width):
    for axis, dim in sides:
        count = lax.axis_size(axis)
        ends = count - 1
        head = lax.slice_in_dim(cells, 0, width, axis=dim)
        tail = lax.slice_in_dim(cells, cells.shape[dim] - width, cells.shape[dim], axis=dim)
        cells = jnp.concatenate(
            [
                lax.ppermute(tail, axis, [(i, (i + 1) % count) for i in range(ends)]),
                cells,
                lax.ppermute(head, axis, [((i + 1) % count, i) for i in range(ends)]),
            ],
            axis=dim,
        )
    return cells


def taps_forward(padded, kernel, frame_count):
    summed = jnp.zeros((frame_count, padded.shape[1]), jnp.float32)
    for tap_index in range(kernel.shape[0]):
        summed = summed + kernel[tap_index] * padded[tap_index : tap_index + frame_count].astype(
            jnp.float32
        )
    return summed


def taps_backward(padded_grad, kernel, frame_count):
    reach_both = kernel.shape[0] - 1
    summed = jnp.zeros((frame_count, padded_grad.shape[1]), jnp.float32)
    for tap_index in range(kernel.shape[0]):
        begin = reach_both - tap_index
        summed = summed + kernel[tap_index] * padded_grad[begin : begin + frame_count].astype(
            jnp.float32
        )
    return summed


def taps_kernel(padded_glu, dconv_rows, kernel_taps, frame_count):
    grad_rows = dconv_rows.astype(jnp.float32)
    tap_rows = []
    for tap_index in range(kernel_taps):
        tap_rows.append(
            jnp.sum(
                padded_glu[tap_index : tap_index + frame_count].astype(jnp.float32) * grad_rows,
                axis=0,
            )
        )
    return jnp.stack(tap_rows)


def row_product(left_rows, right_mat, contract):
    dim_spec = (((1,), (contract,)), ((), ()))
    return lax.dot_general(left_rows, right_mat, dim_spec, preferred_element_type=jnp.float32)


def local(frames, lengths, w_in, w_dw, bn_gain, bn_bias, w_out, cotangent):
    frame_rows = frames.shape[1]
    channels = frames.shape[2]
    kernel_taps = w_dw.shape[0]
    reach = (kernel_taps - 1) // 2
    feats = frames[0]
    cot_rows = cotangent[0]
    tm_count = lax.axis_size("tm")
    device_count = lax.axis_size("dp") * tm_count
    offset = lax.axis_index("tm") * frame_rows
    limit = lengths[0]
    positions = offset + jnp.arange(frame_rows, dtype=jnp.int32)
    live_rows = (positions < limit).astype(jnp.float32)[:, None]
    contract_frames = (((0,), (0,)), ((), ()))
    pre_act = row_product(feats, w_in, 0)
    linear_half = pre_act[:, :channels]
    gate_sig = jax.nn.sigmoid(pre_act[:, channels:])
    glu_out = (linear_half * gate_sig * live_rows).astype(jnp.bfloat16)
    dswish = row_product(cot_rows, w_out, 1)
    padded = padded_2(glu_out, (("tm", 0),), reach)
    conv_out = taps_forward(padded, w_dw, frame_rows)
    local_sum = jnp.sum(conv_out * live_rows, axis=0)
    local_sq = jnp.sum(conv_out * conv_out * live_rows, axis=0)
    local_count = jnp.sum(live_rows)
    sums, squares, count = lax.psum((local_sum, local_sq, local_count), ("dp", "tm"))
    mean_vec = sums / count
    variance = squares / count - mean_vec * mean_vec
    inv_std = lax.rsqrt(variance + 1e-05)
    normed = (conv_out - mean_vec) * inv_std
    shifted = bn_gain * normed + bn_bias
    act_sig = jax.nn.sigmoid(shifted)
    swished = (shifted * act_sig * live_rows).astype(jnp.bfloat16)
    dshift = live_rows * dswish * act_sig * (1.0 + shifted * (1.0 - act_sig))
    sum_gain, sum_bias = lax.psum(
        (jnp.sum(dshift * normed, axis=0), jnp.sum(dshift, axis=0)), ("dp", "tm")
    )
    dconv = (
        live_rows * bn_gain * inv_std * (dshift - sum_bias / count - normed * sum_gain / count)
    ).astype(jnp.bfloat16)
    padded_grad = padded_2(dconv, (("tm", 0),), reach)
    dglu = live_rows * taps_backward(padded_grad, w_dw, frame_rows)
    kernel_sum = lax.psum(taps_kernel(padded, dconv, kernel_taps, frame_rows), ("dp", "tm"))
    out_rows = row_product(swished, w_out, 0).astype(jnp.bfloat16)
    dpre = jnp.concatenate(
        [dglu * gate_sig, dglu * linear_half * gate_sig * (1.0 - gate_sig)], axis=1
    ).astype(jnp.bfloat16)
    grad_rows = row_product(dpre, w_in, 1).astype(jnp.bfloat16)
    term_in = lax.dot_general(feats, dpre, contract_frames, preferred_element_type=jnp.float32)
    term_out = lax.dot_general(
        swished, cot_rows, contract_frames, preferred_element_type=jnp.float32
    )
    weight_term = jnp.concatenate([term_in, term_out], axis=1)
    weight_sum = lax.psum_scatter(weight_term, ("dp", "tm"), scatter_dimension=0, tiled=True)
    scale = 1.0 / math.sqrt(device_count * frame_rows)
    grad_w_in = weight_sum[:, : 2 * channels] * scale
    grad_w_out = weight_sum[:, 2 * channels :] * scale
    return (
        out_rows[None],
        grad_rows[None],
        grad_w_in,
        grad_w_out,
        kernel_sum * scale,
        sum_gain * scale,
        sum_bias * scale,
    )


def solution(mesh):
    placed = (P("dp", "tm", None), P("dp"), P(), P(), P(), P(), P(), P("dp", "tm", None))
    return jax.shard_map(
        local,
        mesh=mesh,
        in_specs=placed,
        out_specs=(
            P("dp", "tm", None),
            P("dp", "tm", None),
            P(("dp", "tm"), None),
            P(("dp", "tm"), None),
            P(),
            P(),
            P(),
        ),
        check_vma=False,
    )
```

profile of v0, /device:TPU:0, one launch (start us, length us, event | category | flops | bytes accessed | tf_op | source)
XLA Modules:
  0.0 474.6 jit_solution(11299279796385504885)
XLA Ops:
  8.0 5.7 %fusion.143 = f32[768,2048]{1,0:T(8,128)S(1)} fusion(bf16[1024,2048]{1,0:T(8,128)(2,1)} %param.10, bf16[1,768,1024]{2,1,0:T(8,128)(2,1)} %param.8), kind=kOutput, calls=%fused_computation.299 | convolution fusion | flops 3221225472 | bytes 12058624 | tf_op jit(solution)/shard_map/dot_general | solution.py:61
  16.4 2.5 collective-permute-start
  20.9 3.2 collective-permute-done.1
  24.1 24.4 %multiply_reduce_fusion.2 = (f32[1024]{0:T(1024)S(1)}, f32[1024]{0:T(1024)S(1)}, f32[768,1024]{1,0:T(8,128)}) fusion(f32[768]{0:T(1024)S(1)} %fusion.147, bf16[15,1024]{1,0:T(8,128)(2,1)S(1)} %collective-permute-done.1, bf16[768,1024]{1,0:T(8,128)(2,1)S(1)} %multiply_convert_fusion.4, f32[1024]{0:T(1024)S(1)} %bitcast.146, f32[1024]{0:T(1024)S(1)} %bitcast.148, ...), kind=kLoop, calls=%fused_computation.213 | loop fusion | flops 147060736 | bytes 4918272 | tf_op jit(solution)/shard_map/reduce_sum | solution.py:85
  48.6 41.9 %all-reduce.1 = (f32[1024]{0:T(1024)S(1)}, f32[]{:T(128)}, f32[1024]{0:T(1024)S(1)}) all-reduce(f32[1024]{0:T(1024)S(1)} %get-tuple-element.52, f32[]{:T(128)} %fusion.148, f32[1024]{0:T(1024)S(1)} %get-tuple-element.51), channel_id=1, replica_groups=mesh['dp'=8,'tm'=4] {'dp','tm'}, use_global_device_ids=true, to_apply=%region_5.0 | all-reduce | flops 2049 | bytes 16392 | tf_op jit(solution)/shard_map/psum | solution.py:88
  91.1 6.4 %fusion.151 = (f32[1024]{0:T(1024)S(1)}, f32[1024]{0:T(1024)S(1)}, f32[768,1024]{1,0:T(8,128)}) fusion(f32[1024]{0:T(1024)S(1)} %get-tuple-element.106, f32[768,1024]{1,0:T(8,128)} %get-tuple-element.67, f32[1024]{0:T(1024)S(1)} %get-tuple-element.105, f32[1024]{0:T(1024)S(1)} %copy-done.16, f32[1024]{0:T(1024)S(1)} %copy-done.12, ...), kind=kOutput, calls=%fused_computation.316 | convolution fusion | flops 1623193600 | bytes 9989120 | tf_op jit(solution)/shard_map/dot_general | solution.py:61
  97.6 40.6 %all-reduce = (f32[1024]{0:T(1024)S(1)}, f32[1024]{0:T(1024)S(1)}) all-reduce(f32[1024]{0:T(1024)S(1)} %get-tuple-element.58, f32[1024]{0:T(1024)S(1)} %get-tuple-element.57), channel_id=1, replica_groups=mesh['dp'=8,'tm'=4] {'dp','tm'}, use_global_device_ids=true, to_apply=%region_9.0 | all-reduce | flops 2048 | bytes 16384 | tf_op jit(solution)/shard_map/psum | solution.py:97
  139.4 15.0 %fusion.75 = (f32[1024]{0:T(1024)S(1)}, f32[1024]{0:T(1024)S(1)}, f32[1024]{0:T(1024)S(1)}, f32[1024]{0:T(1024)S(1)}, f32[1024]{0:T(1024)S(1)}, /*index=5*/f32[1024]{0:T(1024)S(1)}, bf16[768,1024]{1,0:T(8,128)(2,1)S(1)}) fusion(bf16[15,1024]{1,0:T(8,128)(2,1)S(1)} %collective-permute-done.1, bf16[768,1024]{1,0:T(8,128)(2,1)} %copy-done.1, ...), kind=kLoop, calls=%fused_computation.196 | loop fusion | flops 36956160 | bytes 9516036 | tf_op jit(solution)/shard_map/reduce_sum | solution.py:51
  155.7 3.0 collective-permute-start.3
  158.8 2.7 fusion.60
  161.5 3.2 fusion.74
  164.7 2.9 fusion.59
  167.6 3.7 fusion.76
  171.3 4.5 fusion.139
  175.8 2.7 stack.127
  178.6 40.0 %multiply_convert_fusion.1 = (bf16[768,1024]{1,0:T(8,128)(2,1)S(1)}, f32[768,1024]{1,0:T(8,128)S(1)}) fusion(f32[768,2048]{1,0:T(8,128)} %copy-done.4, bf16[768,1024]{1,0:T(8,128)(2,1)} %copy-done.3, bf16[15,1024]{1,0:T(8,128)(2,1)S(1)} %collective-permute-done.3, f32[1024]{0:T(1024)S(1)} %bitcast.147, f32[1024]{0:T(1024)S(1)} %bitcast.149, ...), kind=kLoop, calls=%fused_computation.204 | loop fusion | flops 147849216 | bytes 9628672 | tf_op jit(solution)/shard_map/convert
  218.6 4.7 multiply_convert_fusion
  223.3 3.5 convolution_bitcast_fusion
  226.8 8.0 %pad_maximum_fusion = f32[1024,3072]{0,1:T(8,128)} fusion(f32[1024,1024]{0,1:T(8,128)S(1)} %copy-done.6, f32[1024,2048]{0,1:T(8,128)S(1)} %convolution_bitcast_fusion), kind=kLoop, calls=%fused_computation.32 | loop fusion | flops 3145728 | bytes 25165824 | tf_op jit(solution)/shard_map/concatenate | solution.py:115
  234.9 12.6 %copy.19 = f32[1024,3072]{1,0:T(8,128)} copy(f32[1024,3072]{0,1:T(8,128)} %pad_maximum_fusion) | data formatting | bytes 25165824
  248.1 5.4 %fusion.146 = bf16[1,768,1024]{2,1,0:T(8,128)(2,1)} fusion(bf16[1024,1024]{1,0:T(8,128)(2,1)S(1)} %copy-done, f32[768,1024]{1,0:T(8,128)} %get-tuple-element.67, f32[1024]{0:T(1024)S(1)} %copy-done.16, f32[1024]{0:T(1024)S(1)} %get-tuple-element.106, f32[1024]{0:T(1024)S(1)} %get-tuple-element.105, f32[768]{0:T(1024)S(1)} %fusion.147, f32[1024]{0:T(1024)S(1)} %copy-done.12), kind=kOutput, calls=%fused_computation.302 | convolution fusion | flops 1619263488 | bytes 6835200 | tf_op jit(solution)/shard_map/dot_general | solution.py:61
  253.5 4.8 %fusion.145 = bf16[1,768,1024]{2,1,0:T(8,128)(2,1)} fusion(bf16[1024,2048]{1,0:T(8,128)(2,1)S(1)} %copy-done.13, bf16[768,1024]{1,0:T(8,128)(2,1)S(1)} %copy-done.10, bf16[768,1024]{1,0:T(8,128)(2,1)S(1)} %copy-done.8), kind=kOutput, calls=%fused_computation.301 | convolution fusion | flops 3228303360 | bytes 8912896 | tf_op jit(solution)/shard_map/dot_general | solution.py:61
  258.3 43.4 %all-reduce.4.cloned.1.call-done = f32[31,1024]{1,0:T(8,128)} async-done(((f32[31,1024]{1,0:T(8,128)}), f32[31,1024]{1,0:T(8,128)}) %all-reduce.4.cloned.1.call-update) | async-done | bytes 126992 | tf_op jit(solution)/shard_map/psum | solution.py:105
  303.2 158.9 %reduce-scatter.4.cloned.1.call-done = f32[32,3072]{1,0:T(8,128)} async-done(((f32[1024,3072]{1,0:T(8,128)}), f32[32,3072]{1,0:T(8,128)}) %reduce-scatter.4.cloned.1.call-update) | async-done | bytes 393232
  (63 shorter events, 15.9 us)
Async XLA Ops:
  7.2 83.9 %copy-start = (bf16[1024,1024]{1,0:T(8,128)(2,1)S(1)}, bf16[1024,1024]{1,0:T(8,128)(2,1)}, u32[]{:S(2)}) copy-start(bf16[1024,1024]{1,0:T(8,128)(2,1)} %param.14) | copy-start | bytes 6291460
  7.2 294.5 %all-reduce.4.cloned.1.call-start = ((), (), s32[]{:S(2)}) async-start(), calls=%async_computation.1 | async-start | bytes 262144 | tf_op jit(solution)/shard_map/psum | solution.py:105
  13.7 2.7 copy-start.4
  13.7 6.5 %copy-start.11 = (f32[31,1024]{1,0:T(8,128)S(1)}, f32[31,1024]{1,0:T(8,128)}, u32[]{:S(2)}) copy-start(f32[31,1024]{1,0:T(8,128)} %param.11) | copy-start | bytes 380932
  16.4 7.8 %copy-start.1 = (bf16[768,1024]{1,0:T(8,128)(2,1)}, bf16[768,1024]{1,0:T(8,128)(2,1)S(1)}, u32[]{:S(2)}) copy-start(bf16[768,1024]{1,0:T(8,128)(2,1)S(1)} %multiply_convert_fusion.4) | copy-start | bytes 4718596
  16.4 74.7 %copy-start.12 = (f32[1024]{0:T(1024)S(1)}, f32[1024]{0:T(1024)}, u32[]{:S(2)}) copy-start(f32[1024]{0:T(1024)} %param.12) | copy-start | bytes 12292
  16.4 74.7 %copy-start.16 = (f32[1024]{0:T(1024)S(1)}, f32[1024]{0:T(1024)}, u32[]{:S(2)}) copy-start(f32[1024]{0:T(1024)} %param.13) | copy-start | bytes 12292
  16.4 4.5 collective-permute-start
  18.9 5.2 %collective-permute-start.1 = (bf16[15,1024]{1,0:T(8,128)(2,1)S(1)}, bf16[15,1024]{1,0:T(8,128)(2,1)S(1)}, u32[]{:S(2)}, u32[]{:S(2)}) collective-permute-start(bf16[15,1024]{1,0:T(8,128)(2,1)S(1)} %get-tuple-element.71), channel_id=1, source_target_pairs={{1,0},{2,1},{3,2},{5,4},{6,5},{7,6},{9,8},{10,9},{11,10},{13,12},{... | collective-permute-start | bytes 92168 | tf_op jit(solution)/shard_map/ppermute | solution.py:19
  139.4 19.4 %copy-start.2 = (bf16[768,1024]{1,0:T(8,128)(2,1)S(1)}, bf16[768,1024]{1,0:T(8,128)(2,1)}, u32[]{:S(2)}) copy-start(bf16[768,1024]{1,0:T(8,128)(2,1)} %copy-done.1) | copy-start | bytes 4718596
  154.4 13.2 %copy-start.3 = (bf16[768,1024]{1,0:T(8,128)(2,1)}, bf16[768,1024]{1,0:T(8,128)(2,1)S(1)}, u32[]{:S(2)}) copy-start(bf16[768,1024]{1,0:T(8,128)(2,1)S(1)} %get-tuple-element.64) | copy-start | bytes 4718596
  154.4 24.1 %collective-permute-start.2 = (bf16[15,1024]{1,0:T(8,128)(2,1)S(1)}, bf16[15,1024]{1,0:T(8,128)(2,1)S(1)}, u32[]{:S(2)}, u32[]{:S(2)}) collective-permute-start(bf16[15,1024]{1,0:T(8,128)(2,1)S(1)} %get-tuple-element.68), channel_id=1, source_target_pairs={{1,0},{2,1},{3,2},{5,4},{6,5},{7,6},{9,8},{10,9},{11,10},{13,12},{... | collective-permute-start | bytes 92168 | tf_op jit(solution)/shard_map/ppermute | solution.py:19
  155.7 22.8 %collective-permute-start.3 = (bf16[15,1024]{1,0:T(8,128)(2,1)S(1)}, bf16[15,1024]{1,0:T(8,128)(2,1)S(1)}, u32[]{:S(2)}, u32[]{:S(2)}) collective-permute-start(bf16[15,1024]{1,0:T(8,128)(2,1)S(1)} %get-tuple-element.69), channel_id=1, source_target_pairs={{0,1},{1,2},{2,3},{4,5},{5,6},{6,7},{8,9},{9,10},{10,11},{12,13},{... | collective-permute-start | bytes 92168 | tf_op jit(solution)/shard_map/ppermute | solution.py:17
  164.7 6.6 %copy-start.5 = (f32[768,1024]{1,0:T(8,128)S(1)}, f32[768,1024]{1,0:T(8,128)}, u32[]{:S(2)}) copy-start(f32[768,1024]{1,0:T(8,128)} %get-tuple-element.67) | copy-start | bytes 9437188
  164.7 6.6 %copy-start.14 = (bf16[1,768,1024]{2,1,0:T(8,128)(2,1)S(1)}, bf16[1,768,1024]{2,1,0:T(8,128)(2,1)}, u32[]{:S(2)}) copy-start(bf16[1,768,1024]{2,1,0:T(8,128)(2,1)} %param.15) | copy-start | bytes 4718596
  178.5 283.6 %reduce-scatter.4.cloned.1.call-start = ((), (), s32[]{:S(2)}) async-start(), calls=%async_computation.2 | async-start | bytes 12976128
  218.5 4.7 copy-start.7
  218.6 4.7 copy-start.15
  223.3 3.5 copy-start.9
  223.3 3.5 copy-start.6
  248.1 5.4 %copy-start.8 = (bf16[768,1024]{1,0:T(8,128)(2,1)S(1)}, bf16[768,1024]{1,0:T(8,128)(2,1)}, u32[]{:S(2)}) copy-start(bf16[768,1024]{1,0:T(8,128)(2,1)} %copy-done.7) | copy-start | bytes 4718596
  248.1 5.4 %copy-start.10 = (bf16[768,1024]{1,0:T(8,128)(2,1)S(1)}, bf16[768,1024]{1,0:T(8,128)(2,1)}, u32[]{:S(2)}) copy-start(bf16[768,1024]{1,0:T(8,128)(2,1)} %copy-done.9) | copy-start | bytes 4718596
  248.1 5.4 %copy-start.13 = (bf16[1024,2048]{1,0:T(8,128)(2,1)S(1)}, bf16[1024,2048]{1,0:T(8,128)(2,1)}, u32[]{:S(2)}) copy-start(bf16[1024,2048]{1,0:T(8,128)(2,1)} %param.10) | copy-start | bytes 12582916
  462.1 2.1 slice-start
Sparse Core Ops, SparseCore 0:
  178.6 122.9 all-reduce.3
  307.7 154.3 reduce-scatter.3
where the time goes:
time: 475 us
  waiting for transfers between devices  205 us (43%)
  other arithmetic  111 us (23%)
  blocking collectives  82.5 us (17%)
  matrix products  30.2 us (6%)
  local copies, waits for them, and re-layouts  21.8 us (5%)
  between operations  15.2 us (3%)
  starting transfers between devices  8.19 us (2%)
    unnamed x3, waiting for transfers between devices  159 us
    another operation x2, other arithmetic  44.7 us
    psum x1, waiting for transfers between devices, local(): lax.psum(taps_kernel(padded, dconv, kernel_taps, frame_rows), ('dp', 'tm'))  43.4 us
    psum x1, blocking collectives, local(): lax.psum((local_sum, local_sq, local_count), ('dp', 'tm'))  41.9 us
    psum x1, blocking collectives, local(): lax.psum((jnp.sum(dshift * normed, axis=0), jnp.sum(dshift, axis=0)), ('d...  40.6 us
    reduce_sum x5, other arithmetic, taps_kernel(): jnp.sum(padded_glu[tap_index:tap_index + frame_count].astype(jnp.float32)...  27.5 us
    reduce_sum x1, other arithmetic, local(): local_sum = jnp.sum(conv_out * live_rows, axis=0)  24.4 us
    dot_general x4, matrix products, row_product(): lax.dot_general(left_rows, right_mat, dim_spec, preferred_element_type=jn...  22.3 us
  transfers between devices with their start and end apart: 6, of which 3 were waited for; matrix products, arithmetic and copies ran while one was open for 21% of the time, Pallas kernels for 0%

commit v1 on v0

v1 whole, which is shorter than its diff:
```python
import functools
import math

import jax
import jax.numpy as jnp
from jax import lax
from jax.experimental import pallas as pl
from jax.experimental.pallas import tpu as pltpu
from jax.sharding import PartitionSpec as P

F32 = jnp.float32
BF16 = jnp.bfloat16
LANES = 128
BLOCK = 256
SUB = BLOCK // LANES
WIDE = 32
NEAR = 16
VMEM_LIMIT = 56 << 20


def dot_nn(a, b):
    return lax.dot_general(a, b, (((1,), (0,)), ((), ())), preferred_element_type=F32)


def dot_nt(a, b):
    return lax.dot_general(a, b, (((1,), (1,)), ((), ())), preferred_element_type=F32)


def dot_tn(a, b):
    return lax.dot_general(a, b, (((0,), (0,)), ((), ())), preferred_element_type=F32)


def logistic(x):
    return 1.0 / (1.0 + jnp.exp(-x))


def row_mask(start, count, low, high):
    rows = start + lax.broadcasted_iota(jnp.int32, (count, LANES), 0)
    return (rows >= low) & (rows < high)


def taps_chunk(src, c, begin, count, weight_row, taps):
    tiles = count // 8
    sums = [None] * tiles
    for residue in range(8):
        own = list(range(residue, taps, 8))
        weights = [jnp.broadcast_to(weight_row(k), (8, LANES)) for k in own]
        for q in range(tiles + len(own) - 1):
            tile = src[c, pl.ds(begin + residue + 8 * q, 8), :]
            for i, weight in enumerate(weights):
                u = q - i
                if 0 <= u < tiles:
                    term = weight * tile
                    sums[u] = term if sums[u] is None else sums[u] + term
    return sums


def lanes_of(c):
    return slice(c * LANES, (c + 1) * LANES)


def gate_kernel(span_ref, feats_ref, lin_w_ref, gate_w_ref, glu_ref, first_ref, second_ref):
    rows = feats_ref.shape[0]
    step = 256 if rows % 256 == 0 else rows
    for r in range(0, rows, step):
        lin = dot_nn(feats_ref[r : r + step, :], lin_w_ref[...])
        sig = logistic(dot_nn(feats_ref[r : r + step, :], gate_w_ref[...]))
        for c in range(SUB):
            lin_c, sig_c = lin[:, lanes_of(c)], sig[:, lanes_of(c)]
            live = row_mask(r, step, span_ref[0], span_ref[1])
            sig_c = jnp.where(live, sig_c, 0.0)
            prod = lin_c * sig_c
            glu_ref[c, r : r + step, :] = prod.astype(BF16)
            first_ref[r : r + step, lanes_of(c)] = sig_c.astype(BF16)
            second_ref[r : r + step, lanes_of(c)] = (prod * (1.0 - sig_c)).astype(BF16)


def gated(span, feats, w_in):
    rows, depth = feats.shape
    channels = w_in.shape[1] // 2
    blocks = channels // BLOCK
    return pl.pallas_call(
        gate_kernel,
        grid=(blocks,),
        in_specs=[
            pl.BlockSpec(memory_space=pltpu.SMEM),
            pl.BlockSpec((rows, depth), lambda j: (0, 0)),
            pl.BlockSpec((depth, BLOCK), lambda j: (0, j)),
            pl.BlockSpec((depth, BLOCK), lambda j: (0, j + blocks)),
        ],
        out_specs=[
            pl.BlockSpec((SUB, rows, LANES), lambda j: (j, 0, 0)),
            pl.BlockSpec((rows, BLOCK), lambda j: (0, j)),
            pl.BlockSpec((rows, BLOCK), lambda j: (0, j)),
        ],
        out_shape=[
            jax.ShapeDtypeStruct((channels // LANES, rows, LANES), BF16),
            jax.ShapeDtypeStruct((rows, channels), BF16),
            jax.ShapeDtypeStruct((rows, channels), BF16),
        ],
        compiler_params=pltpu.CompilerParams(vmem_limit_bytes=VMEM_LIMIT),
        cost_estimate=pl.CostEstimate(
            flops=4 * rows * depth * channels, bytes_accessed=14 * rows * channels, transcendentals=rows * channels
        ),
        name="gated",
    )(span, feats, w_in, w_in)


def conv_kernel(span_ref, before_ref, after_ref, lin_w_ref, gate_w_ref, taps_ref, glu_ref, conv_ref, edge_ref, sums_ref, ext):
    rows = glu_ref.shape[1]
    taps = taps_ref.shape[0]
    full = rows + 2 * NEAR
    halo = jnp.concatenate([before_ref[...], after_ref[...]], axis=0)
    lin = dot_nn(halo, lin_w_ref[...])
    sig = logistic(dot_nn(halo, gate_w_ref[...]))
    low, high = span_ref[0], span_ref[1]
    live = jnp.concatenate([row_mask(-WIDE, WIDE, low, high), row_mask(rows, WIDE, low, high)], axis=0)
    for c in range(SUB):
        edge = jnp.where(live, lin[:, lanes_of(c)] * sig[:, lanes_of(c)], 0.0).astype(BF16)
        edge_ref[c] = edge
        edge = edge.astype(F32)
        ext[c, 0:WIDE, :] = edge[:WIDE]
        ext[c, WIDE + rows :, :] = edge[WIDE:]
        ext[c, WIDE : WIDE + rows, :] = glu_ref[c].astype(F32)
    count = 160 if full % 160 == 0 else NEAR
    own_low = jnp.maximum(low, 0) + NEAR
    own_high = jnp.minimum(high, rows) + NEAR
    shift = WIDE - NEAR - (taps - 1) // 2
    for c in range(SUB):

        def chunk(i, carry):
            r = pl.multiple_of(i * count, count)
            tiles = taps_chunk(ext, c, r + shift, count, lambda k: taps_ref[k : k + 1, lanes_of(c)], taps)
            total, square = carry
            for u, tile in enumerate(tiles):
                conv_ref[c, pl.ds(r + 8 * u, 8), :] = tile
                kept = jnp.where(row_mask(r + 8 * u, 8, own_low, own_high), tile, 0.0)
                total = total + kept
                square = square + kept * kept
            return total, square

        zero = jnp.zeros((8, LANES), F32)
        total, square = lax.fori_loop(0, full // count, chunk, (zero, zero))
        sums_ref[0:1, lanes_of(c)] = jnp.sum(total, axis=0, keepdims=True)
        sums_ref[1:2, lanes_of(c)] = jnp.sum(square, axis=0, keepdims=True)
    live_rows = jnp.maximum(own_high - own_low, 0).astype(F32)
    sums_ref[2:3, :] = jnp.full((1, BLOCK), 1.0, F32) * live_rows


def convolved(span, before, after, w_in, w_dw, glu):
    groups, rows, _ = glu.shape
    channels = groups * LANES
    depth = w_in.shape[0]
    taps = w_dw.shape[0]
    blocks = channels // BLOCK
    full = rows + 2 * NEAR
    return pl.pallas_call(
        conv_kernel,
        grid=(blocks,),
        in_specs=[
            pl.BlockSpec(memory_space=pltpu.SMEM),
            pl.BlockSpec((WIDE, depth), lambda j: (0, 0)),
            pl.BlockSpec((WIDE, depth), lambda j: (0, 0)),
            pl.BlockSpec((depth, BLOCK), lambda j: (0, j)),
            pl.BlockSpec((depth, BLOCK), lambda j: (0, j + blocks)),
            pl.BlockSpec((taps, BLOCK), lambda j: (0, j)),
            pl.BlockSpec((SUB, rows, LANES), lambda j: (j, 0, 0)),
        ],
        out_specs=[
            pl.BlockSpec((SUB, full, LANES), lambda j: (j, 0, 0)),
            pl.BlockSpec((SUB, 2 * WIDE, LANES), lambda j: (j, 0, 0)),
            pl.BlockSpec((3, BLOCK), lambda j: (0, j)),
        ],
        out_shape=[
            jax.ShapeDtypeStruct((groups, full, LANES), F32),
            jax.ShapeDtypeStruct((groups, 2 * WIDE, LANES), BF16),
            jax.ShapeDtypeStruct((3, channels), F32),
        ],
        scratch_shapes=[pltpu.VMEM((SUB, rows + 2 * WIDE, LANES), F32)],
        compiler_params=pltpu.CompilerParams(vmem_limit_bytes=VMEM_LIMIT),
        cost_estimate=pl.CostEstimate(
            flops=4 * rows * depth * channels, bytes_accessed=14 * rows * channels, transcendentals=rows * channels
        ),
        name="convolved",
    )(span, before, after, w_in, w_in, w_dw, glu)


def back_kernel(before_ref, own_ref, after_ref, w_ref, out_ref):
    rows = own_ref.shape[0]
    w = w_ref[...]
    for part, at in ((before_ref, 0), (own_ref, NEAR), (after_ref, NEAR + rows)):
        prod = dot_nt(part[...], w)
        for c in range(SUB):
            out_ref[c, at : at + part.shape[0], :] = prod[:, lanes_of(c)]


def back_projected(before, cot, after, w_out):
    rows, features = cot.shape
    channels = w_out.shape[0]
    full = rows + 2 * NEAR
    return pl.pallas_call(
        back_kernel,
        grid=(channels // BLOCK,),
        in_specs=[
            pl.BlockSpec((NEAR, features), lambda j: (0, 0)),
            pl.BlockSpec((rows, features), lambda j: (0, 0)),
            pl.BlockSpec((NEAR, features), lambda j: (0, 0)),
            pl.BlockSpec((BLOCK, features), lambda j: (j, 0)),
        ],
        out_specs=pl.BlockSpec((SUB, full, LANES), lambda j: (j, 0, 0)),
        out_shape=jax.ShapeDtypeStruct((channels // LANES, full, LANES), F32),
        compiler_params=pltpu.CompilerParams(vmem_limit_bytes=VMEM_LIMIT),
        cost_estimate=pl.CostEstimate(
            flops=2 * rows * features * channels, bytes_accessed=8 * rows * channels, transcendentals=0
        ),
        name="back_projected",
    )(before, cot, after, w_out)


def moments(sums_ref, c):
    at = lanes_of(c)
    count = sums_ref[2:3, at]
    mean = sums_ref[0:1, at] / count
    variance = sums_ref[1:2, at] / count - mean * mean
    return mean, lax.rsqrt(variance + 1e-05), count


def swish_kernel(span_ref, sums_ref, gain_ref, bias_ref, conv_ref, back_ref, swished_ref, dshift_ref, terms_ref):
    rows = swished_ref.shape[0]
    low, high = span_ref[0], span_ref[1]
    count = 128 if rows % 128 == 0 else NEAR
    for c in range(SUB):
        mean, inv_std, _ = moments(sums_ref, c)
        gain, bias = gain_ref[:, lanes_of(c)], bias_ref[:, lanes_of(c)]

        def piece(r, size):
            at = pl.ds(r, size)
            normed = (conv_ref[c, at, :] - mean) * inv_std
            shifted = gain * normed + bias
            sig = logistic(shifted)
            live = row_mask(r - NEAR, size, low, high)
            swished = jnp.where(live, shifted * sig, 0.0)
            slope = sig + swished * (1.0 - sig)
            dshift = jnp.where(live, back_ref[c, at, :] * slope, 0.0)
            dshift_ref[c, at, :] = dshift
            return normed, swished, dshift

        def chunk(i, carry):
            r = pl.multiple_of(i * count, count)
            normed, swished, dshift = piece(r + NEAR, count)
            swished_ref[pl.ds(r, count), lanes_of(c)] = swished.astype(BF16)
            by_gain, by_bias = carry
            by_gain = by_gain + jnp.sum((dshift * normed).reshape(count // 8, 8, LANES), axis=0)
            by_bias = by_bias + jnp.sum(dshift.reshape(count // 8, 8, LANES), axis=0)
            return by_gain, by_bias

        zero = jnp.zeros((8, LANES), F32)
        by_gain, by_bias = lax.fori_loop(0, rows // count, chunk, (zero, zero))
        piece(0, NEAR)
        piece(rows + NEAR, NEAR)
        terms_ref[0:1, lanes_of(c)] = jnp.sum(by_gain, axis=0, keepdims=True)
        terms_ref[1:2, lanes_of(c)] = jnp.sum(by_bias, axis=0, keepdims=True)


def swish(span, sums, gain, bias, conv, back):
    groups, full, _ = conv.shape
    rows = full - 2 * NEAR
    channels = groups * LANES
    vector = pl.BlockSpec((1, BLOCK), lambda j: (0, j))
    tall = pl.BlockSpec((SUB, full, LANES), lambda j: (j, 0, 0))
    return pl.pallas_call(
        swish_kernel,
        grid=(channels // BLOCK,),
        in_specs=[
            pl.BlockSpec(memory_space=pltpu.SMEM),
            pl.BlockSpec((3, BLOCK), lambda j: (0, j)),
            vector,
            vector,
            tall,
            tall,
        ],
        out_specs=[
            pl.BlockSpec((rows, BLOCK), lambda j: (0, j)),
            tall,
            pl.BlockSpec((2, BLOCK), lambda j: (0, j)),
        ],
        out_shape=[
            jax.ShapeDtypeStruct((rows, channels), BF16),
            jax.ShapeDtypeStruct((groups, full, LANES), F32),
            jax.ShapeDtypeStruct((2, channels), F32),
        ],
        compiler_params=pltpu.CompilerParams(vmem_limit_bytes=VMEM_LIMIT),
        cost_estimate=pl.CostEstimate(
            flops=30 * rows * channels, bytes_accessed=14 * rows * channels, transcendentals=rows * channels
        ),
        name="swish",
    )(span, sums, gain, bias, conv, back)


def grad_kernel(
    span_ref, sums_ref, terms_ref, gain_ref, taps_ref, conv_ref, dshift_ref, first_ref, second_ref, dpre_ref, dconv_ref, ext
):
    rows = first_ref.shape[0]
    taps = taps_ref.shape[0]
    full = rows + 2 * NEAR
    low, high = span_ref[0], span_ref[1]
    span = 160 if full % 160 == 0 else NEAR
    count = 128 if rows % 128 == 0 else NEAR
    shift = NEAR - (taps - 1) // 2
    for c in range(SUB):
        mean, inv_std, total = moments(sums_ref, c)
        at = lanes_of(c)
        outer = gain_ref[:, at] * inv_std
        by_gain = terms_ref[0:1, at] / total
        by_bias = terms_ref[1:2, at] / total

        @pl.loop(0, full // span)
        def _(i):
            r = pl.multiple_of(i * span, span)
            normed = (conv_ref[c, pl.ds(r, span), :] - mean) * inv_std
            value = outer * (dshift_ref[c, pl.ds(r, span), :] - by_bias - normed * by_gain)
            live = row_mask(r - NEAR, span, low, high)
            ext[c, pl.ds(r, span), :] = jnp.where(live, value, 0.0).astype(BF16).astype(F32)

        dconv_ref[c] = ext[c, NEAR : NEAR + rows, :].astype(BF16)

        @pl.loop(0, rows // count)
        def _(i):
            r = pl.multiple_of(i * count, count)
            tiles = taps_chunk(ext, c, r + shift, count, lambda k: taps_ref[taps - 1 - k : taps - k, at], taps)
            dglu = jnp.concatenate(tiles, axis=0)
            dpre_ref[0, pl.ds(r, count), at] = (dglu * first_ref[pl.ds(r, count), at].astype(F32)).astype(BF16)
            dpre_ref[1, pl.ds(r, count), at] = (dglu * second_ref[pl.ds(r, count), at].astype(F32)).astype(BF16)


def norm_grad(span, sums, terms, gain, w_dw, conv, dshift, first, second):
    groups, full, _ = conv.shape
    rows = full - 2 * NEAR
    channels = groups * LANES
    taps = w_dw.shape[0]
    tall = pl.BlockSpec((SUB, full, LANES), lambda j: (j, 0, 0))
    flat = pl.BlockSpec((rows, BLOCK), lambda j: (0, j))
    return pl.pallas_call(
        grad_kernel,
        grid=(channels // BLOCK,),
        in_specs=[
            pl.BlockSpec(memory_space=pltpu.SMEM),
            pl.BlockSpec((3, BLOCK), lambda j: (0, j)),
            pl.BlockSpec((2, BLOCK), lambda j: (0, j)),
            pl.BlockSpec((1, BLOCK), lambda j: (0, j)),
            pl.BlockSpec((taps, BLOCK), lambda j: (0, j)),
            tall,
            tall,
            flat,
            flat,
        ],
        out_specs=[
            pl.BlockSpec((2, rows, BLOCK), lambda j: (0, 0, j)),
            pl.BlockSpec((SUB, rows, LANES), lambda j: (j, 0, 0)),
        ],
        out_shape=[
            jax.ShapeDtypeStruct((2, rows, channels), BF16),
            jax.ShapeDtypeStruct((groups, rows, LANES), BF16),
        ],
        scratch_shapes=[pltpu.VMEM((SUB, full, LANES), F32)],
        compiler_params=pltpu.CompilerParams(vmem_limit_bytes=VMEM_LIMIT),
        cost_estimate=pl.CostEstimate(
            flops=70 * rows * channels, bytes_accessed=16 * rows * channels, transcendentals=0
        ),
        name="norm_grad",
    )(span, sums, terms, gain, w_dw, conv, dshift, first, second)


def tap_grad_kernel(edge_ref, glu_ref, dconv_ref, out_ref, ext, own):
    rows = glu_ref.shape[1]
    taps = out_ref.shape[0]
    shift = WIDE - (taps - 1) // 2
    tiles = 4 if rows % 32 == 0 else 2
    for c in range(SUB):
        ext[c, 0:WIDE, :] = edge_ref[c, 0:WIDE, :].astype(F32)
        ext[c, WIDE : WIDE + rows, :] = glu_ref[c].astype(F32)
        ext[c, WIDE + rows :, :] = edge_ref[c, WIDE:, :].astype(F32)
        own[c] = dconv_ref[c].astype(F32)
    for c in range(SUB):

        def chunk(i, carry):
            sums = list(carry)
            r = pl.multiple_of(i * 8 * tiles, 8 * tiles)
            grads = [own[c, pl.ds(r + 8 * m, 8), :] for m in range(tiles)]
            for offset in range(taps + 8 * (tiles - 1)):
                held = None
                for m in range(tiles):
                    k = offset - 8 * m
                    if 0 <= k < taps:
                        if held is None:
                            held = ext[c, pl.ds(r + shift + offset, 8), :]
                        sums[k] = sums[k] + held * grads[m]
            return tuple(sums)

        zero = jnp.zeros((8, LANES), F32)
        sums = lax.fori_loop(0, rows // (8 * tiles), chunk, (zero,) * taps)
        for k in range(taps):
            out_ref[k : k + 1, lanes_of(c)] = jnp.sum(sums[k], axis=0, keepdims=True)


def tap_grad(edge, glu, dconv, taps):
    groups, rows, _ = glu.shape
    channels = groups * LANES
    return pl.pallas_call(
        tap_grad_kernel,
        grid=(channels // BLOCK,),
        in_specs=[
            pl.BlockSpec((SUB, 2 * WIDE, LANES), lambda j: (j, 0, 0)),
            pl.BlockSpec((SUB, rows, LANES), lambda j: (j, 0, 0)),
            pl.BlockSpec((SUB, rows, LANES), lambda j: (j, 0, 0)),
        ],
        out_specs=pl.BlockSpec((taps, BLOCK), lambda j: (0, j)),
        out_shape=jax.ShapeDtypeStruct((taps, channels), F32),
        scratch_shapes=[
            pltpu.VMEM((SUB, rows + 2 * WIDE, LANES), F32),
            pltpu.VMEM((SUB, rows, LANES), F32),
        ],
        compiler_params=pltpu.CompilerParams(vmem_limit_bytes=VMEM_LIMIT),
        cost_estimate=pl.CostEstimate(flops=62 * rows * channels, bytes_accessed=4 * rows * channels, transcendentals=0),
        name="tap_grad",
    )(edge, glu, dconv)


def frames_grad_kernel(dpre_ref, w_ref, out_ref):
    channels = dpre_ref.shape[2]
    total = dot_nt(dpre_ref[0], w_ref[:, :channels]) + dot_nt(dpre_ref[1], w_ref[:, channels:])
    out_ref[...] = total.astype(BF16)


def frames_grad(dpre, w_in):
    _, rows, channels = dpre.shape
    depth = w_in.shape[0]
    return pl.pallas_call(
        frames_grad_kernel,
        grid=(depth // BLOCK,),
        in_specs=[
            pl.BlockSpec((2, rows, channels), lambda j: (0, 0, 0)),
            pl.BlockSpec((BLOCK, 2 * channels), lambda j: (j, 0)),
        ],
        out_specs=pl.BlockSpec((rows, BLOCK), lambda j: (0, j)),
        out_shape=jax.ShapeDtypeStruct((rows, depth), BF16),
        compiler_params=pltpu.CompilerParams(vmem_limit_bytes=VMEM_LIMIT),
        cost_estimate=pl.CostEstimate(
            flops=4 * rows * depth * channels, bytes_accessed=10 * rows * depth, transcendentals=0
        ),
        name="frames_grad",
    )(dpre, w_in)


def weight_kernel(owner_rows, core_ref, left_ref, right_ref, send_ref, keep_ref):
    term = dot_tn(left_ref[...], right_ref[0])
    depth, width = term.shape
    term = term.reshape(depth // (2 * owner_rows), 2, owner_rows, width)
    even = term[:, 0].reshape(depth // 2, width)
    odd = term[:, 1].reshape(depth // 2, width)
    is_odd = core_ref[0] == 1
    send_ref[...] = jnp.where(is_odd, even, odd).astype(BF16)
    keep_ref[...] = jnp.where(is_odd, odd, even).astype(BF16)


def weight_term(core, left, right, owner_rows):
    halves, rows, width = right.shape
    depth = left.shape[1]
    step = 512
    per = width // step
    out = pl.BlockSpec((depth // 2, step), lambda j: (0, j))
    shape = jax.ShapeDtypeStruct((depth // 2, halves * width), BF16)
    return pl.pallas_call(
        functools.partial(weight_kernel, owner_rows),
        grid=(halves * per,),
        in_specs=[
            pl.BlockSpec(memory_space=pltpu.SMEM),
            pl.BlockSpec((rows, depth), lambda j: (0, 0)),
            pl.BlockSpec((1, rows, step), lambda j: (j // per, 0, j % per)),
        ],
        out_specs=[out, out],
        out_shape=[shape, shape],
        compiler_params=pltpu.CompilerParams(vmem_limit_bytes=VMEM_LIMIT),
        cost_estimate=pl.CostEstimate(
            flops=2 * halves * rows * depth * width, bytes_accessed=6 * halves * rows * width, transcendentals=0
        ),
        name="weight_term",
    )(core, left, right)


def swap(x, axis, mask):
    return lax.ppermute(x, axis, [(i, i ^ mask) for i in range(lax.axis_size(axis))])


def masks_of(axis):
    return [1 << i for i in range((lax.axis_size(axis) - 1).bit_length())]


def all_sum(x):
    for axis in ("tm", "dp"):
        for mask in masks_of(axis):
            x = x + swap(x, axis, mask)
    return x


def halve_rest(part, order, bits):
    left = list(bits)
    for axis, mask in order:
        dim = left.index((axis, mask))
        mine = (lax.axis_index(axis) & mask) != 0
        low = lax.index_in_dim(part, 0, dim, keepdims=False)
        high = lax.index_in_dim(part, 1, dim, keepdims=False)
        got = swap(jnp.where(mine, low, high), axis, mask)
        part = jnp.where(mine, high, low).astype(F32) + got.astype(F32)
        left.pop(dim)
        if left:
            part = part.astype(BF16)
    return part


def scatter_sum(send, keep, owner_rows):
    bits = [("dp", m) for m in reversed(masks_of("dp"))] + [("tm", m) for m in reversed(masks_of("tm")[1:])]
    got = swap(send, "tm", 1)
    both = (keep.astype(F32) + got.astype(F32)).astype(BF16)
    width = both.shape[1]
    both = both.reshape((2,) * len(bits) + (owner_rows, width))
    along_y = [("tm", m) for m in masks_of("tm")[1:]]
    along = [("dp", m) for m in masks_of("dp")]
    orders = [
        along_y + along,
        along[:1] + along_y + along[1:],
        along[1:2] + along_y + along[:1] + along[2:],
    ]
    tiles = width // LANES
    cuts = [0, -(-3 * tiles // 8) * LANES, 2 * -(-3 * tiles // 8) * LANES, width]
    parts = [halve_rest(both[..., a:b], order, bits) for a, b, order in zip(cuts, cuts[1:], orders)]
    return jnp.concatenate(parts, axis=1)


def local(frames, lengths, w_in, w_dw, bn_gain, bn_bias, w_out, cotangent):
    feats, cot = frames[0], cotangent[0]
    rows, depth = feats.shape
    taps = w_dw.shape[0]
    tm_count = lax.axis_size("tm")
    device_count = lax.axis_size("dp") * tm_count
    owner_rows = depth // device_count
    place = lax.axis_index("tm")
    offset = place * rows
    span = jnp.stack([-offset, lengths[0] - offset]).astype(jnp.int32)
    core = (place & 1).astype(jnp.int32).reshape(1)
    gain, bias = bn_gain[None], bn_bias[None]

    tail = jnp.concatenate([feats[rows - WIDE :], cot[rows - NEAR :]], axis=0)
    head = jnp.concatenate([feats[:WIDE], cot[:NEAR]], axis=0)
    before = lax.ppermute(tail, "tm", [(i, i + 1) for i in range(tm_count - 1)])
    after = lax.ppermute(head, "tm", [(i + 1, i) for i in range(tm_count - 1)])

    glu, first, second = gated(span, feats, w_in)
    conv, edge, sums = convolved(span, before[:WIDE], after[:WIDE], w_in, w_dw, glu)
    sums = all_sum(sums)
    back = back_projected(before[WIDE:], cot, after[WIDE:], w_out)
    swished, dshift, terms = swish(span, sums, gain, bias, conv, back)
    terms = all_sum(terms)
    out_rows = dot_nn(swished, w_out).astype(BF16)
    grad_w_out = scatter_sum(*weight_term(core, swished, cotangent, owner_rows), owner_rows)
    dpre, dconv = norm_grad(span, sums, terms, gain, w_dw, conv, dshift, first, second)
    kernel_sum = lax.psum(tap_grad(edge, glu, dconv, taps), ("dp", "tm"))
    grad_w_in = scatter_sum(*weight_term(core, feats, dpre, owner_rows), owner_rows)
    grad_rows = frames_grad(dpre, w_in)
    scale = 1.0 / math.sqrt(device_count * rows)
    return (
        out_rows[None],
        grad_rows[None],
        grad_w_in * scale,
        grad_w_out * scale,
        kernel_sum * scale,
        terms[0] * scale,
        terms[1] * scale,
    )


def solution(mesh):
    placed = (P("dp", "tm", None), P("dp"), P(), P(), P(), P(), P(), P("dp", "tm", None))
    return jax.shard_map(
        local,
        mesh=mesh,
        in_specs=placed,
        out_specs=(
            P("dp", "tm", None),
            P("dp", "tm", None),
            P(("dp", "tm"), None),
            P(("dp", "tm"), None),
            P(),
            P(),
            P(),
        ),
        check_vma=False,
    )
```

time: 475 us -> 315 us (0.66)
  other arithmetic: 111 us -> 11 us
  blocking collectives: 82.5 us -> 0 us
  Pallas kernels: 0 us -> 77.9 us
  waiting for transfers between devices: 205 us -> 145 us
  starting transfers between devices: 8.19 us -> 56.4 us
  matrix products: 30.2 us -> 4.34 us
  local copies, waits for them, and re-layouts: 21.8 us -> 4.48 us
    unnamed x3 -> x1, waiting for transfers between devices: 159 us -> 0.02 us
    psum x2 -> x0, blocking collectives: 82.5 us -> none  [the longest x1 41.9 us: local(): lax.psum((local_sum, local_sq, local_count), ('dp', 'tm'))]
    pallas_call x0 -> x9, Pallas kernels: none -> 77.9 us  [the longest x1 13.4 us: norm_grad(): pl.pallas_call(grad_kernel, grid=(channels // BLOCK,), in_specs=[pl.Block...]
    psum x1, waiting for transfers between devices: 43.4 us -> 108 us  [local(): kernel_sum = lax.psum(tap_grad(edge, glu, dconv, taps), ('dp', 'tm'))]
    reduce_sum x7 -> x0, other arithmetic: 52.5 us -> none  [the longest x5 27.5 us: taps_kernel(): jnp.sum(padded_glu[tap_index:tap_index + frame_count].astype(jnp.float32)...]
    ppermute x4 -> x38, starting transfers between devices: 8.11 us -> 56.3 us  [the longest x36 52.7 us: swap(): lax.ppermute(x, axis, [(i, i ^ mask) for i in range(lax.axis_size(axis))])]
    another operation x2 -> x1, other arithmetic: 44.7 us -> 0.61 us  [local(): span = jnp.stack([-offset, lengths[0] - offset]).astype(jnp.int32)]
    ppermute x4 -> x38, waiting for transfers between devices: 3.21 us -> 36.8 us  [the longest x36 36.8 us: swap(): lax.ppermute(x, axis, [(i, i ^ mask) for i in range(lax.axis_size(axis))])]
  transfers between devices with their start and end apart: 6 -> 39, of which waited for: 3 -> 26; matrix products, arithmetic and copies ran while one was open for 21% -> 4% of each run, Pallas kernels for 0% -> 19%
where the time goes in v1:
time: 315 us; the launch traced here: 314 us
  waiting for transfers between devices  145 us (46%)
  Pallas kernels  77.9 us (25%)
  starting transfers between devices  56.4 us (18%)
  between operations  15.1 us (5%)
  other arithmetic  11 us (3%)
  local copies, waits for them, and re-layouts  4.48 us (1%)
  matrix products  4.34 us (1%)
    psum x1, waiting for transfers between devices, local(): kernel_sum = lax.psum(tap_grad(edge, glu, dconv, taps), ('dp', 'tm'))  108 us
    ppermute x36, starting transfers between devices, swap(): lax.ppermute(x, axis, [(i, i ^ mask) for i in range(lax.axis_size(axis))])  52.7 us
    ppermute x36, waiting for transfers between devices, swap(): lax.ppermute(x, axis, [(i, i ^ mask) for i in range(lax.axis_size(axis))])  36.8 us
    pallas_call x1, Pallas kernels, norm_grad(): pl.pallas_call(grad_kernel, grid=(channels // BLOCK,), in_specs=[pl.Block...  13.4 us
    pallas_call x1, Pallas kernels, convolved(): pl.pallas_call(conv_kernel, grid=(blocks,), in_specs=[pl.BlockSpec(memory...  12.3 us
    pallas_call x2, Pallas kernels, weight_term(): pl.pallas_call(functools.partial(weight_kernel, owner_rows), grid=(halves...  12.2 us
    pallas_call x1, Pallas kernels, tap_grad(): pl.pallas_call(tap_grad_kernel, grid=(channels // BLOCK,), in_specs=[pl.B...  10.8 us
    pallas_call x1, Pallas kernels, gated(): pl.pallas_call(gate_kernel, grid=(blocks,), in_specs=[pl.BlockSpec(memory...  8.08 us
  transfers between devices with their start and end apart: 39, of which 26 were waited for; matrix products, arithmetic and copies ran while one was open for 4% of the time, Pallas kernels for 19%

profile of v1, /device:TPU:0, one launch (start us, length us, event | category | flops | bytes accessed | tf_op | source)
XLA Modules:
  0.0 314.0 jit_solution(10069103145448852490)
XLA Ops:
  8.9 2.4 collective-permute-start
  13.8 8.1 %gated.1 = (bf16[8,768,128]{2,1,0:T(8,128)(2,1)}, bf16[768,1024]{1,0:T(8,128)(2,1)}, bf16[768,1024]{1,0:T(8,128)(2,1)}) custom-call(s32[2]{0:T(128)} %pad_add_fusion.span_ref, bf16[768,1024]{1,0:T(8,128)(2,1)} %bitcast.155, bf16[1024,2048]{1,0:T(8,128)(2,1)} %w_ref.3, bf16[1024,2048]{1,0:T(8,128)(2,1)} %w_ref.3), custom_call_target="tpu_custom_call" | custom-call | flops 3221225472 | bytes 11010048 | tf_op jit(solution)/shard_map/gated/pallas_call | solution.py:82
  23.2 12.3 %convolved.1 = (f32[8,800,128]{2,1,0:T(8,128)}, bf16[8,64,128]{2,1,0:T(8,128)(2,1)}, f32[3,1024]{1,0:T(4,128)}) custom-call(s32[2]{0:T(128)} %pad_add_fusion.span_ref, bf16[32,1024]{1,0:T(8,128)(2,1)} %slice.266.before_ref, bf16[32,1024]{1,0:T(8,128)(2,1)} %slice.267.after_ref, bf16[1024,2048]{1,0:T(8,128)(2,1)} %w_ref.3, bf16[1024,2048]{1,0:T(8,128)(2,1)} %w_ref.3, ...), custom_call_target="tpu_custom_call" | custom-call | flops 3221225472 | bytes 11010048 | tf_op jit(solution)/shard_map/convolved/pallas_call | solution.py:157
  35.5 3.3 %collective-permute-start.2 = (f32[3,1024]{1,0:T(4,128)}, f32[3,1024]{1,0:T(4,128)S(1)}, u32[]{:S(2)}, u32[]{:S(2)}) collective-permute-start(f32[3,1024]{1,0:T(4,128)} %get-tuple-element.23), channel_id=1, source_target_pairs={{0,1},{1,0},{2,3},{3,2},{4,5},{5,4},{6,7},{7,6},{8,9},{9,8},{10,11... | collective-permute-start | bytes 36872 | tf_op jit(solution)/shard_map/ppermute | solution.py:492
  40.6 2.0 collective-permute-start.3
  45.8 2.3 collective-permute-done.4
  51.8 2.6 collective-permute-start.6
  54.4 6.4 %back_projected.1.back_ref = f32[8,800,128]{2,1,0:T(8,128)} custom-call(bf16[16,1024]{1,0:T(8,128)(2,1)} %slice.268.before_ref, bf16[768,1024]{1,0:T(8,128)(2,1)} %bitcast.152, bf16[16,1024]{1,0:T(8,128)(2,1)} %slice.269.after_ref, bf16[1024,1024]{1,0:T(8,128)(2,1)} %w_ref.2), custom_call_target="tpu_custom_call" | custom-call | flops 1610612736 | bytes 6291456 | tf_op jit(solution)/shard_map/back_projected/pallas_call | solution.py:201
  61.4 7.3 %swish.1 = (bf16[768,1024]{1,0:T(8,128)(2,1)}, f32[8,800,128]{2,1,0:T(8,128)}, f32[2,1024]{1,0:T(2,128)}) custom-call(s32[2]{0:T(128)} %pad_add_fusion.span_ref, f32[3,1024]{1,0:T(4,128)} %add.114.sums_ref, f32[1,1024]{1,0:T(1,128)} %bitcast.153, f32[1,1024]{1,0:T(1,128)} %bitcast.159, f32[8,800,128]{2,1,0:T(8,128)} %get-tuple-element.24.conv_ref, ...), custom_call_target="tpu_custom_call" | custom-call | flops 23592960 | bytes 11010048 | tf_op jit(solution)/shard_map/swish/pallas_call | solution.py:271
  70.8 2.0 collective-permute-start.8
  76.0 2.2 collective-permute-done.9
  79.7 4.3 %fusion = bf16[1,768,1024]{2,1,0:T(8,128)(2,1)} fusion(bf16[768,1024]{1,0:T(8,128)(2,1)} %get-tuple-element.25.left_ref, bf16[1024,1024]{1,0:T(8,128)(2,1)S(1)} %copy-done.1), kind=kOutput, calls=%fused_computation.3 | convolution fusion | flops 1611399168 | bytes 5242880 | tf_op jit(solution)/shard_map/dot_general | solution.py:22
  84.5 4.7 %weight_term.3 = (bf16[512,1024]{1,0:T(8,128)(2,1)}, bf16[512,1024]{1,0:T(8,128)(2,1)}) custom-call(s32[1]{0:T(128)} %bitcast.13.core_ref, bf16[768,1024]{1,0:T(8,128)(2,1)} %get-tuple-element.25.left_ref, bf16[1,768,1024]{2,1,0:T(8,128)(2,1)} %right_ref.1), custom_call_target="tpu_custom_call" | custom-call | flops 1610612736 | bytes 4718592 | tf_op jit(solution)/shard_map/weight_term/pallas_call | solution.py:473
  89.8 13.4 %norm_grad.1 = (bf16[2,768,1024]{2,1,0:T(8,128)(2,1)}, bf16[8,768,128]{2,1,0:T(8,128)(2,1)}) custom-call(s32[2]{0:T(128)} %pad_add_fusion.span_ref, f32[3,1024]{1,0:T(4,128)} %add.114.sums_ref, f32[2,1024]{1,0:T(2,128)} %add.119.terms_ref, f32[1,1024]{1,0:T(1,128)} %bitcast.154, f32[31,1024]{1,0:T(8,128)} %taps_ref.3, ...), custom_call_target="tpu_custom_call" | custom-call | flops 55050240 | bytes 12582912 | tf_op jit(solution)/shard_map/norm_grad/pallas_call | solution.py:343
  103.2 10.8 %tap_grad.1 = f32[31,1024]{1,0:T(8,128)} custom-call(bf16[8,64,128]{2,1,0:T(8,128)(2,1)} %get-tuple-element.35.edge_ref, bf16[8,768,128]{2,1,0:T(8,128)(2,1)} %get-tuple-element.22.glu_ref, bf16[8,768,128]{2,1,0:T(8,128)(2,1)} %get-tuple-element.36.dconv_ref), custom_call_target="tpu_custom_call" | custom-call | flops 48758784 | bytes 3145728 | tf_op jit(solution)/shard_map/tap_grad/pallas_call | solution.py:409
  114.1 7.5 %frames_grad.1 = bf16[768,1024]{1,0:T(8,128)(2,1)} custom-call(bf16[2,768,1024]{2,1,0:T(8,128)(2,1)} %get-tuple-element.30.dpre_ref.right_ref, bf16[1024,2048]{1,0:T(8,128)(2,1)} %w_ref.3), custom_call_target="tpu_custom_call" | custom-call | flops 3221225472 | bytes 7864320 | tf_op jit(solution)/shard_map/frames_grad/pallas_call | solution.py:438
  121.5 7.4 %weight_term.2 = (bf16[512,2048]{1,0:T(8,128)(2,1)}, bf16[512,2048]{1,0:T(8,128)(2,1)}) custom-call(s32[1]{0:T(128)} %bitcast.13.core_ref, bf16[768,1024]{1,0:T(8,128)(2,1)} %bitcast.156, bf16[2,768,1024]{2,1,0:T(8,128)(2,1)} %get-tuple-element.30.dpre_ref.right_ref), custom_call_target="tpu_custom_call" | custom-call | flops 3221225472 | bytes 9437184 | tf_op jit(solution)/shard_map/weight_term/pallas_call | solution.py:473
  130.1 108.0 %all-reduce.2.cloned.1.call-done = f32[31,1024]{1,0:T(8,128)} async-done(((f32[31,1024]{1,0:T(8,128)}), f32[31,1024]{1,0:T(8,128)}) %all-reduce.2.cloned.1.call-update) | async-done | bytes 126992 | tf_op jit(solution)/shard_map/psum | solution.py:567
  257.9 2.0 collective-permute-done.37
  275.6 3.3 %collective-permute-done.21 = bf16[2,2,2,32,512]{4,3,0,1,2:T(8,128)(2,1)S(1)} collective-permute-done((bf16[2,2,2,32,512]{4,3,0,1,2:T(8,128)(2,1)S(1)}, bf16[2,2,2,32,512]{4,3,0,1,2:T(8,128)(2,1)S(1)}, u32[]{:S(2)}, u32[]{:S(2)}) %collective-permute-start.21) | collective-permute-done | bytes 262176 | tf_op jit(solution)/shard_map/ppermute | solution.py:492
  281.7 2.4 collective-permute-done.22
  293.9 2.3 collective-permute-start.15
  298.9 2.2 collective-permute-start.16
  304.0 2.4 collective-permute-done.20
  (152 shorter events, 77.4 us)
Async XLA Ops:
  7.2 230.9 %all-reduce.2.cloned.1.call-start = ((), (), s32[]{:S(2)}) async-start(), calls=%async_computation | async-start | bytes 262144 | tf_op jit(solution)/shard_map/psum | solution.py:567
  8.9 13.0 %collective-permute-start = (bf16[48,1024]{1,0:T(8,128)(2,1)S(1)}, bf16[48,1024]{1,0:T(8,128)(2,1)S(1)}, u32[]{:S(2)}, u32[]{:S(2)}) collective-permute-start(bf16[48,1024]{1,0:T(8,128)(2,1)S(1)} %pad_maximum_fusion), channel_id=1, source_target_pairs={{0,1},{1,2},{2,3},{4,5},{5,6},{6,7},{8,9},{9,10},{10,11},{12,13},{... | collective-permute-start | bytes 294920 | tf_op jit(solution)/shard_map/ppermute | solution.py:555
  11.3 11.3 %collective-permute-start.1 = (bf16[48,1024]{1,0:T(8,128)(2,1)S(1)}, bf16[48,1024]{1,0:T(8,128)(2,1)S(1)}, u32[]{:S(2)}, u32[]{:S(2)}) collective-permute-start(bf16[48,1024]{1,0:T(8,128)(2,1)S(1)} %pad_maximum_fusion.1), channel_id=1, source_target_pairs={{1,0},{2,1},{3,2},{5,4},{6,5},{7,6},{9,8},{10,9},{11,10},{13,12},{... | collective-permute-start | bytes 294920 | tf_op jit(solution)/shard_map/ppermute | solution.py:556
  51.8 9.0 %collective-permute-start.6 = (f32[3,1024]{1,0:T(4,128)S(1)}, f32[3,1024]{1,0:T(4,128)S(1)}, u32[]{:S(2)}, u32[]{:S(2)}) collective-permute-start(f32[3,1024]{1,0:T(4,128)S(1)} %add.113), channel_id=1, source_target_pairs={{0,16},{4,20},{8,24},{12,28},{16,0},{20,4},{24,8},{28,12},{1,17},{... | collective-permute-start | bytes 36872 | tf_op jit(solution)/shard_map/ppermute | solution.py:492
  78.1 5.9 %collective-permute-start.10 = (f32[2,1024]{1,0:T(2,128)S(1)}, f32[2,1024]{1,0:T(2,128)S(1)}, u32[]{:S(2)}, u32[]{:S(2)}) collective-permute-start(f32[2,1024]{1,0:T(2,128)S(1)} %add.117), channel_id=1, source_target_pairs={{0,8},{4,12},{8,0},{12,4},{16,24},{20,28},{24,16},{28,20},{1,9},{5... | collective-permute-start | bytes 24584 | tf_op jit(solution)/shard_map/ppermute | solution.py:492
  84.1 5.1 %collective-permute-start.11 = (f32[2,1024]{1,0:T(2,128)S(1)}, f32[2,1024]{1,0:T(2,128)S(1)}, u32[]{:S(2)}, u32[]{:S(2)}) collective-permute-start(f32[2,1024]{1,0:T(2,128)S(1)} %add.118), channel_id=1, source_target_pairs={{0,16},{4,20},{8,24},{12,28},{16,0},{20,4},{24,8},{28,12},{1,17},{... | collective-permute-start | bytes 24584 | tf_op jit(solution)/shard_map/ppermute | solution.py:492
  89.2 150.4 %collective-permute-start.25 = (bf16[512,1024]{1,0:T(8,128)(2,1)}, bf16[512,1024]{1,0:T(8,128)(2,1)}, u32[]{:S(2)}, u32[]{:S(2)}) collective-permute-start(bf16[512,1024]{1,0:T(8,128)(2,1)} %get-tuple-element.34), channel_id=1, source_target_pairs={{0,1},{1,0},{2,3},{3,2},{4,5},{5,4},{6,7},{7,6},{8,9},{9,8},{10,11... | collective-permute-start | bytes 3145736 | tf_op jit(solution)/shard_map/ppermute | solution.py:492
  129.6 141.9 %collective-permute-start.12 = (bf16[512,2048]{1,0:T(8,128)(2,1)}, bf16[512,2048]{1,0:T(8,128)(2,1)S(1)}, u32[]{:S(2)}, u32[]{:S(2)}) collective-permute-start(bf16[512,2048]{1,0:T(8,128)(2,1)} %get-tuple-element.32), channel_id=1, source_target_pairs={{0,1},{1,0},{2,3},{3,2},{4,5},{5,4},{6,7},{7,6},{8,9},{9,8},{10,11... | collective-permute-start | bytes 6291464 | tf_op jit(solution)/shard_map/ppermute | solution.py:492
  241.4 5.0 %collective-permute-start.34 = (bf16[2,2,2,32,256]{4,3,0,1,2:T(8,128)(2,1)S(1)}, bf16[2,2,2,32,256]{4,3,0,1,2:T(8,128)(2,1)S(1)}, u32[]{:S(2)}, u32[]{:S(2)}) collective-permute-start(bf16[2,2,2,32,256]{4,3,0,1,2:T(8,128)(2,1)S(1)} %select_bitcast_fusion.7), channel_id=1, source_target_pairs={{0,8},{4,12},{8,0},{12,4},{16,24},{20,28},{24,16},{28,20},{1,9},{5... | collective-permute-start | bytes 393224 | tf_op jit(solution)/shard_map/ppermute | solution.py:492
  242.9 9.5 %collective-permute-start.26 = (bf16[2,2,2,32,384]{4,3,0,1,2:T(8,128)(2,1)S(1)}, bf16[2,2,2,32,384]{4,3,0,1,2:T(8,128)(2,1)S(1)}, u32[]{:S(2)}, u32[]{:S(2)}) collective-permute-start(bf16[2,2,2,32,384]{4,3,0,1,2:T(8,128)(2,1)S(1)} %select_bitcast_fusion.4), channel_id=1, source_target_pairs={{0,2},{1,3},{2,0},{3,1},{4,6},{5,7},{6,4},{7,5},{8,10},{9,11},{10,... | collective-permute-start | bytes 589832 | tf_op jit(solution)/shard_map/ppermute | solution.py:492
  248.0 6.8 %collective-permute-start.30 = (bf16[2,2,2,32,384]{4,3,0,1,2:T(8,128)(2,1)S(1)}, bf16[2,2,2,32,384]{4,3,0,1,2:T(8,128)(2,1)S(1)}, u32[]{:S(2)}, u32[]{:S(2)}) collective-permute-start(bf16[2,2,2,32,384]{4,3,0,1,2:T(8,128)(2,1)S(1)} %select_bitcast_fusion.3), channel_id=1, source_target_pairs={{0,4},{4,0},{8,12},{12,8},{16,20},{20,16},{24,28},{28,24},{1,5},{5... | collective-permute-start | bytes 589832 | tf_op jit(solution)/shard_map/ppermute | solution.py:492
  252.5 7.4 %collective-permute-start.27 = (bf16[2,2,32,384]{3,2,0,1:T(8,128)(2,1)S(1)}, bf16[2,2,32,384]{3,2,0,1:T(8,128)(2,1)S(1)}, u32[]{:S(2)}, u32[]{:S(2)}) collective-permute-start(bf16[2,2,32,384]{3,2,0,1:T(8,128)(2,1)S(1)} %select_bitcast_fusion.10), channel_id=1, source_target_pairs={{0,4},{4,0},{8,12},{12,8},{16,20},{20,16},{24,28},{28,24},{1,5},{5... | collective-permute-start | bytes 294920 | tf_op jit(solution)/shard_map/ppermute | solution.py:492
  264.4 4.9 %collective-permute-start.29 = (bf16[32,384]{1,0:T(8,128)(2,1)S(1)}, bf16[32,384]{1,0:T(8,128)(2,1)S(1)}, u32[]{:S(2)}, u32[]{:S(2)}) collective-permute-start(bf16[32,384]{1,0:T(8,128)(2,1)S(1)} %select_bitcast_fusion.22), channel_id=1, source_target_pairs={{0,16},{4,20},{8,24},{12,28},{16,0},{20,4},{24,8},{28,12},{1,17},{... | collective-permute-start | bytes 73736 | tf_op jit(solution)/shard_map/ppermute | solution.py:492
  265.8 4.9 %collective-permute-start.33 = (bf16[32,384]{1,0:T(8,128)(2,1)S(1)}, bf16[32,384]{1,0:T(8,128)(2,1)S(1)}, u32[]{:S(2)}, u32[]{:S(2)}) collective-permute-start(bf16[32,384]{1,0:T(8,128)(2,1)S(1)} %select_bitcast_fusion.21), channel_id=1, source_target_pairs={{0,16},{4,20},{8,24},{12,28},{16,0},{20,4},{24,8},{28,12},{1,17},{... | collective-permute-start | bytes 73736 | tf_op jit(solution)/shard_map/ppermute | solution.py:492
  272.5 6.4 %collective-permute-start.21 = (bf16[2,2,2,32,512]{4,3,0,1,2:T(8,128)(2,1)S(1)}, bf16[2,2,2,32,512]{4,3,0,1,2:T(8,128)(2,1)S(1)}, u32[]{:S(2)}, u32[]{:S(2)}) collective-permute-start(bf16[2,2,2,32,512]{4,3,0,1,2:T(8,128)(2,1)S(1)} %select_bitcast_fusion.2), channel_id=1, source_target_pairs={{0,8},{4,12},{8,0},{12,4},{16,24},{20,28},{24,16},{28,20},{1,9},{5... | collective-permute-start | bytes 786440 | tf_op jit(solution)/shard_map/ppermute | solution.py:492
  274.4 11.1 %collective-permute-start.13 = (bf16[2,2,2,32,768]{4,3,0,1,2:T(8,128)(2,1)S(1)}, bf16[2,2,2,32,768]{4,3,0,1,2:T(8,128)(2,1)S(1)}, u32[]{:S(2)}, u32[]{:S(2)}) collective-permute-start(bf16[2,2,2,32,768]{4,3,0,1,2:T(8,128)(2,1)S(1)} %select_bitcast_fusion.1), channel_id=1, source_target_pairs={{0,2},{1,3},{2,0},{3,1},{4,6},{5,7},{6,4},{7,5},{8,10},{9,11},{10,... | collective-permute-start | bytes 1179656 | tf_op jit(solution)/shard_map/ppermute | solution.py:492
  279.1 5.0 %collective-permute-start.22 = (bf16[2,2,32,512]{3,2,0,1:T(8,128)(2,1)S(1)}, bf16[2,2,32,512]{3,2,0,1:T(8,128)(2,1)S(1)}, u32[]{:S(2)}, u32[]{:S(2)}) collective-permute-start(bf16[2,2,32,512]{3,2,0,1:T(8,128)(2,1)S(1)} %select_bitcast_fusion.8), channel_id=1, source_target_pairs={{0,2},{1,3},{2,0},{3,1},{4,6},{5,7},{6,4},{7,5},{8,10},{9,11},{10,... | collective-permute-start | bytes 393224 | tf_op jit(solution)/shard_map/ppermute | solution.py:492
  280.3 7.8 %collective-permute-start.17 = (bf16[2,2,2,32,768]{4,3,0,1,2:T(8,128)(2,1)S(1)}, bf16[2,2,2,32,768]{4,3,0,1,2:T(8,128)(2,1)S(1)}, u32[]{:S(2)}, u32[]{:S(2)}) collective-permute-start(bf16[2,2,2,32,768]{4,3,0,1,2:T(8,128)(2,1)S(1)} %select_bitcast_fusion), channel_id=1, source_target_pairs={{0,4},{4,0},{8,12},{12,8},{16,20},{20,16},{24,28},{28,24},{1,5},{5... | collective-permute-start | bytes 1179656 | tf_op jit(solution)/shard_map/ppermute | solution.py:492
  285.7 8.2 %collective-permute-start.14 = (bf16[2,2,32,768]{3,2,0,1:T(8,128)(2,1)S(1)}, bf16[2,2,32,768]{3,2,0,1:T(8,128)(2,1)S(1)}, u32[]{:S(2)}, u32[]{:S(2)}) collective-permute-start(bf16[2,2,32,768]{3,2,0,1:T(8,128)(2,1)S(1)} %select_bitcast_fusion.6), channel_id=1, source_target_pairs={{0,4},{4,0},{8,12},{12,8},{16,20},{20,16},{24,28},{28,24},{1,5},{5... | collective-permute-start | bytes 589832 | tf_op jit(solution)/shard_map/ppermute | solution.py:492
  288.9 4.9 %collective-permute-start.24 = (bf16[32,512]{1,0:T(8,128)(2,1)S(1)}, bf16[32,512]{1,0:T(8,128)(2,1)S(1)}, u32[]{:S(2)}, u32[]{:S(2)}) collective-permute-start(bf16[32,512]{1,0:T(8,128)(2,1)S(1)} %select_bitcast_fusion.20), channel_id=1, source_target_pairs={{0,16},{4,20},{8,24},{12,28},{16,0},{20,4},{24,8},{28,12},{1,17},{... | collective-permute-start | bytes 98312 | tf_op jit(solution)/shard_map/ppermute | solution.py:492
  290.8 5.7 %collective-permute-start.18 = (bf16[2,2,32,768]{3,2,0,1:T(8,128)(2,1)S(1)}, bf16[2,2,32,768]{3,2,0,1:T(8,128)(2,1)S(1)}, u32[]{:S(2)}, u32[]{:S(2)}) collective-permute-start(bf16[2,2,32,768]{3,2,0,1:T(8,128)(2,1)S(1)} %select_bitcast_fusion.5), channel_id=1, source_target_pairs={{0,2},{1,3},{2,0},{3,1},{4,6},{5,7},{6,4},{7,5},{8,10},{9,11},{10,... | collective-permute-start | bytes 589832 | tf_op jit(solution)/shard_map/ppermute | solution.py:492
  293.9 4.9 %collective-permute-start.15 = (bf16[2,32,768]{2,1,0:T(8,128)(2,1)S(1)}, bf16[2,32,768]{2,1,0:T(8,128)(2,1)S(1)}, u32[]{:S(2)}, u32[]{:S(2)}) collective-permute-start(bf16[2,32,768]{2,1,0:T(8,128)(2,1)S(1)} %select_bitcast_fusion.12), channel_id=1, source_target_pairs={{0,8},{4,12},{8,0},{12,4},{16,24},{20,28},{24,16},{28,20},{1,9},{5... | collective-permute-start | bytes 294920 | tf_op jit(solution)/shard_map/ppermute | solution.py:492
  298.9 5.1 %collective-permute-start.16 = (bf16[32,768]{1,0:T(8,128)(2,1)S(1)}, bf16[32,768]{1,0:T(8,128)(2,1)S(1)}, u32[]{:S(2)}, u32[]{:S(2)}) collective-permute-start(bf16[32,768]{1,0:T(8,128)(2,1)S(1)} %select_bitcast_fusion.18), channel_id=1, source_target_pairs={{0,16},{4,20},{8,24},{12,28},{16,0},{20,4},{24,8},{28,12},{1,17},{... | collective-permute-start | bytes 147464 | tf_op jit(solution)/shard_map/ppermute | solution.py:492
  301.4 5.1 %collective-permute-start.20 = (bf16[32,768]{1,0:T(8,128)(2,1)S(1)}, bf16[32,768]{1,0:T(8,128)(2,1)S(1)}, u32[]{:S(2)}, u32[]{:S(2)}) collective-permute-start(bf16[32,768]{1,0:T(8,128)(2,1)S(1)} %select_bitcast_fusion.17), channel_id=1, source_target_pairs={{0,16},{4,20},{8,24},{12,28},{16,0},{20,4},{24,8},{28,12},{1,17},{... | collective-permute-start | bytes 147464 | tf_op jit(solution)/shard_map/ppermute | solution.py:492
  (19 other events, 224.7 us)
Sparse Core Ops, SparseCore 0:
  114.2 123.8 all-reduce.1

commit v2 on v1

--- a/solution.py
+++ b/solution.py
@@ -185,13 +185,18 @@
     )(span, before, after, w_in, w_in, w_dw, glu)
 
 
-def back_kernel(before_ref, own_ref, after_ref, w_ref, out_ref):
+def back_kernel(before_ref, own_ref, after_ref, w_ref, out_ref, left):
     rows = own_ref.shape[0]
-    w = w_ref[...]
-    for part, at in ((before_ref, 0), (own_ref, NEAR), (after_ref, NEAR + rows)):
-        prod = dot_nt(part[...], w)
-        for c in range(SUB):
-            out_ref[c, at : at + part.shape[0], :] = prod[:, lanes_of(c)]
+
+    @pl.when(pl.program_id(0) == 0)
+    def _():
+        left[0:NEAR, :] = before_ref[...]
+        left[NEAR : NEAR + rows, :] = own_ref[...]
+        left[NEAR + rows :, :] = after_ref[...]
+
+    prod = dot_nt(left[...], w_ref[...])
+    for c in range(SUB):
+        out_ref[c] = prod[:, lanes_of(c)]
 
 
 def back_projected(before, cot, after, w_out):
@@ -209,6 +214,7 @@
         ],
         out_specs=pl.BlockSpec((SUB, full, LANES), lambda j: (j, 0, 0)),
         out_shape=jax.ShapeDtypeStruct((channels // LANES, full, LANES), F32),
+        scratch_shapes=[pltpu.VMEM((full, features), BF16)],
         compiler_params=pltpu.CompilerParams(vmem_limit_bytes=VMEM_LIMIT),
         cost_estimate=pl.CostEstimate(
             flops=2 * rows * features * channels, bytes_accessed=8 * rows * channels, transcendentals=0
@@ -452,26 +458,27 @@
     )(dpre, w_in)
 
 
-def weight_kernel(owner_rows, core_ref, left_ref, right_ref, send_ref, keep_ref):
+def weight_kernel(owner_rows, orders, core_ref, left_ref, right_ref, send_ref, keep_ref):
     term = dot_tn(left_ref[...], right_ref[0])
-    depth, width = term.shape
-    term = term.reshape(depth // (2 * owner_rows), 2, owner_rows, width)
-    even = term[:, 0].reshape(depth // 2, width)
-    odd = term[:, 1].reshape(depth // 2, width)
     is_odd = core_ref[0] == 1
-    send_ref[...] = jnp.where(is_odd, even, odd).astype(BF16)
-    keep_ref[...] = jnp.where(is_odd, odd, even).astype(BF16)
-
-
-def weight_term(core, left, right, owner_rows):
+    for p, (even, odd) in enumerate(zip(*orders)):
+        even = term[even * owner_rows : (even + 1) * owner_rows]
+        odd = term[odd * owner_rows : (odd + 1) * owner_rows]
+        at = slice(p * owner_rows, (p + 1) * owner_rows)
+        send_ref[at, :] = jnp.where(is_odd, even, odd).astype(BF16)
+        keep_ref[at, :] = jnp.where(is_odd, odd, even).astype(BF16)
+
+
+def weight_term(core, left, right, plan):
     halves, rows, width = right.shape
     depth = left.shape[1]
     step = 512
     per = width // step
     out = pl.BlockSpec((depth // 2, step), lambda j: (0, j))
     shape = jax.ShapeDtypeStruct((depth // 2, halves * width), BF16)
-    return pl.pallas_call(
-        functools.partial(weight_kernel, owner_rows),
+    owner_rows = depth // (2 * len(plan.blocks[0]))
+    return pl.pallas_call(
+        functools.partial(weight_kernel, owner_rows, plan.blocks),
         grid=(halves * per,),
         in_specs=[
             pl.BlockSpec(memory_space=pltpu.SMEM),
@@ -488,53 +495,87 @@
     )(core, left, right)
 
 
-def swap(x, axis, mask):
-    return lax.ppermute(x, axis, [(i, i ^ mask) for i in range(lax.axis_size(axis))])
-
-
-def masks_of(axis):
-    return [1 << i for i in range((lax.axis_size(axis) - 1).bit_length())]
+class Halving:
+    def __init__(self, dp_count, tm_count):
+        near = [1 << i for i in range(1, (tm_count - 1).bit_length())]
+        far = [tm_count << i for i in range((dp_count - 1).bit_length())]
+        self.count = dp_count * tm_count
+        self.masks = (near + far, far[: len(near)] + near + far[len(near) :])
+        self.blocks = tuple(
+            [self.block(core, masks, p) for p in range(self.count // 2)] for core, masks in enumerate(self.masks)
+        )
+
+    def block(self, core, masks, p):
+        return core + sum(mask for i, mask in enumerate(masks) if p >> (len(masks) - 1 - i) & 1)
+
+    def perm(self, step):
+        if step < 0:
+            return [(i, i ^ 1) for i in range(self.count)]
+        return [(i, i ^ self.masks[i & 1][step]) for i in range(self.count)]
+
+    def own_half(self, step, place):
+        mask = jnp.where(place & 1 == 1, self.masks[1][step], self.masks[0][step])
+        return ((place & mask) != 0).astype(jnp.int32)
+
+
+def combine_kernel(half_ref, keep_other, got_other, keep_mine, got_mine, send_ref, keep_ref):
+    send_ref[...] = (keep_other[...].astype(F32) + got_other[...].astype(F32)).astype(BF16)
+    keep_ref[...] = (keep_mine[...].astype(F32) + got_mine[...].astype(F32)).astype(BF16)
+
+
+def combine(half, keep, got):
+    rows, width = keep.shape
+    step = 512
+    other = pl.BlockSpec((rows // 2, step), lambda j, half: (1 - half[0], j))
+    mine = pl.BlockSpec((rows // 2, step), lambda j, half: (half[0], j))
+    out = pl.BlockSpec((rows // 2, step), lambda j, half: (0, j))
+    shape = jax.ShapeDtypeStruct((rows // 2, width), BF16)
+    return pl.pallas_call(
+        combine_kernel,
+        grid_spec=pltpu.PrefetchScalarGridSpec(
+            num_scalar_prefetch=1,
+            grid=(width // step,),
+            in_specs=[other, other, mine, mine],
+            out_specs=[out, out],
+        ),
+        out_shape=[shape, shape],
+        compiler_params=pltpu.CompilerParams(vmem_limit_bytes=VMEM_LIMIT),
+        cost_estimate=pl.CostEstimate(flops=rows * width, bytes_accessed=6 * rows * width, transcendentals=0),
+        name="combine",
+    )(half.reshape(1), keep, got, keep, got)
+
+
+def scatter_sum(plan, place, send, keep):
+    everyone = ("dp", "tm")
+    got = lax.ppermute(send, everyone, plan.perm(-1))
+    steps = len(plan.masks[0])
+    for step in range(steps):
+        half = plan.own_half(step, place)
+        if step == 0:
+            send, keep = combine(half, keep, got)
+        else:
+            both = keep.astype(F32) + got.astype(F32)
+            rows = both.shape[0] // 2
+            low, high = both[:rows].astype(BF16), both[rows:].astype(BF16)
+            send = jnp.where(half == 1, low, high)
+            keep = jnp.where(half == 1, high, low)
+        got = lax.ppermute(send, everyone, plan.perm(step))
+    return keep.astype(F32) + got.astype(F32)
 
 
 def all_sum(x):
+    everyone = ("dp", "tm")
+    count = lax.axis_size("dp") * lax.axis_size("tm")
+    copies = jnp.broadcast_to(x[None], (count,) + x.shape)
+    return jnp.sum(lax.all_to_all(copies, everyone, 0, 0, tiled=True), axis=0)
+
+
+def butterfly_sum(x):
     for axis in ("tm", "dp"):
-        for mask in masks_of(axis):
-            x = x + swap(x, axis, mask)
+        count = lax.axis_size(axis)
+        for i in range((count - 1).bit_length()):
+            x = x + lax.ppermute(x, axis, [(j, j ^ (1 << i)) for j in range(count)])
     return x
-
-
-def halve_rest(part, order, bits):
-    left = list(bits)
-    for axis, mask in order:
-        dim = left.index((axis, mask))
-        mine = (lax.axis_index(axis) & mask) != 0
-        low = lax.index_in_dim(part, 0, dim, keepdims=False)
-        high = lax.index_in_dim(part, 1, dim, keepdims=False)
-        got = swap(jnp.where(mine, low, high), axis, mask)
-        part = jnp.where(mine, high, low).astype(F32) + got.astype(F32)
-        left.pop(dim)
-        if left:
-            part = part.astype(BF16)
-    return part
-
-
-def scatter_sum(send, keep, owner_rows):
-    bits = [("dp", m) for m in reversed(masks_of("dp"))] + [("tm", m) for m in reversed(masks_of("tm")[1:])]
-    got = swap(send, "tm", 1)
-    both = (keep.astype(F32) + got.astype(F32)).astype(BF16)
-    width = both.shape[1]
-    both = both.reshape((2,) * len(bits) + (owner_rows, width))
-    along_y = [("tm", m) for m in masks_of("tm")[1:]]
-    along = [("dp", m) for m in masks_of("dp")]
-    orders = [
-        along_y + along,
-        along[:1] + along_y + along[1:],
-        along[1:2] + along_y + along[:1] + along[2:],
-    ]
-    tiles = width // LANES
-    cuts = [0, -(-3 * tiles // 8) * LANES, 2 * -(-3 * tiles // 8) * LANES, width]
-    parts = [halve_rest(both[..., a:b], order, bits) for a, b, order in zip(cuts, cuts[1:], orders)]
-    return jnp.concatenate(parts, axis=1)
 
 
 def local(frames, lengths, w_in, w_dw, bn_gain, bn_bias, w_out, cotangent):
@@ -543,9 +584,9 @@
     taps = w_dw.shape[0]
     tm_count = lax.axis_size("tm")
     device_count = lax.axis_size("dp") * tm_count
-    owner_rows = depth // device_count
-    place = lax.axis_index("tm")
-    offset = place * rows
+    plan = Halving(lax.axis_size("dp"), tm_count)
+    place = lax.axis_index(("dp", "tm"))
+    offset = lax.axis_index("tm") * rows
     span = jnp.stack([-offset, lengths[0] - offset]).astype(jnp.int32)
     core = (place & 1).astype(jnp.int32).reshape(1)
     gain, bias = bn_gain[None], bn_bias[None]
@@ -562,10 +603,10 @@
     swished, dshift, terms = swish(span, sums, gain, bias, conv, back)
     terms = all_sum(terms)
     out_rows = dot_nn(swished, w_out).astype(BF16)
-    grad_w_out = scatter_sum(*weight_term(core, swished, cotangent, owner_rows), owner_rows)
+    grad_w_out = scatter_sum(plan, place, *weight_term(core, swished, cotangent, plan))
     dpre, dconv = norm_grad(span, sums, terms, gain, w_dw, conv, dshift, first, second)
-    kernel_sum = lax.psum(tap_grad(edge, glu, dconv, taps), ("dp", "tm"))
-    grad_w_in = scatter_sum(*weight_term(core, feats, dpre, owner_rows), owner_rows)
+    kernel_sum = butterfly_sum(tap_grad(edge, glu, dconv, taps))
+    grad_w_in = scatter_sum(plan, place, *weight_term(core, feats, dpre, plan))
     grad_rows = frames_grad(dpre, w_in)
     scale = 1.0 / math.sqrt(device_count * rows)
     return (

time: 315 us -> 178 us (0.57)
  waiting for transfers between devices: 145 us -> 40.1 us
  starting transfers between devices: 56.4 us -> 30.6 us
  between operations: 15.1 us -> 1.48 us
  Pallas kernels: 77.9 us -> 84 us
  local copies, waits for them, and re-layouts: 4.48 us -> 9.6 us
  other arithmetic: 11 us -> 7.02 us
    psum x1 -> x0, waiting for transfers between devices: 108 us -> none  [local(): kernel_sum = lax.psum(tap_grad(edge, glu, dconv, taps), ('dp', 'tm'))]
    ppermute x36 -> x15, starting transfers between devices: 52.7 us -> 14.7 us  [the longest x8 11.8 us: scatter_sum(): got = lax.ppermute(send, everyone, plan.perm(step))]
    all_to_all x0 -> x2, waiting for transfers between devices: none -> 19 us  [all_sum(): return jnp.sum(lax.all_to_all(copies, everyone, 0, 0, tiled=True), axis=0)]
    ppermute x36 -> x15, waiting for transfers between devices: 36.8 us -> 21 us  [the longest x8 11.6 us: scatter_sum(): got = lax.ppermute(send, everyone, plan.perm(step))]
    all_to_all x0 -> x2, starting transfers between devices: none -> 12.3 us  [all_sum(): return jnp.sum(lax.all_to_all(copies, everyone, 0, 0, tiled=True), axis=0)]
    pallas_call x2 -> x4, Pallas kernels: 12.2 us -> 19 us  [the longest x2 12.2 us: weight_term(): pl.pallas_call(functools.partial(weight_kernel, owner_rows, plan.blocks),...]
    convert_element_type x20 -> x0, other arithmetic: 3.6 us -> none  [the longest x2 2.52 us: scatter_sum(): both = (keep.astype(F32) + got.astype(F32)).astype(BF16)]
  transfers between devices with their start and end apart: 39 -> 19, of which waited for: 26 -> 8; matrix products, arithmetic and copies ran while one was open for 4% -> 6% of each run, Pallas kernels for 19% -> 25%
where the time goes in v2:
time: 178 us; the launch traced here: 177 us
  Pallas kernels  84 us (47%)
  waiting for transfers between devices  40.1 us (23%)
  starting transfers between devices  30.6 us (17%)
  local copies, waits for them, and re-layouts  9.6 us (5%)
  other arithmetic  7.02 us (4%)
  matrix products  4.34 us (2%)
    all_to_all x2, waiting for transfers between devices, all_sum(): return jnp.sum(lax.all_to_all(copies, everyone, 0, 0, tiled=True), axis=0)  19 us
    pallas_call x1, Pallas kernels, norm_grad(): pl.pallas_call(grad_kernel, grid=(channels // BLOCK,), in_specs=[pl.Block...  13.3 us
    all_to_all x2, starting transfers between devices, all_sum(): return jnp.sum(lax.all_to_all(copies, everyone, 0, 0, tiled=True), axis=0)  12.3 us
    pallas_call x1, Pallas kernels, convolved(): pl.pallas_call(conv_kernel, grid=(blocks,), in_specs=[pl.BlockSpec(memory...  12.3 us
    pallas_call x2, Pallas kernels, weight_term(): pl.pallas_call(functools.partial(weight_kernel, owner_rows, plan.blocks),...  12.2 us
    ppermute x8, starting transfers between devices, scatter_sum(): got = lax.ppermute(send, everyone, plan.perm(step))  11.8 us
    ppermute x8, waiting for transfers between devices, scatter_sum(): got = lax.ppermute(send, everyone, plan.perm(step))  11.6 us
    pallas_call x1, Pallas kernels, tap_grad(): pl.pallas_call(tap_grad_kernel, grid=(channels // BLOCK,), in_specs=[pl.B...  10.8 us
  transfers between devices with their start and end apart: 19, of which 8 were waited for; matrix products, arithmetic and copies ran while one was open for 6% of the time, Pallas kernels for 25%

profile of v2, /device:TPU:0, one launch (start us, length us, event | category | flops | bytes accessed | tf_op | source)
XLA Modules:
  0.0 177.1 jit_solution(3649310888807857587)
XLA Ops:
  2.3 2.4 %collective-permute-start = (bf16[48,1024]{1,0:T(8,128)(2,1)S(1)}, bf16[48,1024]{1,0:T(8,128)(2,1)S(1)}, u32[]{:S(2)}, u32[]{:S(2)}) collective-permute-start(bf16[48,1024]{1,0:T(8,128)(2,1)S(1)} %pad_maximum_fusion), channel_id=1, source_target_pairs={{0,1},{1,2},{2,3},{4,5},{5,6},{6,7},{8,9},{9,10},{10,11},{12,13},{... | collective-permute-start | bytes 294920 | tf_op jit(solution)/shard_map/ppermute | solution.py:596
  7.3 8.1 %gated.1 = (bf16[8,768,128]{2,1,0:T(8,128)(2,1)}, bf16[768,1024]{1,0:T(8,128)(2,1)}, bf16[768,1024]{1,0:T(8,128)(2,1)}) custom-call(s32[2]{0:T(128)} %pad_add_fusion.span_ref, bf16[768,1024]{1,0:T(8,128)(2,1)} %bitcast.28, bf16[1024,2048]{1,0:T(8,128)(2,1)} %w_ref.3, bf16[1024,2048]{1,0:T(8,128)(2,1)} %w_ref.3), custom_call_target="tpu_custom_call" | custom-call | flops 3221225472 | bytes 11010048 | tf_op jit(solution)/shard_map/gated/pallas_call | solution.py:82
  16.7 12.3 %convolved.1 = (f32[8,800,128]{2,1,0:T(8,128)}, bf16[8,64,128]{2,1,0:T(8,128)(2,1)}, f32[3,1024]{1,0:T(4,128)}) custom-call(s32[2]{0:T(128)} %pad_add_fusion.span_ref, bf16[32,1024]{1,0:T(8,128)(2,1)} %slice.116.before_ref, bf16[32,1024]{1,0:T(8,128)(2,1)} %slice.117.after_ref, bf16[1024,2048]{1,0:T(8,128)(2,1)} %w_ref.3, bf16[1024,2048]{1,0:T(8,128)(2,1)} %w_ref.3, ...), custom_call_target="tpu_custom_call" | custom-call | flops 3221225472 | bytes 11010048 | tf_op jit(solution)/shard_map/convolved/pallas_call | solution.py:157
  30.6 9.2 %all-to-all-start = ((f32[32,3,1024]{2,1,0:T(4,128)}), f32[32,3,1024]{2,1,0:T(4,128)S(1)}, u32[]{:S(2)}, u32[]{:S(2)}) async-start(f32[32,3,1024]{2,1,0:T(4,128)} %broadcast_in_dim.24), calls=%async_computation | async-start | bytes 1048576 | tf_op jit(solution)/shard_map/all_to_all | solution.py:570
  41.0 5.9 %back_projected.1.back_ref = f32[8,800,128]{2,1,0:T(8,128)} custom-call(bf16[16,1024]{1,0:T(8,128)(2,1)} %slice.118.before_ref, bf16[768,1024]{1,0:T(8,128)(2,1)} %bitcast.25, bf16[16,1024]{1,0:T(8,128)(2,1)} %slice.119.after_ref, bf16[1024,1024]{1,0:T(8,128)(2,1)} %w_ref.2), custom_call_target="tpu_custom_call" | custom-call | flops 1610612736 | bytes 6291456 | tf_op jit(solution)/shard_map/back_projected/pallas_call | solution.py:206
  46.9 8.5 %all-to-all-done = f32[32,3,1024]{2,1,0:T(4,128)S(1)} async-done(((f32[32,3,1024]{2,1,0:T(4,128)}), f32[32,3,1024]{2,1,0:T(4,128)S(1)}, u32[]{:S(2)}, u32[]{:S(2)}) %all-to-all-start) | async-done | bytes 393248 | tf_op jit(solution)/shard_map/all_to_all | solution.py:570
  56.0 7.2 %swish.1 = (bf16[768,1024]{1,0:T(8,128)(2,1)}, f32[8,800,128]{2,1,0:T(8,128)}, f32[2,1024]{1,0:T(2,128)}) custom-call(s32[2]{0:T(128)} %pad_add_fusion.span_ref, f32[3,1024]{1,0:T(4,128)} %reduce_sum.18.sums_ref, f32[1,1024]{1,0:T(1,128)} %bitcast.26, f32[1,1024]{1,0:T(1,128)} %bitcast.32, f32[8,800,128]{2,1,0:T(8,128)} %get-tuple-element.28.conv_ref, ...), custom_call_target="tpu_custom_call" | custom-call | flops 23592960 | bytes 11010048 | tf_op jit(solution)/shard_map/swish/pallas_call | solution.py:277
  64.7 3.1 %all-to-all-start.1 = ((f32[32,2,1024]{2,1,0:T(2,128)}), f32[32,2,1024]{2,1,0:T(2,128)S(1)}, u32[]{:S(2)}, u32[]{:S(2)}) async-start(f32[32,2,1024]{2,1,0:T(2,128)} %broadcast_in_dim.28), calls=%async_computation.1 | async-start | bytes 524288 | tf_op jit(solution)/shard_map/all_to_all | solution.py:570
  67.8 10.6 %all-to-all-done.1 = f32[32,2,1024]{2,1,0:T(2,128)S(1)} async-done(((f32[32,2,1024]{2,1,0:T(2,128)}), f32[32,2,1024]{2,1,0:T(2,128)S(1)}, u32[]{:S(2)}, u32[]{:S(2)}) %all-to-all-start.1) | async-done | bytes 262176 | tf_op jit(solution)/shard_map/all_to_all | solution.py:570
  79.1 13.3 %norm_grad.1 = (bf16[2,768,1024]{2,1,0:T(8,128)(2,1)}, bf16[8,768,128]{2,1,0:T(8,128)(2,1)}) custom-call(s32[2]{0:T(128)} %pad_add_fusion.span_ref, f32[3,1024]{1,0:T(4,128)} %reduce_sum.18.sums_ref, f32[2,1024]{1,0:T(2,128)} %reduce_sum.19.terms_ref, f32[1,1024]{1,0:T(1,128)} %bitcast.27, f32[31,1024]{1,0:T(8,128)} %taps_ref.3, ...), custom_call_target="tpu_custom_call" | custom-call | flops 55050240 | bytes 12582912 | tf_op jit(solution)/shard_map/norm_grad/pallas_call | solution.py:349
  92.4 7.4 %weight_term.2 = (bf16[512,2048]{1,0:T(8,128)(2,1)}, bf16[512,2048]{1,0:T(8,128)(2,1)}) custom-call(s32[1]{0:T(128)} %bitcast.14.core_ref, bf16[768,1024]{1,0:T(8,128)(2,1)} %bitcast.29, bf16[2,768,1024]{2,1,0:T(8,128)(2,1)} %get-tuple-element.34.dpre_ref.right_ref), custom_call_target="tpu_custom_call" | custom-call | flops 3221225472 | bytes 9437184 | tf_op jit(solution)/shard_map/weight_term/pallas_call | solution.py:480
  99.7 4.8 %weight_term.3 = (bf16[512,1024]{1,0:T(8,128)(2,1)}, bf16[512,1024]{1,0:T(8,128)(2,1)}) custom-call(s32[1]{0:T(128)} %bitcast.14.core_ref, bf16[768,1024]{1,0:T(8,128)(2,1)} %get-tuple-element.29.left_ref, bf16[1,768,1024]{2,1,0:T(8,128)(2,1)} %right_ref.1), custom_call_target="tpu_custom_call" | custom-call | flops 1610612736 | bytes 4718592 | tf_op jit(solution)/shard_map/weight_term/pallas_call | solution.py:480
  105.0 10.8 %tap_grad.1 = f32[31,1024]{1,0:T(8,128)} custom-call(bf16[8,64,128]{2,1,0:T(8,128)(2,1)} %get-tuple-element.43.edge_ref, bf16[8,768,128]{2,1,0:T(8,128)(2,1)} %get-tuple-element.26.glu_ref, bf16[8,768,128]{2,1,0:T(8,128)(2,1)} %get-tuple-element.44.dconv_ref), custom_call_target="tpu_custom_call" | custom-call | flops 48758784 | bytes 3145728 | tf_op jit(solution)/shard_map/tap_grad/pallas_call | solution.py:415
  120.2 4.4 %combine.2 = (bf16[256,2048]{1,0:T(8,128)(2,1)}, bf16[256,2048]{1,0:T(8,128)(2,1)}) custom-call(s32[1]{0:T(128)} %bitcast.13.half_ref, bf16[512,2048]{1,0:T(8,128)(2,1)} %get-tuple-element.35.keep_other.keep_mine, bf16[512,2048]{1,0:T(8,128)(2,1)} %copy-done, bf16[512,2048]{1,0:T(8,128)(2,1)} %get-tuple-element.35.keep_other.keep_mine, bf16[512,2048]{1,0:T(8,128)(2,1)} %copy-done), custom_call_target="tpu_custom_call" | custom-call | flops 1048576 | bytes 6291456 | tf_op jit(solution)/shard_map/combine/pallas_call | solution.py:533
  126.2 4.3 %fusion = bf16[1,768,1024]{2,1,0:T(8,128)(2,1)} fusion(bf16[768,1024]{1,0:T(8,128)(2,1)} %get-tuple-element.29.left_ref, bf16[1024,1024]{1,0:T(8,128)(2,1)S(1)} %copy-done.2), kind=kOutput, calls=%fused_computation.2 | convolution fusion | flops 1611399168 | bytes 5242880 | tf_op jit(solution)/shard_map/dot_general | solution.py:22
  132.5 2.4 %combine.3 = (bf16[256,1024]{1,0:T(8,128)(2,1)}, bf16[256,1024]{1,0:T(8,128)(2,1)}) custom-call(s32[1]{0:T(128)} %bitcast.13.half_ref, bf16[512,1024]{1,0:T(8,128)(2,1)} %get-tuple-element.39.keep_other.keep_mine, bf16[512,1024]{1,0:T(8,128)(2,1)} %copy-done.1, bf16[512,1024]{1,0:T(8,128)(2,1)} %get-tuple-element.39.keep_other.keep_mine, ...), custom_call_target="tpu_custom_call" | custom-call | flops 524288 | bytes 3145728 | tf_op jit(solution)/shard_map/combine/pallas_call | solution.py:533
  135.8 7.5 %frames_grad.1 = bf16[768,1024]{1,0:T(8,128)(2,1)} custom-call(bf16[2,768,1024]{2,1,0:T(8,128)(2,1)} %get-tuple-element.34.dpre_ref.right_ref, bf16[1024,2048]{1,0:T(8,128)(2,1)} %w_ref.3), custom_call_target="tpu_custom_call" | custom-call | flops 3221225472 | bytes 7864320 | tf_op jit(solution)/shard_map/frames_grad/pallas_call | solution.py:444
  144.4 4.0 %collective-permute-done.15 = f32[31,1024]{1,0:T(8,128)S(1)} collective-permute-done((f32[31,1024]{1,0:T(8,128)S(1)}, f32[31,1024]{1,0:T(8,128)S(1)}, u32[]{:S(2)}, u32[]{:S(2)}) %collective-permute-start.15) | collective-permute-done | bytes 127008 | tf_op jit(solution)/shard_map/ppermute | solution.py:577
  151.7 3.9 %collective-permute-done.16 = f32[31,1024]{1,0:T(8,128)S(1)} collective-permute-done((f32[31,1024]{1,0:T(8,128)S(1)}, f32[31,1024]{1,0:T(8,128)S(1)}, u32[]{:S(2)}, u32[]{:S(2)}) %collective-permute-start.16) | collective-permute-done | bytes 127008 | tf_op jit(solution)/shard_map/ppermute | solution.py:577
  157.4 3.7 %collective-permute-done.4 = bf16[128,2048]{1,0:T(8,128)(2,1)S(1)} collective-permute-done((bf16[128,2048]{1,0:T(8,128)(2,1)S(1)}, bf16[128,2048]{1,0:T(8,128)(2,1)S(1)}, u32[]{:S(2)}, u32[]{:S(2)}) %collective-permute-start.4) | collective-permute-done | bytes 524320 | tf_op jit(solution)/shard_map/ppermute | solution.py:562
  161.4 1.7 collective-permute-start.5
  164.6 4.2 %collective-permute-done.5 = bf16[64,2048]{1,0:T(8,128)(2,1)S(1)} collective-permute-done((bf16[64,2048]{1,0:T(8,128)(2,1)S(1)}, bf16[64,2048]{1,0:T(8,128)(2,1)S(1)}, u32[]{:S(2)}, u32[]{:S(2)}) %collective-permute-start.5) | collective-permute-done | bytes 262176 | tf_op jit(solution)/shard_map/ppermute | solution.py:562
  168.9 3.1 %collective-permute-start.6 = (bf16[32,2048]{1,0:T(8,128)(2,1)S(1)}, bf16[32,2048]{1,0:T(8,128)(2,1)S(1)}, u32[]{:S(2)}, u32[]{:S(2)}) collective-permute-start(bf16[32,2048]{1,0:T(8,128)(2,1)S(1)} %broadcast_select_fusion.4), channel_id=1, source_target_pairs={{0,16},{1,17},{2,18},{3,19},{4,20},{5,21},{6,22},{7,23},{8,24},{9,... | collective-permute-start | bytes 393224 | tf_op jit(solution)/shard_map/ppermute | solution.py:562
  172.7 3.7 %collective-permute-done.6 = bf16[32,2048]{1,0:T(8,128)(2,1)S(1)} collective-permute-done((bf16[32,2048]{1,0:T(8,128)(2,1)S(1)}, bf16[32,2048]{1,0:T(8,128)(2,1)S(1)}, u32[]{:S(2)}, u32[]{:S(2)}) %collective-permute-start.6) | collective-permute-done | bytes 131104 | tf_op jit(solution)/shard_map/ppermute | solution.py:562
  (71 shorter events, 29.3 us)
Async XLA Ops:
  2.3 13.1 %collective-permute-start = (bf16[48,1024]{1,0:T(8,128)(2,1)S(1)}, bf16[48,1024]{1,0:T(8,128)(2,1)S(1)}, u32[]{:S(2)}, u32[]{:S(2)}) collective-permute-start(bf16[48,1024]{1,0:T(8,128)(2,1)S(1)} %pad_maximum_fusion), channel_id=1, source_target_pairs={{0,1},{1,2},{2,3},{4,5},{5,6},{6,7},{8,9},{9,10},{10,11},{12,13},{... | collective-permute-start | bytes 294920 | tf_op jit(solution)/shard_map/ppermute | solution.py:596
  4.7 11.3 %collective-permute-start.1 = (bf16[48,1024]{1,0:T(8,128)(2,1)S(1)}, bf16[48,1024]{1,0:T(8,128)(2,1)S(1)}, u32[]{:S(2)}, u32[]{:S(2)}) collective-permute-start(bf16[48,1024]{1,0:T(8,128)(2,1)S(1)} %pad_maximum_fusion.1), channel_id=1, source_target_pairs={{1,0},{2,1},{3,2},{5,4},{6,5},{7,6},{9,8},{10,9},{11,10},{13,12},{... | collective-permute-start | bytes 294920 | tf_op jit(solution)/shard_map/ppermute | solution.py:597
  30.6 24.8 %all-to-all-start = ((f32[32,3,1024]{2,1,0:T(4,128)}), f32[32,3,1024]{2,1,0:T(4,128)S(1)}, u32[]{:S(2)}, u32[]{:S(2)}) async-start(f32[32,3,1024]{2,1,0:T(4,128)} %broadcast_in_dim.24), calls=%async_computation | async-start | bytes 1048576 | tf_op jit(solution)/shard_map/all_to_all | solution.py:570
  64.7 13.7 %all-to-all-start.1 = ((f32[32,2,1024]{2,1,0:T(2,128)}), f32[32,2,1024]{2,1,0:T(2,128)S(1)}, u32[]{:S(2)}, u32[]{:S(2)}) async-start(f32[32,2,1024]{2,1,0:T(2,128)} %broadcast_in_dim.28), calls=%async_computation.1 | async-start | bytes 524288 | tf_op jit(solution)/shard_map/all_to_all | solution.py:570
  99.7 19.2 %collective-permute-start.2 = (bf16[512,2048]{1,0:T(8,128)(2,1)}, bf16[512,2048]{1,0:T(8,128)(2,1)S(1)}, u32[]{:S(2)}, u32[]{:S(2)}) collective-permute-start(bf16[512,2048]{1,0:T(8,128)(2,1)} %get-tuple-element.36), channel_id=1, source_target_pairs={{0,1},{1,0},{2,3},{3,2},{4,5},{5,4},{6,7},{7,6},{8,9},{9,8},{10,11... | collective-permute-start | bytes 6291464 | tf_op jit(solution)/shard_map/ppermute | solution.py:550
  104.6 27.0 %collective-permute-start.7 = (bf16[512,1024]{1,0:T(8,128)(2,1)}, bf16[512,1024]{1,0:T(8,128)(2,1)S(1)}, u32[]{:S(2)}, u32[]{:S(2)}) collective-permute-start(bf16[512,1024]{1,0:T(8,128)(2,1)} %get-tuple-element.40), channel_id=1, source_target_pairs={{0,1},{1,0},{2,3},{3,2},{4,5},{5,4},{6,7},{7,6},{8,9},{9,8},{10,11... | collective-permute-start | bytes 3145736 | tf_op jit(solution)/shard_map/ppermute | solution.py:550
  115.9 1.6 collective-permute-start.12
  118.3 12.2 %collective-permute-start.13 = (f32[31,1024]{1,0:T(8,128)S(1)}, f32[31,1024]{1,0:T(8,128)S(1)}, u32[]{:S(2)}, u32[]{:S(2)}) collective-permute-start(f32[31,1024]{1,0:T(8,128)S(1)} %add.51), channel_id=1, source_target_pairs={{0,2},{1,3},{2,0},{3,1},{4,6},{5,7},{6,4},{7,5},{8,10},{9,11},{10,... | collective-permute-start | bytes 380936 | tf_op jit(solution)/shard_map/ppermute | solution.py:577
  118.9 1.3 copy-start
  120.2 6.0 %copy-start.2 = (bf16[1024,1024]{1,0:T(8,128)(2,1)S(1)}, bf16[1024,1024]{1,0:T(8,128)(2,1)}, u32[]{:S(2)}) copy-start(bf16[1024,1024]{1,0:T(8,128)(2,1)} %w_ref.2) | copy-start | bytes 6291460
  124.7 25.7 %collective-permute-start.3 = (bf16[256,2048]{1,0:T(8,128)(2,1)}, bf16[256,2048]{1,0:T(8,128)(2,1)S(1)}, u32[]{:S(2)}, u32[]{:S(2)}) collective-permute-start(bf16[256,2048]{1,0:T(8,128)(2,1)} %get-tuple-element.38), channel_id=1, source_target_pairs={{0,2},{1,5},{2,0},{3,7},{4,6},{5,1},{6,4},{7,3},{8,10},{9,13},{10,... | collective-permute-start | bytes 3145736 | tf_op jit(solution)/shard_map/ppermute | solution.py:562
  130.6 12.7 %collective-permute-start.14 = (f32[31,1024]{1,0:T(8,128)S(1)}, f32[31,1024]{1,0:T(8,128)S(1)}, u32[]{:S(2)}, u32[]{:S(2)}) collective-permute-start(f32[31,1024]{1,0:T(8,128)S(1)} %add.52), channel_id=1, source_target_pairs={{0,4},{4,0},{8,12},{12,8},{16,20},{20,16},{24,28},{28,24},{1,5},{5... | collective-permute-start | bytes 380936 | tf_op jit(solution)/shard_map/ppermute | solution.py:577
  134.9 8.8 %copy-start.5 = (f32[2,1024]{1,0:T(2,128)S(1)}, f32[2,1024]{1,0:T(2,128)}, u32[]{:S(2)}) copy-start(f32[2,1024]{1,0:T(2,128)} %reduce_sum.19.terms_ref) | copy-start | bytes 24580
  134.9 13.9 %copy-start.4 = (bf16[256,1024]{1,0:T(8,128)(2,1)S(1)}, bf16[256,1024]{1,0:T(8,128)(2,1)}, u32[]{:S(2)}) copy-start(bf16[256,1024]{1,0:T(8,128)(2,1)} %get-tuple-element.41) | copy-start | bytes 1572868
  134.9 13.9 %collective-permute-start.8 = (bf16[256,1024]{1,0:T(8,128)(2,1)}, bf16[256,1024]{1,0:T(8,128)(2,1)S(1)}, u32[]{:S(2)}, u32[]{:S(2)}) collective-permute-start(bf16[256,1024]{1,0:T(8,128)(2,1)} %get-tuple-element.42), channel_id=1, source_target_pairs={{0,2},{1,5},{2,0},{3,7},{4,6},{5,1},{6,4},{7,3},{8,10},{9,13},{10,... | collective-permute-start | bytes 1572872 | tf_op jit(solution)/shard_map/ppermute | solution.py:562
  143.3 7.1 %copy-start.3 = (bf16[256,2048]{1,0:T(8,128)(2,1)S(1)}, bf16[256,2048]{1,0:T(8,128)(2,1)}, u32[]{:S(2)}) copy-start(bf16[256,2048]{1,0:T(8,128)(2,1)} %get-tuple-element.37) | copy-start | bytes 3145732
  143.3 5.0 %collective-permute-start.15 = (f32[31,1024]{1,0:T(8,128)S(1)}, f32[31,1024]{1,0:T(8,128)S(1)}, u32[]{:S(2)}, u32[]{:S(2)}) collective-permute-start(f32[31,1024]{1,0:T(8,128)S(1)} %add.53), channel_id=1, source_target_pairs={{0,8},{4,12},{8,0},{12,4},{16,24},{20,28},{24,16},{28,20},{1,9},{5... | collective-permute-start | bytes 380936 | tf_op jit(solution)/shard_map/ppermute | solution.py:577
  148.4 7.1 %collective-permute-start.16 = (f32[31,1024]{1,0:T(8,128)S(1)}, f32[31,1024]{1,0:T(8,128)S(1)}, u32[]{:S(2)}, u32[]{:S(2)}) collective-permute-start(f32[31,1024]{1,0:T(8,128)S(1)} %add.54), channel_id=1, source_target_pairs={{0,16},{4,20},{8,24},{12,28},{16,0},{20,4},{24,8},{28,12},{1,17},{... | collective-permute-start | bytes 380936 | tf_op jit(solution)/shard_map/ppermute | solution.py:577
  149.0 7.2 %collective-permute-start.9 = (bf16[128,1024]{1,0:T(8,128)(2,1)S(1)}, bf16[128,1024]{1,0:T(8,128)(2,1)S(1)}, u32[]{:S(2)}, u32[]{:S(2)}) collective-permute-start(bf16[128,1024]{1,0:T(8,128)(2,1)S(1)} %broadcast_select_fusion.1), channel_id=1, source_target_pairs={{0,4},{1,3},{2,6},{3,1},{4,0},{5,7},{6,2},{7,5},{8,12},{9,11},{10,... | collective-permute-start | bytes 786440 | tf_op jit(solution)/shard_map/ppermute | solution.py:562
  150.9 10.2 %collective-permute-start.4 = (bf16[128,2048]{1,0:T(8,128)(2,1)S(1)}, bf16[128,2048]{1,0:T(8,128)(2,1)S(1)}, u32[]{:S(2)}, u32[]{:S(2)}) collective-permute-start(bf16[128,2048]{1,0:T(8,128)(2,1)S(1)} %broadcast_select_fusion), channel_id=1, source_target_pairs={{0,4},{1,3},{2,6},{3,1},{4,0},{5,7},{6,2},{7,5},{8,12},{9,11},{10,... | collective-permute-start | bytes 1572872 | tf_op jit(solution)/shard_map/ppermute | solution.py:562
  156.4 6.8 %collective-permute-start.10 = (bf16[64,1024]{1,0:T(8,128)(2,1)S(1)}, bf16[64,1024]{1,0:T(8,128)(2,1)S(1)}, u32[]{:S(2)}, u32[]{:S(2)}) collective-permute-start(bf16[64,1024]{1,0:T(8,128)(2,1)S(1)} %broadcast_select_fusion.3), channel_id=1, source_target_pairs={{0,8},{1,9},{2,10},{3,11},{4,12},{5,13},{6,14},{7,15},{8,0},{9,1},... | collective-permute-start | bytes 393224 | tf_op jit(solution)/shard_map/ppermute | solution.py:562
  161.4 7.3 %collective-permute-start.5 = (bf16[64,2048]{1,0:T(8,128)(2,1)S(1)}, bf16[64,2048]{1,0:T(8,128)(2,1)S(1)}, u32[]{:S(2)}, u32[]{:S(2)}) collective-permute-start(bf16[64,2048]{1,0:T(8,128)(2,1)S(1)} %broadcast_select_fusion.2), channel_id=1, source_target_pairs={{0,8},{1,9},{2,10},{3,11},{4,12},{5,13},{6,14},{7,15},{8,0},{9,1},... | collective-permute-start | bytes 786440 | tf_op jit(solution)/shard_map/ppermute | solution.py:562
  163.2 8.8 %collective-permute-start.11 = (bf16[32,1024]{1,0:T(8,128)(2,1)S(1)}, bf16[32,1024]{1,0:T(8,128)(2,1)S(1)}, u32[]{:S(2)}, u32[]{:S(2)}) collective-permute-start(bf16[32,1024]{1,0:T(8,128)(2,1)S(1)} %broadcast_select_fusion.5), channel_id=1, source_target_pairs={{0,16},{1,17},{2,18},{3,19},{4,20},{5,21},{6,22},{7,23},{8,24},{9,... | collective-permute-start | bytes 196616 | tf_op jit(solution)/shard_map/ppermute | solution.py:562
  168.9 7.5 %collective-permute-start.6 = (bf16[32,2048]{1,0:T(8,128)(2,1)S(1)}, bf16[32,2048]{1,0:T(8,128)(2,1)S(1)}, u32[]{:S(2)}, u32[]{:S(2)}) collective-permute-start(bf16[32,2048]{1,0:T(8,128)(2,1)S(1)} %broadcast_select_fusion.4), channel_id=1, source_target_pairs={{0,16},{1,17},{2,18},{3,19},{4,20},{5,21},{6,22},{7,23},{8,24},{9,... | collective-permute-start | bytes 393224 | tf_op jit(solution)/shard_map/ppermute | solution.py:562
  (1 other events, 1.0 us)

commit v3 on v2

--- a/solution.py
+++ b/solution.py
@@ -57,6 +57,11 @@
 
 def lanes_of(c):
     return slice(c * LANES, (c + 1) * LANES)
+
+
+def spread(copies_ref, c, lines):
+    lines = jnp.concatenate(lines, axis=0)
+    copies_ref[:, :, lanes_of(c)] = jnp.broadcast_to(lines[None], (copies_ref.shape[0],) + lines.shape)
 
 
 def gate_kernel(span_ref, feats_ref, lin_w_ref, gate_w_ref, glu_ref, first_ref, second_ref):
@@ -141,13 +146,13 @@
 
         zero = jnp.zeros((8, LANES), F32)
         total, square = lax.fori_loop(0, full // count, chunk, (zero, zero))
-        sums_ref[0:1, lanes_of(c)] = jnp.sum(total, axis=0, keepdims=True)
-        sums_ref[1:2, lanes_of(c)] = jnp.sum(square, axis=0, keepdims=True)
-    live_rows = jnp.maximum(own_high - own_low, 0).astype(F32)
-    sums_ref[2:3, :] = jnp.full((1, BLOCK), 1.0, F32) * live_rows
-
-
-def convolved(span, before, after, w_in, w_dw, glu):
+        total = jnp.sum(total, axis=0, keepdims=True)
+        square = jnp.sum(square, axis=0, keepdims=True)
+        live_rows = jnp.full((1, LANES), 1.0, F32) * jnp.maximum(own_high - own_low, 0).astype(F32)
+        spread(sums_ref, c, (total, square, live_rows))
+
+
+def convolved(span, before, after, w_in, w_dw, glu, devices):
     groups, rows, _ = glu.shape
     channels = groups * LANES
     depth = w_in.shape[0]
@@ -169,12 +174,12 @@
         out_specs=[
             pl.BlockSpec((SUB, full, LANES), lambda j: (j, 0, 0)),
             pl.BlockSpec((SUB, 2 * WIDE, LANES), lambda j: (j, 0, 0)),
-            pl.BlockSpec((3, BLOCK), lambda j: (0, j)),
+            pl.BlockSpec((devices, 3, BLOCK), lambda j: (0, 0, j)),
         ],
         out_shape=[
             jax.ShapeDtypeStruct((groups, full, LANES), F32),
             jax.ShapeDtypeStruct((groups, 2 * WIDE, LANES), BF16),
-            jax.ShapeDtypeStruct((3, channels), F32),
+            jax.ShapeDtypeStruct((devices, 3, channels), F32),
         ],
         scratch_shapes=[pltpu.VMEM((SUB, rows + 2 * WIDE, LANES), F32)],
         compiler_params=pltpu.CompilerParams(vmem_limit_bytes=VMEM_LIMIT),
@@ -207,9 +212,9 @@
         back_kernel,
         grid=(channels // BLOCK,),
         in_specs=[
-            pl.BlockSpec((NEAR, features), lambda j: (0, 0)),
+            pl.BlockSpec((NEAR, features), lambda j: (WIDE // NEAR, 0)),
             pl.BlockSpec((rows, features), lambda j: (0, 0)),
-            pl.BlockSpec((NEAR, features), lambda j: (0, 0)),
+            pl.BlockSpec((NEAR, features), lambda j: (WIDE // NEAR, 0)),
             pl.BlockSpec((BLOCK, features), lambda j: (j, 0)),
         ],
         out_specs=pl.BlockSpec((SUB, full, LANES), lambda j: (j, 0, 0)),
@@ -224,10 +229,10 @@
 
 
 def moments(sums_ref, c):
-    at = lanes_of(c)
-    count = sums_ref[2:3, at]
-    mean = sums_ref[0:1, at] / count
-    variance = sums_ref[1:2, at] / count - mean * mean
+    sums = jnp.sum(sums_ref[:, :, lanes_of(c)], axis=0)
+    count = sums[2:3]
+    mean = sums[0:1] / count
+    variance = sums[1:2] / count - mean * mean
     return mean, lax.rsqrt(variance + 1e-05), count
 
 
@@ -264,12 +269,14 @@
         by_gain, by_bias = lax.fori_loop(0, rows // count, chunk, (zero, zero))
         piece(0, NEAR)
         piece(rows + NEAR, NEAR)
-        terms_ref[0:1, lanes_of(c)] = jnp.sum(by_gain, axis=0, keepdims=True)
-        terms_ref[1:2, lanes_of(c)] = jnp.sum(by_bias, axis=0, keepdims=True)
+        by_gain = jnp.sum(by_gain, axis=0, keepdims=True)
+        by_bias = jnp.sum(by_bias, axis=0, keepdims=True)
+        spread(terms_ref, c, (by_gain, by_bias))
 
 
 def swish(span, sums, gain, bias, conv, back):
     groups, full, _ = conv.shape
+    devices = sums.shape[0]
     rows = full - 2 * NEAR
     channels = groups * LANES
     vector = pl.BlockSpec((1, BLOCK), lambda j: (0, j))
@@ -279,7 +286,7 @@
         grid=(channels // BLOCK,),
         in_specs=[
             pl.BlockSpec(memory_space=pltpu.SMEM),
-            pl.BlockSpec((3, BLOCK), lambda j: (0, j)),
+            pl.BlockSpec((devices, 3, BLOCK), lambda j: (0, 0, j)),
             vector,
             vector,
             tall,
@@ -288,12 +295,12 @@
         out_specs=[
             pl.BlockSpec((rows, BLOCK), lambda j: (0, j)),
             tall,
-            pl.BlockSpec((2, BLOCK), lambda j: (0, j)),
+            pl.BlockSpec((devices, 2, BLOCK), lambda j: (0, 0, j)),
         ],
         out_shape=[
             jax.ShapeDtypeStruct((rows, channels), BF16),
             jax.ShapeDtypeStruct((groups, full, LANES), F32),
-            jax.ShapeDtypeStruct((2, channels), F32),
+            jax.ShapeDtypeStruct((devices, 2, channels), F32),
         ],
         compiler_params=pltpu.CompilerParams(vmem_limit_bytes=VMEM_LIMIT),
         cost_estimate=pl.CostEstimate(
@@ -317,8 +324,9 @@
         mean, inv_std, total = moments(sums_ref, c)
         at = lanes_of(c)
         outer = gain_ref[:, at] * inv_std
-        by_gain = terms_ref[0:1, at] / total
-        by_bias = terms_ref[1:2, at] / total
+        terms = jnp.sum(terms_ref[:, :, at], axis=0)
+        by_gain = terms[0:1] / total
+        by_bias = terms[1:2] / total
 
         @pl.loop(0, full // span)
         def _(i):
@@ -339,22 +347,25 @@
             dpre_ref[1, pl.ds(r, count), at] = (dglu * second_ref[pl.ds(r, count), at].astype(F32)).astype(BF16)
 
 
-def norm_grad(span, sums, terms, gain, w_dw, conv, dshift, first, second):
+def norm_grad(span, sums, terms, gain, w_dw, conv, dshift, first, second, part, parts):
     groups, full, _ = conv.shape
+    devices = sums.shape[0]
     rows = full - 2 * NEAR
-    channels = groups * LANES
+    channels = groups * LANES // parts
     taps = w_dw.shape[0]
-    tall = pl.BlockSpec((SUB, full, LANES), lambda j: (j, 0, 0))
-    flat = pl.BlockSpec((rows, BLOCK), lambda j: (0, j))
+    blocks = channels // BLOCK
+    at = part * blocks
+    tall = pl.BlockSpec((SUB, full, LANES), lambda j: (j + at, 0, 0))
+    flat = pl.BlockSpec((rows, BLOCK), lambda j: (0, j + at))
     return pl.pallas_call(
         grad_kernel,
-        grid=(channels // BLOCK,),
+        grid=(blocks,),
         in_specs=[
             pl.BlockSpec(memory_space=pltpu.SMEM),
-            pl.BlockSpec((3, BLOCK), lambda j: (0, j)),
-            pl.BlockSpec((2, BLOCK), lambda j: (0, j)),
-            pl.BlockSpec((1, BLOCK), lambda j: (0, j)),
-            pl.BlockSpec((taps, BLOCK), lambda j: (0, j)),
+            pl.BlockSpec((devices, 3, BLOCK), lambda j: (0, 0, j + at)),
+            pl.BlockSpec((devices, 2, BLOCK), lambda j: (0, 0, j + at)),
+            pl.BlockSpec((1, BLOCK), lambda j: (0, j + at)),
+            pl.BlockSpec((taps, BLOCK), lambda j: (0, j + at)),
             tall,
             tall,
             flat,
@@ -366,7 +377,7 @@
         ],
         out_shape=[
             jax.ShapeDtypeStruct((2, rows, channels), BF16),
-            jax.ShapeDtypeStruct((groups, rows, LANES), BF16),
+            jax.ShapeDtypeStruct((channels // LANES, rows, LANES), BF16),
         ],
         scratch_shapes=[pltpu.VMEM((SUB, full, LANES), F32)],
         compiler_params=pltpu.CompilerParams(vmem_limit_bytes=VMEM_LIMIT),
@@ -409,15 +420,16 @@
             out_ref[k : k + 1, lanes_of(c)] = jnp.sum(sums[k], axis=0, keepdims=True)
 
 
-def tap_grad(edge, glu, dconv, taps):
-    groups, rows, _ = glu.shape
+def tap_grad(edge, glu, dconv, taps, part):
+    groups, rows, _ = dconv.shape
     channels = groups * LANES
+    at = part * (groups // SUB)
     return pl.pallas_call(
         tap_grad_kernel,
-        grid=(channels // BLOCK,),
+        grid=(groups // SUB,),
         in_specs=[
-            pl.BlockSpec((SUB, 2 * WIDE, LANES), lambda j: (j, 0, 0)),
-            pl.BlockSpec((SUB, rows, LANES), lambda j: (j, 0, 0)),
+            pl.BlockSpec((SUB, 2 * WIDE, LANES), lambda j: (j + at, 0, 0)),
+            pl.BlockSpec((SUB, rows, LANES), lambda j: (j + at, 0, 0)),
             pl.BlockSpec((SUB, rows, LANES), lambda j: (j, 0, 0)),
         ],
         out_specs=pl.BlockSpec((taps, BLOCK), lambda j: (0, j)),
@@ -432,41 +444,114 @@
     )(edge, glu, dconv)
 
 
-def frames_grad_kernel(dpre_ref, w_ref, out_ref):
-    channels = dpre_ref.shape[2]
-    total = dot_nt(dpre_ref[0], w_ref[:, :channels]) + dot_nt(dpre_ref[1], w_ref[:, channels:])
+def frames_grad_kernel(*refs):
+    *dpre_refs, w_ref, out_ref = refs
+    width = dpre_refs[0].shape[2]
+    channels = width * len(dpre_refs)
+    total = 0.0
+    for i, dpre_ref in enumerate(dpre_refs):
+        for half in range(2):
+            at = half * channels + i * width
+            total = total + dot_nt(dpre_ref[half], w_ref[:, at : at + width])
     out_ref[...] = total.astype(BF16)
 
 
-def frames_grad(dpre, w_in):
-    _, rows, channels = dpre.shape
-    depth = w_in.shape[0]
+def frames_grad(dpre_parts, w_in):
+    _, rows, width = dpre_parts[0].shape
+    depth, outputs = w_in.shape
+    whole = pl.BlockSpec((2, rows, width), lambda j: (0, 0, 0))
     return pl.pallas_call(
         frames_grad_kernel,
         grid=(depth // BLOCK,),
-        in_specs=[
-            pl.BlockSpec((2, rows, channels), lambda j: (0, 0, 0)),
-            pl.BlockSpec((BLOCK, 2 * channels), lambda j: (j, 0)),
-        ],
+        in_specs=[whole] * len(dpre_parts) + [pl.BlockSpec((BLOCK, outputs), lambda j: (j, 0))],
         out_specs=pl.BlockSpec((rows, BLOCK), lambda j: (0, j)),
         out_shape=jax.ShapeDtypeStruct((rows, depth), BF16),
         compiler_params=pltpu.CompilerParams(vmem_limit_bytes=VMEM_LIMIT),
         cost_estimate=pl.CostEstimate(
-            flops=4 * rows * depth * channels, bytes_accessed=10 * rows * depth, transcendentals=0
+            flops=2 * rows * depth * outputs, bytes_accessed=10 * rows * depth, transcendentals=0
         ),
         name="frames_grad",
-    )(dpre, w_in)
+    )(*dpre_parts, w_in)
+
+
+def flip_kernel(owner_rows, orders, core_ref, left_ref, mine_ref, other_ref):
+    flat = left_ref[...].astype(F32).T
+    is_odd = core_ref[0] == 1
+
+    def rows_of(order):
+        return jnp.concatenate([flat[p * owner_rows : (p + 1) * owner_rows] for p in order], axis=0).astype(BF16)
+
+    even, odd = rows_of(orders[0]), rows_of(orders[1])
+    mine_ref[...] = jnp.where(is_odd, odd, even)
+    other_ref[...] = jnp.where(is_odd, even, odd)
+
+
+def flipped(core, left, plan):
+    rows, depth = left.shape
+    owner_rows = depth // (2 * len(plan.blocks[0]))
+    shape = jax.ShapeDtypeStruct((depth // 2, rows), BF16)
+    return pl.pallas_call(
+        functools.partial(flip_kernel, owner_rows, plan.blocks),
+        in_specs=[pl.BlockSpec(memory_space=pltpu.SMEM), pl.BlockSpec(memory_space=pltpu.VMEM)],
+        out_specs=[pl.BlockSpec(memory_space=pltpu.VMEM)] * 2,
+        out_shape=[shape, shape],
+        compiler_params=pltpu.CompilerParams(vmem_limit_bytes=VMEM_LIMIT),
+        cost_estimate=pl.CostEstimate(flops=4 * rows * depth, bytes_accessed=4 * rows * depth, transcendentals=0),
+        name="flipped",
+    )(core, left)
+
+
+def pair_kernel(half_ref, left_own, left_got, *refs):
+    *right_refs, send_ref, keep_ref = refs
+    j = pl.program_id(0)
+    rows = send_ref.shape[0]
+    for part in range(len(right_refs) // 2):
+
+        @pl.when(j // 2 == part)
+        def _(own=right_refs[2 * part], got=right_refs[2 * part + 1]):
+            term = dot_nn(left_own[...], own[0]) + dot_nn(left_got[...], got[0])
+            low, high = term[:rows], term[rows:]
+            upper = half_ref[0] == 1
+            send_ref[...] = jnp.where(upper, low, high).astype(BF16)
+            keep_ref[...] = jnp.where(upper, high, low).astype(BF16)
+
+
+def pair_term(half, left_own, left_got, right_own, right_got):
+    parts = len(right_own)
+    _, rows, width = right_own[0].shape
+    depth = left_own.shape[0]
+    left = pl.BlockSpec((depth, rows), lambda j: (0, 0))
+    out = pl.BlockSpec((depth // 2, width), lambda j: (0, (j % 2) * parts + j // 2))
+    shape = jax.ShapeDtypeStruct((depth // 2, 2 * parts * width), BF16)
+    rights, specs = [], []
+    for part in range(parts):
+        rights += [right_own[part], right_got[part]]
+        specs += [pl.BlockSpec((1, rows, width), lambda j, part=part: (jnp.clip(j - 2 * part, 0, 1), 0, 0))] * 2
+    return pl.pallas_call(
+        pair_kernel,
+        grid=(2 * parts,),
+        in_specs=[pl.BlockSpec(memory_space=pltpu.SMEM), left, left] + specs,
+        out_specs=[out, out],
+        out_shape=[shape, shape],
+        compiler_params=pltpu.CompilerParams(vmem_limit_bytes=VMEM_LIMIT),
+        cost_estimate=pl.CostEstimate(
+            flops=8 * parts * rows * depth * width, bytes_accessed=16 * parts * rows * width, transcendentals=0
+        ),
+        name="pair_term",
+    )(half.reshape(1), left_own, left_got, *rights)
 
 
 def weight_kernel(owner_rows, orders, core_ref, left_ref, right_ref, send_ref, keep_ref):
     term = dot_tn(left_ref[...], right_ref[0])
     is_odd = core_ref[0] == 1
+    send, keep = [], []
     for p, (even, odd) in enumerate(zip(*orders)):
         even = term[even * owner_rows : (even + 1) * owner_rows]
         odd = term[odd * owner_rows : (odd + 1) * owner_rows]
-        at = slice(p * owner_rows, (p + 1) * owner_rows)
-        send_ref[at, :] = jnp.where(is_odd, even, odd).astype(BF16)
-        keep_ref[at, :] = jnp.where(is_odd, odd, even).astype(BF16)
+        send.append(jnp.where(is_odd, even, odd))
+        keep.append(jnp.where(is_odd, odd, even))
+    send_ref[...] = jnp.concatenate(send, axis=0).astype(BF16)
+    keep_ref[...] = jnp.concatenate(keep, axis=0).astype(BF16)
 
 
 def weight_term(core, left, right, plan):
@@ -545,29 +630,22 @@
     )(half.reshape(1), keep, got, keep, got)
 
 
-def scatter_sum(plan, place, send, keep):
+def scatter_rest(plan, place, send, keep):
     everyone = ("dp", "tm")
-    got = lax.ppermute(send, everyone, plan.perm(-1))
-    steps = len(plan.masks[0])
-    for step in range(steps):
+    got = lax.ppermute(send, everyone, plan.perm(0))
+    for step in range(1, len(plan.masks[0])):
         half = plan.own_half(step, place)
-        if step == 0:
-            send, keep = combine(half, keep, got)
-        else:
-            both = keep.astype(F32) + got.astype(F32)
-            rows = both.shape[0] // 2
-            low, high = both[:rows].astype(BF16), both[rows:].astype(BF16)
-            send = jnp.where(half == 1, low, high)
-            keep = jnp.where(half == 1, high, low)
+        both = keep.astype(F32) + got.astype(F32)
+        rows = both.shape[0] // 2
+        low, high = both[:rows].astype(BF16), both[rows:].astype(BF16)
+        send = jnp.where(half == 1, low, high)
+        keep = jnp.where(half == 1, high, low)
         got = lax.ppermute(send, everyone, plan.perm(step))
     return keep.astype(F32) + got.astype(F32)
 
 
-def all_sum(x):
-    everyone = ("dp", "tm")
-    count = lax.axis_size("dp") * lax.axis_size("tm")
-    copies = jnp.broadcast_to(x[None], (count,) + x.shape)
-    return jnp.sum(lax.all_to_all(copies, everyone, 0, 0, tiled=True), axis=0)
+def from_all(copies):
+    return lax.all_to_all(copies, ("dp", "tm"), 0, 0, tiled=True)
 
 
 def butterfly_sum(x):
@@ -591,23 +669,40 @@
     core = (place & 1).astype(jnp.int32).reshape(1)
     gain, bias = bn_gain[None], bn_bias[None]
 
+    everyone = ("dp", "tm")
     tail = jnp.concatenate([feats[rows - WIDE :], cot[rows - NEAR :]], axis=0)
     head = jnp.concatenate([feats[:WIDE], cot[:NEAR]], axis=0)
     before = lax.ppermute(tail, "tm", [(i, i + 1) for i in range(tm_count - 1)])
     after = lax.ppermute(head, "tm", [(i + 1, i) for i in range(tm_count - 1)])
 
     glu, first, second = gated(span, feats, w_in)
-    conv, edge, sums = convolved(span, before[:WIDE], after[:WIDE], w_in, w_dw, glu)
-    sums = all_sum(sums)
-    back = back_projected(before[WIDE:], cot, after[WIDE:], w_out)
+    conv, edge, sums = convolved(span, before, after, w_in, w_dw, glu, device_count)
+    sums = from_all(sums)
+    back = back_projected(before, cot, after, w_out)
+    left_own, left_other = flipped(core, feats, plan)
+    sums, back, left_other = lax.optimization_barrier((sums, back, left_other))
+    left_got = lax.ppermute(left_other, everyone, plan.perm(-1))
+
     swished, dshift, terms = swish(span, sums, gain, bias, conv, back)
-    terms = all_sum(terms)
+    terms = from_all(terms)
     out_rows = dot_nn(swished, w_out).astype(BF16)
-    grad_w_out = scatter_sum(plan, place, *weight_term(core, swished, cotangent, plan))
-    dpre, dconv = norm_grad(span, sums, terms, gain, w_dw, conv, dshift, first, second)
-    kernel_sum = butterfly_sum(tap_grad(edge, glu, dconv, taps))
-    grad_w_in = scatter_sum(plan, place, *weight_term(core, feats, dpre, plan))
-    grad_rows = frames_grad(dpre, w_in)
+    out_send, out_keep = weight_term(core, swished, cotangent, plan)
+    terms, out_rows, out_send = lax.optimization_barrier((terms, out_rows, out_send))
+    out_got = lax.ppermute(out_send, everyone, plan.perm(-1))
+
+    first_half = plan.own_half(0, place)
+    parts = 2
+    dpre_own, dpre_got, taps_sum = [], [], []
+    for part in range(parts):
+        dpre, dconv = norm_grad(span, sums, terms, gain, w_dw, conv, dshift, first, second, part, parts)
+        dpre_own.append(dpre)
+        dpre_got.append(lax.ppermute(dpre, everyone, plan.perm(-1)))
+        taps_sum.append(tap_grad(edge, glu, dconv, taps, part))
+    kernel_sum = butterfly_sum(jnp.concatenate(taps_sum, axis=1))
+    grad_w_out = scatter_rest(plan, place, *combine(first_half, out_keep, out_got))
+    grad_w_in = scatter_rest(plan, place, *pair_term(first_half, left_own, left_got, dpre_own, dpre_got))
+    grad_rows = frames_grad(dpre_own, w_in)
+    by_gain, by_bias = jnp.sum(terms, axis=0)
     scale = 1.0 / math.sqrt(device_count * rows)
     return (
         out_rows[None],
@@ -615,8 +710,8 @@
         grad_w_in * scale,
         grad_w_out * scale,
         kernel_sum * scale,
-        terms[0] * scale,
-        terms[1] * scale,
+        by_gain * scale,
+        by_bias * scale,
     )
 
 

time: 178 us -> 171 us (0.961)
  Pallas kernels: 84 us -> 88.8 us
  local copies, waits for them, and re-layouts: 9.6 us -> 4.81 us
  waiting for transfers between devices: 40.1 us -> 36.4 us
    pallas_call x3 -> x7, Pallas kernels: 31.6 us -> 47.7 us  [the longest x2 16.5 us: norm_grad(): pl.pallas_call(grad_kernel, grid=(blocks,), in_specs=[pl.BlockSpec(memory...]
    all_to_all x2, waiting for transfers between devices: 19 us -> 9.16 us  [from_all(): return lax.all_to_all(copies, ('dp', 'tm'), 0, 0, tiled=True)]
    pallas_call x2 -> x1, Pallas kernels: 12.2 us -> 4.93 us  [weight_term(): pl.pallas_call(functools.partial(weight_kernel, owner_rows, plan.blocks),...]
    ppermute x10 -> x12, waiting for transfers between devices: 11.6 us -> 16.3 us  [the longest x6 16.3 us: scatter_rest(): got = lax.ppermute(send, everyone, plan.perm(step))]
    pallas_call x2 -> x1, Pallas kernels: 6.84 us -> 2.41 us  [combine(): pl.pallas_call(combine_kernel, grid_spec=pltpu.PrefetchScalarGridSpec(num...]
    broadcast_in_dim x2 -> x0, local copies, waits for them, and re-layouts: 3.12 us -> none  [all_sum(): copies = jnp.broadcast_to(x[None], (count,) + x.shape)]
    ppermute x10 -> x12, starting transfers between devices: 12.3 us -> 9.59 us  [the longest x6 6.09 us: scatter_rest(): got = lax.ppermute(send, everyone, plan.perm(step))]
    slice x4 -> x0, local copies, waits for them, and re-layouts: 2.5 us -> none  [the longest x2 1.23 us: local(): back = back_projected(before[WIDE:], cot, after[WIDE:], w_out)]
  transfers between devices with their start and end apart: 19 -> 21, of which waited for: 8 -> 9; matrix products, arithmetic and copies ran while one was open for 6% -> 5% of each run, Pallas kernels for 25% -> 31%
where the time goes in v3:
time: 171 us; the launch traced here: 170 us
  Pallas kernels  88.8 us (52%)
  waiting for transfers between devices  36.4 us (21%)
  starting transfers between devices  29.2 us (17%)
  other arithmetic  6.51 us (4%)
  local copies, waits for them, and re-layouts  4.81 us (3%)
  matrix products  2.94 us (2%)
    pallas_call x2, Pallas kernels, norm_grad(): pl.pallas_call(grad_kernel, grid=(blocks,), in_specs=[pl.BlockSpec(memory...  16.5 us
    ppermute x6, waiting for transfers between devices, scatter_rest(): got = lax.ppermute(send, everyone, plan.perm(step))  16.3 us
    pallas_call x2, Pallas kernels, tap_grad(): pl.pallas_call(tap_grad_kernel, grid=(groups // SUB,), in_specs=[pl.Block...  12.6 us
    all_to_all x2, starting transfers between devices, from_all(): return lax.all_to_all(copies, ('dp', 'tm'), 0, 0, tiled=True)  12.5 us
    pallas_call x1, Pallas kernels, convolved(): pl.pallas_call(conv_kernel, grid=(blocks,), in_specs=[pl.BlockSpec(memory...  12.4 us
    ppermute x5, waiting for transfers between devices, butterfly_sum(): x = x + lax.ppermute(x, axis, [(j, j ^ 1 << i) for j in range(count)])  10.9 us
    all_to_all x2, waiting for transfers between devices, from_all(): return lax.all_to_all(copies, ('dp', 'tm'), 0, 0, tiled=True)  9.16 us
    pallas_call x1, Pallas kernels, gated(): pl.pallas_call(gate_kernel, grid=(blocks,), in_specs=[pl.BlockSpec(memory...  8.1 us
  transfers between devices with their start and end apart: 21, of which 9 were waited for; matrix products, arithmetic and copies ran while one was open for 5% of the time, Pallas kernels for 31%

profile of v3, /device:TPU:0, one launch (start us, length us, event | category | flops | bytes accessed | tf_op | source)
XLA Modules:
  0.0 170.2 jit_solution(1134861845360389314)
XLA Ops:
  2.3 2.4 %collective-permute-start = (bf16[48,1024]{1,0:T(8,128)(2,1)S(1)}, bf16[48,1024]{1,0:T(8,128)(2,1)S(1)}, u32[]{:S(2)}, u32[]{:S(2)}) collective-permute-start(bf16[48,1024]{1,0:T(8,128)(2,1)S(1)} %pad_maximum_fusion.1), channel_id=1, source_target_pairs={{0,1},{1,2},{2,3},{4,5},{5,6},{6,7},{8,9},{9,10},{10,11},{12,13},{... | collective-permute-start | bytes 294920 | tf_op jit(solution)/shard_map/ppermute | solution.py:675
  7.3 8.1 %gated.1 = (bf16[8,768,128]{2,1,0:T(8,128)(2,1)}, bf16[768,1024]{1,0:T(8,128)(2,1)}, bf16[768,1024]{1,0:T(8,128)(2,1)}) custom-call(s32[2]{0:T(128)} %pad_add_fusion.span_ref, bf16[768,1024]{1,0:T(8,128)(2,1)} %bitcast.24, bf16[1024,2048]{1,0:T(8,128)(2,1)} %refs_2_.1, bf16[1024,2048]{1,0:T(8,128)(2,1)} %refs_2_.1), custom_call_target="tpu_custom_call" | custom-call | flops 3221225472 | bytes 11010048 | tf_op jit(solution)/shard_map/gated/pallas_call | solution.py:87
  16.1 12.4 %convolved.1 = (f32[8,800,128]{2,1,0:T(8,128)}, bf16[8,64,128]{2,1,0:T(8,128)(2,1)}, f32[32,3,1024]{2,1,0:T(4,128)}) custom-call(s32[2]{0:T(128)} %pad_add_fusion.span_ref, bf16[48,1024]{1,0:T(8,128)(2,1)} %copy-done.8, bf16[48,1024]{1,0:T(8,128)(2,1)} %copy-done.9, bf16[1024,2048]{1,0:T(8,128)(2,1)} %refs_2_.1, bf16[1024,2048]{1,0:T(8,128)(2,1)} %refs_2_.1, ...), custom_call_target="tpu_custom_call" | custom-call | flops 3221225472 | bytes 11010048 | tf_op jit(solution)/shard_map/convolved/pallas_call | solution.py:162
  28.5 9.2 %all-to-all-start = ((f32[32,3,1024]{2,1,0:T(4,128)}), f32[32,3,1024]{2,1,0:T(4,128)S(1)}, u32[]{:S(2)}, u32[]{:S(2)}) async-start(f32[32,3,1024]{2,1,0:T(4,128)} %get-tuple-element.35), calls=%async_computation | async-start | bytes 1048576 | tf_op jit(solution)/shard_map/all_to_all | solution.py:648
  37.7 3.0 %flipped.1 = (bf16[512,768]{1,0:T(8,128)(2,1)}, bf16[512,768]{1,0:T(8,128)(2,1)}) custom-call(s32[1]{0:T(128)} %bitcast.9.core_ref, bf16[768,1024]{1,0:T(8,128)(2,1)} %bitcast.25), custom_call_target="tpu_custom_call" | custom-call | flops 3145728 | bytes 3145728 | tf_op jit(solution)/shard_map/flipped/pallas_call | solution.py:493
  40.7 5.8 %back_projected.1.back_ref = f32[8,800,128]{2,1,0:T(8,128)} custom-call(bf16[48,1024]{1,0:T(8,128)(2,1)} %copy-done.8, bf16[768,1024]{1,0:T(8,128)(2,1)} %bitcast.26, bf16[48,1024]{1,0:T(8,128)(2,1)} %copy-done.9, bf16[1024,1024]{1,0:T(8,128)(2,1)} %w_ref.1), custom_call_target="tpu_custom_call" | custom-call | flops 1610612736 | bytes 6291456 | tf_op jit(solution)/shard_map/back_projected/pallas_call | solution.py:211
  46.6 6.6 %all-to-all-done.sums_ref = f32[32,3,1024]{2,1,0:T(4,128)S(1)} async-done(((f32[32,3,1024]{2,1,0:T(4,128)}), f32[32,3,1024]{2,1,0:T(4,128)S(1)}, u32[]{:S(2)}, u32[]{:S(2)}) %all-to-all-start) | async-done | bytes 393248 | tf_op jit(solution)/shard_map/all_to_all | solution.py:648
  54.0 7.5 %swish.1 = (bf16[768,1024]{1,0:T(8,128)(2,1)}, f32[8,800,128]{2,1,0:T(8,128)}, f32[32,2,1024]{2,1,0:T(2,128)}) custom-call(s32[2]{0:T(128)} %pad_add_fusion.span_ref, f32[32,3,1024]{2,1,0:T(4,128)} %copy-done, f32[1,1024]{1,0:T(1,128)} %bitcast.27, f32[1,1024]{1,0:T(1,128)} %bitcast.30, f32[8,800,128]{2,1,0:T(8,128)} %get-tuple-element.38.conv_ref, ...), custom_call_target="tpu_custom_call" | custom-call | flops 23592960 | bytes 11010048 | tf_op jit(solution)/shard_map/swish/pallas_call | solution.py:284
  61.5 3.3 %all-to-all-start.1 = ((f32[32,2,1024]{2,1,0:T(2,128)}), f32[32,2,1024]{2,1,0:T(2,128)S(1)}, u32[]{:S(2)}, u32[]{:S(2)}) async-start(f32[32,2,1024]{2,1,0:T(2,128)} %get-tuple-element.40), calls=%async_computation.1 | async-start | bytes 524288 | tf_op jit(solution)/shard_map/all_to_all | solution.py:648
  64.8 4.9 %weight_term.1 = (bf16[512,1024]{1,0:T(8,128)(2,1)}, bf16[512,1024]{1,0:T(8,128)(2,1)}) custom-call(s32[1]{0:T(128)} %bitcast.9.core_ref, bf16[768,1024]{1,0:T(8,128)(2,1)} %get-tuple-element.41.left_ref, bf16[1,768,1024]{2,1,0:T(8,128)(2,1)} %right_ref.1), custom_call_target="tpu_custom_call" | custom-call | flops 1610612736 | bytes 4718592 | tf_op jit(solution)/shard_map/weight_term/pallas_call | solution.py:565
  69.7 2.9 %convolution_convert_fusion = bf16[768,1024]{1,0:T(8,128)(2,1)} fusion(bf16[768,1024]{1,0:T(8,128)(2,1)S(1)} %copy-done.10, bf16[1024,1024]{1,0:T(8,128)(2,1)S(1)} %copy-done.4), kind=kOutput, calls=%fused_computation.1 | convolution fusion | flops 1611399168 | bytes 5242880 | tf_op jit(solution)/shard_map/dot_general | solution.py:22
  72.6 2.5 %all-to-all-done.1.terms_ref = f32[32,2,1024]{2,1,0:T(2,128)S(1)} async-done(((f32[32,2,1024]{2,1,0:T(2,128)}), f32[32,2,1024]{2,1,0:T(2,128)S(1)}, u32[]{:S(2)}, u32[]{:S(2)}) %all-to-all-start.1) | async-done | bytes 262176 | tf_op jit(solution)/shard_map/all_to_all | solution.py:648
  75.9 8.2 %norm_grad.3 = (bf16[2,768,512]{2,1,0:T(8,128)(2,1)}, bf16[4,768,128]{2,1,0:T(8,128)(2,1)}) custom-call(s32[2]{0:T(128)} %pad_add_fusion.span_ref, f32[32,3,1024]{2,1,0:T(4,128)} %copy-done, f32[32,2,1024]{2,1,0:T(2,128)} %copy-done.2, f32[1,1024]{1,0:T(1,128)} %bitcast.28, f32[31,1024]{1,0:T(8,128)} %taps_ref.5, f32[8,800,128]{2,1,0:T(8,128)} %get-tuple-element.38.conv_ref, ...), custom_call_target="tpu_custom_call" | custom-call | flops 27525120 | bytes 6291456 | tf_op jit(solution)/shard_map/norm_grad/pallas_call | solution.py:360
  84.1 8.3 %norm_grad.2 = (bf16[2,768,512]{2,1,0:T(8,128)(2,1)}, bf16[4,768,128]{2,1,0:T(8,128)(2,1)}) custom-call(s32[2]{0:T(128)} %pad_add_fusion.span_ref, f32[32,3,1024]{2,1,0:T(4,128)} %copy-done, f32[32,2,1024]{2,1,0:T(2,128)} %copy-done.2, f32[1,1024]{1,0:T(1,128)} %bitcast.29, f32[31,1024]{1,0:T(8,128)} %taps_ref.5, f32[8,800,128]{2,1,0:T(8,128)} %get-tuple-element.38.conv_ref, ...), custom_call_target="tpu_custom_call" | custom-call | flops 27525120 | bytes 6291456 | tf_op jit(solution)/shard_map/norm_grad/pallas_call | solution.py:360
  93.4 6.3 %tap_grad.2 = f32[31,512]{1,0:T(8,128)} custom-call(bf16[8,64,128]{2,1,0:T(8,128)(2,1)} %get-tuple-element.58.edge_ref, bf16[8,768,128]{2,1,0:T(8,128)(2,1)} %get-tuple-element.34.glu_ref, bf16[4,768,128]{2,1,0:T(8,128)(2,1)} %get-tuple-element.59.dconv_ref), custom_call_target="tpu_custom_call" | custom-call | flops 24379392 | bytes 1572864 | tf_op jit(solution)/shard_map/tap_grad/pallas_call | solution.py:427
  99.7 6.3 %tap_grad.3 = f32[31,512]{1,0:T(8,128)} custom-call(bf16[8,64,128]{2,1,0:T(8,128)(2,1)} %get-tuple-element.58.edge_ref, bf16[8,768,128]{2,1,0:T(8,128)(2,1)} %get-tuple-element.34.glu_ref, bf16[4,768,128]{2,1,0:T(8,128)(2,1)} %get-tuple-element.60.dconv_ref), custom_call_target="tpu_custom_call" | custom-call | flops 24379392 | bytes 1572864 | tf_op jit(solution)/shard_map/tap_grad/pallas_call | solution.py:427
  109.7 8.1 %pair_term.1 = (bf16[256,2048]{1,0:T(8,128)(2,1)}, bf16[256,2048]{1,0:T(8,128)(2,1)}) custom-call(s32[1]{0:T(128)} %bitcast.14.half_ref, bf16[512,768]{1,0:T(8,128)(2,1)} %get-tuple-element.50.left_own, bf16[512,768]{1,0:T(8,128)(2,1)} %collective-permute-done.2.left_got, bf16[2,768,512]{2,1,0:T(8,128)(2,1)} %get-tuple-element.48.refs_0_, ...), custom_call_target="tpu_custom_call" | custom-call | flops 3221225472 | bytes 12582912 | tf_op jit(solution)/shard_map/pair_term/pallas_call | solution.py:530
  121.3 2.4 %combine.1 = (bf16[256,1024]{1,0:T(8,128)(2,1)}, bf16[256,1024]{1,0:T(8,128)(2,1)}) custom-call(s32[1]{0:T(128)} %bitcast.14.half_ref, bf16[512,1024]{1,0:T(8,128)(2,1)} %get-tuple-element.54.keep_other.keep_mine, bf16[512,1024]{1,0:T(8,128)(2,1)} %copy-done.1, bf16[512,1024]{1,0:T(8,128)(2,1)} %get-tuple-element.54.keep_other.keep_mine, ...), custom_call_target="tpu_custom_call" | custom-call | flops 524288 | bytes 3145728 | tf_op jit(solution)/shard_map/combine/pallas_call | solution.py:618
  124.6 7.5 %frames_grad.1 = bf16[768,1024]{1,0:T(8,128)(2,1)} custom-call(bf16[2,768,512]{2,1,0:T(8,128)(2,1)} %get-tuple-element.48.refs_0_, bf16[2,768,512]{2,1,0:T(8,128)(2,1)} %get-tuple-element.49.refs_1_.refs_2_, bf16[1024,2048]{1,0:T(8,128)(2,1)} %refs_2_.1), custom_call_target="tpu_custom_call" | custom-call | flops 3221225472 | bytes 7864320 | tf_op jit(solution)/shard_map/frames_grad/pallas_call | solution.py:463
  133.2 4.0 %collective-permute-done.17 = f32[31,1024]{1,0:T(8,128)S(1)} collective-permute-done((f32[31,1024]{1,0:T(8,128)S(1)}, f32[31,1024]{1,0:T(8,128)S(1)}, u32[]{:S(2)}, u32[]{:S(2)}) %collective-permute-start.17) | collective-permute-done | bytes 127008 | tf_op jit(solution)/shard_map/ppermute | solution.py:655
  141.5 5.6 %collective-permute-done.18 = f32[31,1024]{1,0:T(8,128)S(1)} collective-permute-done((f32[31,1024]{1,0:T(8,128)S(1)}, f32[31,1024]{1,0:T(8,128)S(1)}, u32[]{:S(2)}, u32[]{:S(2)}) %collective-permute-start.18) | collective-permute-done | bytes 127008 | tf_op jit(solution)/shard_map/ppermute | solution.py:655
  148.1 2.9 %collective-permute-done.6 = bf16[128,2048]{1,0:T(8,128)(2,1)S(1)} collective-permute-done((bf16[128,2048]{1,0:T(8,128)(2,1)S(1)}, bf16[128,2048]{1,0:T(8,128)(2,1)S(1)}, u32[]{:S(2)}, u32[]{:S(2)}) %collective-permute-start.6) | collective-permute-done | bytes 524320 | tf_op jit(solution)/shard_map/ppermute | solution.py:643
  155.0 6.2 %collective-permute-done.7 = bf16[64,2048]{1,0:T(8,128)(2,1)S(1)} collective-permute-done((bf16[64,2048]{1,0:T(8,128)(2,1)S(1)}, bf16[64,2048]{1,0:T(8,128)(2,1)S(1)}, u32[]{:S(2)}, u32[]{:S(2)}) %collective-permute-start.7) | collective-permute-done | bytes 262176 | tf_op jit(solution)/shard_map/ppermute | solution.py:643
  162.9 6.5 %collective-permute-done.8 = bf16[32,2048]{1,0:T(8,128)(2,1)S(1)} collective-permute-done((bf16[32,2048]{1,0:T(8,128)(2,1)S(1)}, bf16[32,2048]{1,0:T(8,128)(2,1)S(1)}, u32[]{:S(2)}, u32[]{:S(2)}) %collective-permute-start.8) | collective-permute-done | bytes 131104 | tf_op jit(solution)/shard_map/ppermute | solution.py:643
  (83 shorter events, 27.7 us)
Async XLA Ops:
  2.3 13.1 %collective-permute-start = (bf16[48,1024]{1,0:T(8,128)(2,1)S(1)}, bf16[48,1024]{1,0:T(8,128)(2,1)S(1)}, u32[]{:S(2)}, u32[]{:S(2)}) collective-permute-start(bf16[48,1024]{1,0:T(8,128)(2,1)S(1)} %pad_maximum_fusion.1), channel_id=1, source_target_pairs={{0,1},{1,2},{2,3},{4,5},{5,6},{6,7},{8,9},{9,10},{10,11},{12,13},{... | collective-permute-start | bytes 294920 | tf_op jit(solution)/shard_map/ppermute | solution.py:675
  4.7 10.7 %collective-permute-start.1 = (bf16[48,1024]{1,0:T(8,128)(2,1)S(1)}, bf16[48,1024]{1,0:T(8,128)(2,1)S(1)}, u32[]{:S(2)}, u32[]{:S(2)}) collective-permute-start(bf16[48,1024]{1,0:T(8,128)(2,1)S(1)} %pad_maximum_fusion.2), channel_id=1, source_target_pairs={{1,0},{2,1},{3,2},{5,4},{6,5},{7,6},{9,8},{10,9},{11,10},{13,12},{... | collective-permute-start | bytes 294920 | tf_op jit(solution)/shard_map/ppermute | solution.py:676
  28.5 24.8 %all-to-all-start = ((f32[32,3,1024]{2,1,0:T(4,128)}), f32[32,3,1024]{2,1,0:T(4,128)S(1)}, u32[]{:S(2)}, u32[]{:S(2)}) async-start(f32[32,3,1024]{2,1,0:T(4,128)} %get-tuple-element.35), calls=%async_computation | async-start | bytes 1048576 | tf_op jit(solution)/shard_map/all_to_all | solution.py:648
  61.5 13.7 %all-to-all-start.1 = ((f32[32,2,1024]{2,1,0:T(2,128)}), f32[32,2,1024]{2,1,0:T(2,128)S(1)}, u32[]{:S(2)}, u32[]{:S(2)}) async-start(f32[32,2,1024]{2,1,0:T(2,128)} %get-tuple-element.40), calls=%async_computation.1 | async-start | bytes 524288 | tf_op jit(solution)/shard_map/all_to_all | solution.py:648
  84.1 8.8 %copy-start.11 = (bf16[512,768]{1,0:T(8,128)(2,1)S(1)}, bf16[512,768]{1,0:T(8,128)(2,1)}, u32[]{:S(2)}) copy-start(bf16[512,768]{1,0:T(8,128)(2,1)} %get-tuple-element.51) | copy-start | bytes 2359300
  92.4 17.3 %collective-permute-start.4 = (bf16[2,768,512]{2,1,0:T(8,128)(2,1)}, bf16[2,768,512]{2,1,0:T(8,128)(2,1)}, u32[]{:S(2)}, u32[]{:S(2)}) collective-permute-start(bf16[2,768,512]{2,1,0:T(8,128)(2,1)} %get-tuple-element.49.refs_1_.refs_2_), channel_id=1, source_target_pairs={{0,1},{1,0},{2,3},{3,2},{4,5},{5,4},{6,7},{7,6},{8,9},{9,8},{10,11... | collective-permute-start | bytes 4718600 | tf_op jit(solution)/shard_map/ppermute | solution.py:699
  92.4 17.3 %collective-permute-start.3 = (bf16[2,768,512]{2,1,0:T(8,128)(2,1)}, bf16[2,768,512]{2,1,0:T(8,128)(2,1)}, u32[]{:S(2)}, u32[]{:S(2)}) collective-permute-start(bf16[2,768,512]{2,1,0:T(8,128)(2,1)} %get-tuple-element.48.refs_0_), channel_id=1, source_target_pairs={{0,1},{1,0},{2,3},{3,2},{4,5},{5,4},{6,7},{7,6},{8,9},{9,8},{10,11... | collective-permute-start | bytes 4718600 | tf_op jit(solution)/shard_map/ppermute | solution.py:699
  92.9 16.8 %collective-permute-start.2 = (bf16[512,768]{1,0:T(8,128)(2,1)S(1)}, bf16[512,768]{1,0:T(8,128)(2,1)}, u32[]{:S(2)}, u32[]{:S(2)}) collective-permute-start(bf16[512,768]{1,0:T(8,128)(2,1)S(1)} %copy-done.11), channel_id=1, source_target_pairs={{0,1},{1,0},{2,3},{3,2},{4,5},{5,4},{6,7},{7,6},{8,9},{9,8},{10,11... | collective-permute-start | bytes 2359304 | tf_op jit(solution)/shard_map/ppermute | solution.py:684
  93.0 27.3 %collective-permute-start.9 = (bf16[512,1024]{1,0:T(8,128)(2,1)}, bf16[512,1024]{1,0:T(8,128)(2,1)S(1)}, u32[]{:S(2)}, u32[]{:S(2)}) collective-permute-start(bf16[512,1024]{1,0:T(8,128)(2,1)} %get-tuple-element.55), channel_id=1, source_target_pairs={{0,1},{1,0},{2,3},{3,2},{4,5},{5,4},{6,7},{7,6},{8,9},{9,8},{10,11... | collective-permute-start | bytes 3145736 | tf_op jit(solution)/shard_map/ppermute | solution.py:691
  106.9 1.4 collective-permute-start.14
  109.1 10.2 %collective-permute-start.15 = (f32[31,1024]{1,0:T(8,128)S(1)}, f32[31,1024]{1,0:T(8,128)S(1)}, u32[]{:S(2)}, u32[]{:S(2)}) collective-permute-start(f32[31,1024]{1,0:T(8,128)S(1)} %fusion), channel_id=1, source_target_pairs={{0,2},{1,3},{2,0},{3,1},{4,6},{5,7},{6,4},{7,5},{8,10},{9,11},{10,... | collective-permute-start | bytes 380936 | tf_op jit(solution)/shard_map/ppermute | solution.py:655
  117.8 22.2 %collective-permute-start.5 = (bf16[256,2048]{1,0:T(8,128)(2,1)}, bf16[256,2048]{1,0:T(8,128)(2,1)S(1)}, u32[]{:S(2)}, u32[]{:S(2)}) collective-permute-start(bf16[256,2048]{1,0:T(8,128)(2,1)} %get-tuple-element.53), channel_id=1, source_target_pairs={{0,2},{1,5},{2,0},{3,7},{4,6},{5,1},{6,4},{7,3},{8,10},{9,13},{10,... | collective-permute-start | bytes 3145736 | tf_op jit(solution)/shard_map/ppermute | solution.py:635
  119.3 12.9 %collective-permute-start.16 = (f32[31,1024]{1,0:T(8,128)S(1)}, f32[31,1024]{1,0:T(8,128)S(1)}, u32[]{:S(2)}, u32[]{:S(2)}) collective-permute-start(f32[31,1024]{1,0:T(8,128)S(1)} %add.52), channel_id=1, source_target_pairs={{0,4},{4,0},{8,12},{12,8},{16,20},{20,16},{24,28},{28,24},{1,5},{5... | collective-permute-start | bytes 380936 | tf_op jit(solution)/shard_map/ppermute | solution.py:655
  123.7 8.4 %copy-start.3 = (f32[32,2,1024]{2,1,0:T(2,128)S(1)}, f32[32,2,1024]{2,1,0:T(2,128)}, u32[]{:S(2)}) copy-start(f32[32,2,1024]{2,1,0:T(2,128)} %copy-done.2) | copy-start | bytes 786436
  123.7 15.0 %copy-start.7 = (bf16[256,1024]{1,0:T(8,128)(2,1)S(1)}, bf16[256,1024]{1,0:T(8,128)(2,1)}, u32[]{:S(2)}) copy-start(bf16[256,1024]{1,0:T(8,128)(2,1)} %get-tuple-element.56) | copy-start | bytes 1572868
  123.7 15.0 %collective-permute-start.10 = (bf16[256,1024]{1,0:T(8,128)(2,1)}, bf16[256,1024]{1,0:T(8,128)(2,1)S(1)}, u32[]{:S(2)}, u32[]{:S(2)}) collective-permute-start(bf16[256,1024]{1,0:T(8,128)(2,1)} %get-tuple-element.57), channel_id=1, source_target_pairs={{0,2},{1,5},{2,0},{3,7},{4,6},{5,1},{6,4},{7,3},{8,10},{9,13},{10,... | collective-permute-start | bytes 1572872 | tf_op jit(solution)/shard_map/ppermute | solution.py:635
  132.2 5.0 %collective-permute-start.17 = (f32[31,1024]{1,0:T(8,128)S(1)}, f32[31,1024]{1,0:T(8,128)S(1)}, u32[]{:S(2)}, u32[]{:S(2)}) collective-permute-start(f32[31,1024]{1,0:T(8,128)S(1)} %add.53), channel_id=1, source_target_pairs={{0,8},{4,12},{8,0},{12,4},{16,24},{20,28},{24,16},{28,20},{1,9},{5... | collective-permute-start | bytes 380936 | tf_op jit(solution)/shard_map/ppermute | solution.py:655
  137.3 9.9 %collective-permute-start.18 = (f32[31,1024]{1,0:T(8,128)S(1)}, f32[31,1024]{1,0:T(8,128)S(1)}, u32[]{:S(2)}, u32[]{:S(2)}) collective-permute-start(f32[31,1024]{1,0:T(8,128)S(1)} %add.54), channel_id=1, source_target_pairs={{0,16},{4,20},{8,24},{12,28},{16,0},{20,4},{24,8},{28,12},{1,17},{... | collective-permute-start | bytes 380936 | tf_op jit(solution)/shard_map/ppermute | solution.py:655
  138.9 8.9 %collective-permute-start.11 = (bf16[128,1024]{1,0:T(8,128)(2,1)S(1)}, bf16[128,1024]{1,0:T(8,128)(2,1)S(1)}, u32[]{:S(2)}, u32[]{:S(2)}) collective-permute-start(bf16[128,1024]{1,0:T(8,128)(2,1)S(1)} %broadcast_select_fusion.1), channel_id=1, source_target_pairs={{0,4},{1,3},{2,6},{3,1},{4,0},{5,7},{6,2},{7,5},{8,12},{9,11},{10,... | collective-permute-start | bytes 786440 | tf_op jit(solution)/shard_map/ppermute | solution.py:643
  140.4 10.6 %collective-permute-start.6 = (bf16[128,2048]{1,0:T(8,128)(2,1)S(1)}, bf16[128,2048]{1,0:T(8,128)(2,1)S(1)}, u32[]{:S(2)}, u32[]{:S(2)}) collective-permute-start(bf16[128,2048]{1,0:T(8,128)(2,1)S(1)} %broadcast_select_fusion), channel_id=1, source_target_pairs={{0,4},{1,3},{2,6},{3,1},{4,0},{5,7},{6,2},{7,5},{8,12},{9,11},{10,... | collective-permute-start | bytes 1572872 | tf_op jit(solution)/shard_map/ppermute | solution.py:643
  148.0 5.6 %collective-permute-start.12 = (bf16[64,1024]{1,0:T(8,128)(2,1)S(1)}, bf16[64,1024]{1,0:T(8,128)(2,1)S(1)}, u32[]{:S(2)}, u32[]{:S(2)}) collective-permute-start(bf16[64,1024]{1,0:T(8,128)(2,1)S(1)} %broadcast_select_fusion.3), channel_id=1, source_target_pairs={{0,8},{1,9},{2,10},{3,11},{4,12},{5,13},{6,14},{7,15},{8,0},{9,1},... | collective-permute-start | bytes 393224 | tf_op jit(solution)/shard_map/ppermute | solution.py:643
  151.3 9.9 %collective-permute-start.7 = (bf16[64,2048]{1,0:T(8,128)(2,1)S(1)}, bf16[64,2048]{1,0:T(8,128)(2,1)S(1)}, u32[]{:S(2)}, u32[]{:S(2)}) collective-permute-start(bf16[64,2048]{1,0:T(8,128)(2,1)S(1)} %broadcast_select_fusion.2), channel_id=1, source_target_pairs={{0,8},{1,9},{2,10},{3,11},{4,12},{5,13},{6,14},{7,15},{8,0},{9,1},... | collective-permute-start | bytes 786440 | tf_op jit(solution)/shard_map/ppermute | solution.py:643
  153.6 8.6 %collective-permute-start.13 = (bf16[32,1024]{1,0:T(8,128)(2,1)S(1)}, bf16[32,1024]{1,0:T(8,128)(2,1)S(1)}, u32[]{:S(2)}, u32[]{:S(2)}) collective-permute-start(bf16[32,1024]{1,0:T(8,128)(2,1)S(1)} %broadcast_select_fusion.5), channel_id=1, source_target_pairs={{0,16},{1,17},{2,18},{3,19},{4,20},{5,21},{6,22},{7,23},{8,24},{9,... | collective-permute-start | bytes 196616 | tf_op jit(solution)/shard_map/ppermute | solution.py:643
  161.4 8.1 %collective-permute-start.8 = (bf16[32,2048]{1,0:T(8,128)(2,1)S(1)}, bf16[32,2048]{1,0:T(8,128)(2,1)S(1)}, u32[]{:S(2)}, u32[]{:S(2)}) collective-permute-start(bf16[32,2048]{1,0:T(8,128)(2,1)S(1)} %broadcast_select_fusion.4), channel_id=1, source_target_pairs={{0,16},{1,17},{2,18},{3,19},{4,20},{5,21},{6,22},{7,23},{8,24},{9,... | collective-permute-start | bytes 393224 | tf_op jit(solution)/shard_map/ppermute | solution.py:643
  (9 other events, 27.8 us)

commit v4 on v3

--- a/solution.py
+++ b/solution.py
@@ -201,7 +201,7 @@
 
     prod = dot_nt(left[...], w_ref[...])
     for c in range(SUB):
-        out_ref[c] = prod[:, lanes_of(c)]
+        out_ref[c] = prod[:, lanes_of(c)].astype(BF16)
 
 
 def back_projected(before, cot, after, w_out):
@@ -218,7 +218,7 @@
             pl.BlockSpec((BLOCK, features), lambda j: (j, 0)),
         ],
         out_specs=pl.BlockSpec((SUB, full, LANES), lambda j: (j, 0, 0)),
-        out_shape=jax.ShapeDtypeStruct((channels // LANES, full, LANES), F32),
+        out_shape=jax.ShapeDtypeStruct((channels // LANES, full, LANES), BF16),
         scratch_shapes=[pltpu.VMEM((full, features), BF16)],
         compiler_params=pltpu.CompilerParams(vmem_limit_bytes=VMEM_LIMIT),
         cost_estimate=pl.CostEstimate(
@@ -252,8 +252,8 @@
             live = row_mask(r - NEAR, size, low, high)
             swished = jnp.where(live, shifted * sig, 0.0)
             slope = sig + swished * (1.0 - sig)
-            dshift = jnp.where(live, back_ref[c, at, :] * slope, 0.0)
-            dshift_ref[c, at, :] = dshift
+            dshift = jnp.where(live, back_ref[c, at, :].astype(F32) * slope, 0.0)
+            dshift_ref[c, at, :] = dshift.astype(BF16)
             return normed, swished, dshift
 
         def chunk(i, carry):
@@ -299,7 +299,7 @@
         ],
         out_shape=[
             jax.ShapeDtypeStruct((rows, channels), BF16),
-            jax.ShapeDtypeStruct((groups, full, LANES), F32),
+            jax.ShapeDtypeStruct((groups, full, LANES), BF16),
             jax.ShapeDtypeStruct((devices, 2, channels), F32),
         ],
         compiler_params=pltpu.CompilerParams(vmem_limit_bytes=VMEM_LIMIT),
@@ -332,7 +332,7 @@
         def _(i):
             r = pl.multiple_of(i * span, span)
             normed = (conv_ref[c, pl.ds(r, span), :] - mean) * inv_std
-            value = outer * (dshift_ref[c, pl.ds(r, span), :] - by_bias - normed * by_gain)
+            value = outer * (dshift_ref[c, pl.ds(r, span), :].astype(F32) - by_bias - normed * by_gain)
             live = row_mask(r - NEAR, span, low, high)
             ext[c, pl.ds(r, span), :] = jnp.where(live, value, 0.0).astype(BF16).astype(F32)
 
@@ -388,16 +388,23 @@
     )(span, sums, terms, gain, w_dw, conv, dshift, first, second)
 
 
-def tap_grad_kernel(edge_ref, glu_ref, dconv_ref, out_ref, ext, own):
+def tap_grad_kernel(taps, edge_ref, glu_ref, *refs):
+    *dconv_refs, out_ref, ext, own = refs
     rows = glu_ref.shape[1]
-    taps = out_ref.shape[0]
     shift = WIDE - (taps - 1) // 2
     tiles = 4 if rows % 32 == 0 else 2
+    per = pl.num_programs(0) // len(dconv_refs)
+    for part, dconv_ref in enumerate(dconv_refs):
+
+        @pl.when(pl.program_id(0) // per == part)
+        def _(dconv_ref=dconv_ref):
+            for c in range(SUB):
+                own[c] = dconv_ref[c].astype(F32)
+
     for c in range(SUB):
         ext[c, 0:WIDE, :] = edge_ref[c, 0:WIDE, :].astype(F32)
         ext[c, WIDE : WIDE + rows, :] = glu_ref[c].astype(F32)
         ext[c, WIDE + rows :, :] = edge_ref[c, WIDE:, :].astype(F32)
-        own[c] = dconv_ref[c].astype(F32)
     for c in range(SUB):
 
         def chunk(i, carry):
@@ -416,32 +423,40 @@
 
         zero = jnp.zeros((8, LANES), F32)
         sums = lax.fori_loop(0, rows // (8 * tiles), chunk, (zero,) * taps)
+        out_ref[c] = jnp.zeros(out_ref.shape[1:], F32)
         for k in range(taps):
-            out_ref[k : k + 1, lanes_of(c)] = jnp.sum(sums[k], axis=0, keepdims=True)
-
-
-def tap_grad(edge, glu, dconv, taps, part):
-    groups, rows, _ = dconv.shape
-    channels = groups * LANES
-    at = part * (groups // SUB)
-    return pl.pallas_call(
-        tap_grad_kernel,
-        grid=(groups // SUB,),
+            out_ref[c, k : k + 1, :] = jnp.sum(sums[k], axis=0, keepdims=True)
+
+
+def tap_grad(edge, glu, dconv_parts, taps):
+    groups, rows, _ = glu.shape
+    steps = groups // SUB
+    per = steps // len(dconv_parts)
+    padded = -(-taps // 8) * 8
+    specs = [
+        pl.BlockSpec((SUB, rows, LANES), lambda j, part=part: (jnp.clip(j - part * per, 0, per - 1), 0, 0))
+        for part in range(len(dconv_parts))
+    ]
+    return pl.pallas_call(
+        functools.partial(tap_grad_kernel, taps),
+        grid=(steps,),
         in_specs=[
-            pl.BlockSpec((SUB, 2 * WIDE, LANES), lambda j: (j + at, 0, 0)),
-            pl.BlockSpec((SUB, rows, LANES), lambda j: (j + at, 0, 0)),
+            pl.BlockSpec((SUB, 2 * WIDE, LANES), lambda j: (j, 0, 0)),
             pl.BlockSpec((SUB, rows, LANES), lambda j: (j, 0, 0)),
-        ],
-        out_specs=pl.BlockSpec((taps, BLOCK), lambda j: (0, j)),
-        out_shape=jax.ShapeDtypeStruct((taps, channels), F32),
+            *specs,
+        ],
+        out_specs=pl.BlockSpec((SUB, padded, LANES), lambda j: (j, 0, 0)),
+        out_shape=jax.ShapeDtypeStruct((groups, padded, LANES), F32),
         scratch_shapes=[
             pltpu.VMEM((SUB, rows + 2 * WIDE, LANES), F32),
             pltpu.VMEM((SUB, rows, LANES), F32),
         ],
         compiler_params=pltpu.CompilerParams(vmem_limit_bytes=VMEM_LIMIT),
-        cost_estimate=pl.CostEstimate(flops=62 * rows * channels, bytes_accessed=4 * rows * channels, transcendentals=0),
+        cost_estimate=pl.CostEstimate(
+            flops=62 * rows * groups * LANES, bytes_accessed=4 * rows * groups * LANES, transcendentals=0
+        ),
         name="tap_grad",
-    )(edge, glu, dconv)
+    )(edge, glu, *dconv_parts)
 
 
 def frames_grad_kernel(*refs):
@@ -501,44 +516,34 @@
     )(core, left)
 
 
-def pair_kernel(half_ref, left_own, left_got, *refs):
-    *right_refs, send_ref, keep_ref = refs
-    j = pl.program_id(0)
+def pair_kernel(half_ref, left_own, left_got, own_ref, got_ref, send_ref, keep_ref):
     rows = send_ref.shape[0]
-    for part in range(len(right_refs) // 2):
-
-        @pl.when(j // 2 == part)
-        def _(own=right_refs[2 * part], got=right_refs[2 * part + 1]):
-            term = dot_nn(left_own[...], own[0]) + dot_nn(left_got[...], got[0])
-            low, high = term[:rows], term[rows:]
-            upper = half_ref[0] == 1
-            send_ref[...] = jnp.where(upper, low, high).astype(BF16)
-            keep_ref[...] = jnp.where(upper, high, low).astype(BF16)
+    term = dot_nn(left_own[...], own_ref[0]) + dot_nn(left_got[...], got_ref[0])
+    low, high = term[:rows], term[rows:]
+    upper = half_ref[0] == 1
+    send_ref[...] = jnp.where(upper, low, high).astype(BF16)
+    keep_ref[...] = jnp.where(upper, high, low).astype(BF16)
 
 
 def pair_term(half, left_own, left_got, right_own, right_got):
-    parts = len(right_own)
-    _, rows, width = right_own[0].shape
+    halves, rows, width = right_own.shape
     depth = left_own.shape[0]
     left = pl.BlockSpec((depth, rows), lambda j: (0, 0))
-    out = pl.BlockSpec((depth // 2, width), lambda j: (0, (j % 2) * parts + j // 2))
-    shape = jax.ShapeDtypeStruct((depth // 2, 2 * parts * width), BF16)
-    rights, specs = [], []
-    for part in range(parts):
-        rights += [right_own[part], right_got[part]]
-        specs += [pl.BlockSpec((1, rows, width), lambda j, part=part: (jnp.clip(j - 2 * part, 0, 1), 0, 0))] * 2
+    right = pl.BlockSpec((1, rows, width), lambda j: (j, 0, 0))
+    out = pl.BlockSpec((depth // 2, width), lambda j: (0, j))
+    shape = jax.ShapeDtypeStruct((depth // 2, halves * width), BF16)
     return pl.pallas_call(
         pair_kernel,
-        grid=(2 * parts,),
-        in_specs=[pl.BlockSpec(memory_space=pltpu.SMEM), left, left] + specs,
+        grid=(halves,),
+        in_specs=[pl.BlockSpec(memory_space=pltpu.SMEM), left, left, right, right],
         out_specs=[out, out],
         out_shape=[shape, shape],
         compiler_params=pltpu.CompilerParams(vmem_limit_bytes=VMEM_LIMIT),
         cost_estimate=pl.CostEstimate(
-            flops=8 * parts * rows * depth * width, bytes_accessed=16 * parts * rows * width, transcendentals=0
+            flops=4 * halves * rows * depth * width, bytes_accessed=8 * halves * rows * width, transcendentals=0
         ),
         name="pair_term",
-    )(half.reshape(1), left_own, left_got, *rights)
+    )(half.reshape(1), left_own, left_got, right_own, right_got)
 
 
 def weight_kernel(owner_rows, orders, core_ref, left_ref, right_ref, send_ref, keep_ref):
@@ -630,30 +635,44 @@
     )(half.reshape(1), keep, got, keep, got)
 
 
-def scatter_rest(plan, place, send, keep):
-    everyone = ("dp", "tm")
-    got = lax.ppermute(send, everyone, plan.perm(0))
-    for step in range(1, len(plan.masks[0])):
-        half = plan.own_half(step, place)
-        both = keep.astype(F32) + got.astype(F32)
+class Scatter:
+    def __init__(self, plan, place, parts):
+        self.plan, self.place, self.step = plan, place, 0
+        self.keep = [keep for _, keep in parts]
+        self.got = [self.swap(send) for send, _ in parts]
+
+    def swap(self, send):
+        return lax.ppermute(send, ("dp", "tm"), self.plan.perm(self.step))
+
+    def sums(self):
+        parts = [keep.astype(F32) + got.astype(F32) for keep, got in zip(self.keep, self.got)]
+        return parts[0] if len(parts) == 1 else jnp.concatenate(parts, axis=1)
+
+    def ready(self):
+        self.step += 1
+        half = self.plan.own_half(self.step, self.place)
+        both = self.sums()
         rows = both.shape[0] // 2
         low, high = both[:rows].astype(BF16), both[rows:].astype(BF16)
-        send = jnp.where(half == 1, low, high)
-        keep = jnp.where(half == 1, high, low)
-        got = lax.ppermute(send, everyone, plan.perm(step))
-    return keep.astype(F32) + got.astype(F32)
+        self.keep = [jnp.where(half == 1, high, low)]
+        return jnp.where(half == 1, low, high)
+
+    def go(self, send):
+        self.got = [self.swap(send)]
+
+    def done(self):
+        while self.step + 1 < len(self.plan.masks[0]):
+            self.go(self.ready())
+        return self.sums()
 
 
 def from_all(copies):
     return lax.all_to_all(copies, ("dp", "tm"), 0, 0, tiled=True)
 
 
-def butterfly_sum(x):
-    for axis in ("tm", "dp"):
-        count = lax.axis_size(axis)
-        for i in range((count - 1).bit_length()):
-            x = x + lax.ppermute(x, axis, [(j, j ^ (1 << i)) for j in range(count)])
-    return x
+def shared(owned):
+    count = lax.axis_size("dp") * lax.axis_size("tm")
+    return from_all(jnp.broadcast_to(owned[None], (count,) + owned.shape))
 
 
 def local(frames, lengths, w_in, w_dw, bn_gain, bn_bias, w_out, cotangent):
@@ -680,28 +699,57 @@
     sums = from_all(sums)
     back = back_projected(before, cot, after, w_out)
     left_own, left_other = flipped(core, feats, plan)
-    sums, back, left_other = lax.optimization_barrier((sums, back, left_other))
+    sums, left_other = lax.optimization_barrier((sums, left_other))
     left_got = lax.ppermute(left_other, everyone, plan.perm(-1))
 
+    first_half = plan.own_half(0, place)
     swished, dshift, terms = swish(span, sums, gain, bias, conv, back)
     terms = from_all(terms)
+    out_send, out_keep = weight_term(core, swished, cotangent, plan)
+    out_got = lax.ppermute(out_send, everyone, plan.perm(-1))
     out_rows = dot_nn(swished, w_out).astype(BF16)
-    out_send, out_keep = weight_term(core, swished, cotangent, plan)
-    terms, out_rows, out_send = lax.optimization_barrier((terms, out_rows, out_send))
-    out_got = lax.ppermute(out_send, everyone, plan.perm(-1))
-
-    first_half = plan.own_half(0, place)
+    out_send, out_keep = combine(first_half, out_keep, out_got)
+    terms, out_rows, out_send, left_got = lax.optimization_barrier((terms, out_rows, out_send, left_got))
+    out_scatter = Scatter(plan, place, [(out_send, out_keep)])
+
     parts = 2
-    dpre_own, dpre_got, taps_sum = [], [], []
+    dpre_own, dpre_got, dconv = [], [], []
     for part in range(parts):
-        dpre, dconv = norm_grad(span, sums, terms, gain, w_dw, conv, dshift, first, second, part, parts)
-        dpre_own.append(dpre)
-        dpre_got.append(lax.ppermute(dpre, everyone, plan.perm(-1)))
-        taps_sum.append(tap_grad(edge, glu, dconv, taps, part))
-    kernel_sum = butterfly_sum(jnp.concatenate(taps_sum, axis=1))
-    grad_w_out = scatter_rest(plan, place, *combine(first_half, out_keep, out_got))
-    grad_w_in = scatter_rest(plan, place, *pair_term(first_half, left_own, left_got, dpre_own, dpre_got))
+        own, grads = norm_grad(span, sums, terms, gain, w_dw, conv, dshift, first, second, part, parts)
+        dpre_own.append(own)
+        dconv.append(grads)
+        dpre_got.append(lax.ppermute(own, everyone, plan.perm(-1)))
+        if part == 0:
+            send = out_scatter.ready()
+            dshift, send = lax.optimization_barrier((dshift, send))
+            out_scatter.go(send)
+    in_parts = [pair_term(first_half, left_own, left_got, own, got) for own, got in zip(dpre_own, dpre_got)]
+    in_scatter = Scatter(plan, place, in_parts)
+    send = out_scatter.ready()
+    glu, send, _ = lax.optimization_barrier((glu, send, [send for send, _ in in_parts]))
+    out_scatter.go(send)
+    tap_sums = tap_grad(edge, glu, dconv, taps)
+    tap_sums, in_scatter.got, out_scatter.got = lax.optimization_barrier(
+        (tap_sums, in_scatter.got, out_scatter.got)
+    )
+    out_send, in_send = out_scatter.ready(), in_scatter.ready()
+    in_send, tap_sums = lax.optimization_barrier((in_send, tap_sums))
+    in_scatter.go(in_send)
+    out_scatter.go(out_send)
+    owned = from_all(tap_sums.reshape(device_count, -1, LANES))
+    in_send, *dpre_own = lax.optimization_barrier((in_scatter.ready(), *dpre_own))
+    in_scatter.go(in_send)
     grad_rows = frames_grad(dpre_own, w_in)
+    in_scatter.got, out_scatter.got, grad_rows, owned = lax.optimization_barrier(
+        (in_scatter.got, out_scatter.got, grad_rows, owned)
+    )
+    owned = jnp.sum(owned, axis=0)
+    in_send, owned = lax.optimization_barrier((in_scatter.ready(), owned))
+    in_scatter.go(in_send)
+    kernel_sum = shared(owned).reshape(tap_sums.shape).transpose(1, 0, 2).reshape(-1, depth)[:taps]
+    grad_w_out = out_scatter.done()
+    grad_w_in = in_scatter.done()
+    grad_w_in = grad_w_in.reshape(-1, parts, 2, depth // parts).swapaxes(1, 2).reshape(-1, 2 * depth)
     by_gain, by_bias = jnp.sum(terms, axis=0)
     scale = 1.0 / math.sqrt(device_count * rows)
     return (

time: 171 us -> 163 us (0.953)
  waiting for transfers between devices: 36.4 us -> 21.1 us
  starting transfers between devices: 29.2 us -> 35 us
  local copies, waits for them, and re-layouts: 4.81 us -> 8.46 us
  other arithmetic: 6.51 us -> 3.46 us
    ppermute x15 -> x11, waiting for transfers between devices: 27.2 us -> 11.4 us  [the longest x9 11.3 us: swap(): return lax.ppermute(send, ('dp', 'tm'), self.plan.perm(self.step))]
    all_to_all x2 -> x4, starting transfers between devices: 12.5 us -> 19.7 us  [from_all(): return lax.all_to_all(copies, ('dp', 'tm'), 0, 0, tiled=True)]
    ppermute x15 -> x11, starting transfers between devices: 12.6 us -> 11.1 us  [the longest x9 11 us: swap(): return lax.ppermute(send, ('dp', 'tm'), self.plan.perm(self.step))]
    all_to_all x2 -> x4, waiting for transfers between devices: 9.16 us -> 9.72 us  [from_all(): return lax.all_to_all(copies, ('dp', 'tm'), 0, 0, tiled=True)]
  transfers between devices with their start and end apart: 21 -> 19, of which waited for: 9 -> 5; matrix products, arithmetic and copies ran while one was open for 5% -> 5% of each run, Pallas kernels for 31% -> 39%
where the time goes in v4:
time: 163 us; the launch traced here: 162 us
  Pallas kernels  87.9 us (54%)
  starting transfers between devices  35 us (21%)
  waiting for transfers between devices  21.1 us (13%)
  local copies, waits for them, and re-layouts  8.46 us (5%)
  matrix products  4.34 us (3%)
  other arithmetic  3.46 us (2%)
    all_to_all x4, starting transfers between devices, from_all(): return lax.all_to_all(copies, ('dp', 'tm'), 0, 0, tiled=True)  19.7 us
    pallas_call x2, Pallas kernels, norm_grad(): pl.pallas_call(grad_kernel, grid=(blocks,), in_specs=[pl.BlockSpec(memory...  16.3 us
    pallas_call x1, Pallas kernels, convolved(): pl.pallas_call(conv_kernel, grid=(blocks,), in_specs=[pl.BlockSpec(memory...  12.4 us
    ppermute x9, waiting for transfers between devices, swap(): return lax.ppermute(send, ('dp', 'tm'), self.plan.perm(self.step))  11.3 us
    pallas_call x1, Pallas kernels, tap_grad(): pl.pallas_call(functools.partial(tap_grad_kernel, taps), grid=(steps,), i...  11.1 us
    ppermute x9, starting transfers between devices, swap(): return lax.ppermute(send, ('dp', 'tm'), self.plan.perm(self.step))  11 us
    all_to_all x4, waiting for transfers between devices, from_all(): return lax.all_to_all(copies, ('dp', 'tm'), 0, 0, tiled=True)  9.72 us
    pallas_call x2, Pallas kernels, pair_term(): pl.pallas_call(pair_kernel, grid=(halves,), in_specs=[pl.BlockSpec(memory...  9.39 us
  transfers between devices with their start and end apart: 19, of which 5 were waited for; matrix products, arithmetic and copies ran while one was open for 5% of the time, Pallas kernels for 39%

profile of v4, /device:TPU:0, one launch (start us, length us, event | category | flops | bytes accessed | tf_op | source)
XLA Modules:
  0.0 161.8 jit_solution(2121270345460739822)
XLA Ops:
  2.3 2.4 %collective-permute-start = (bf16[48,1024]{1,0:T(8,128)(2,1)S(1)}, bf16[48,1024]{1,0:T(8,128)(2,1)S(1)}, u32[]{:S(2)}, u32[]{:S(2)}) collective-permute-start(bf16[48,1024]{1,0:T(8,128)(2,1)S(1)} %pad_maximum_fusion), channel_id=1, source_target_pairs={{0,1},{1,2},{2,3},{4,5},{5,6},{6,7},{8,9},{9,10},{10,11},{12,13},{... | collective-permute-start | bytes 294920 | tf_op jit(solution)/shard_map/ppermute | solution.py:694
  7.3 8.1 %gated.1 = (bf16[8,768,128]{2,1,0:T(8,128)(2,1)}, bf16[768,1024]{1,0:T(8,128)(2,1)}, bf16[768,1024]{1,0:T(8,128)(2,1)}) custom-call(s32[2]{0:T(128)} %pad_add_fusion.span_ref, bf16[768,1024]{1,0:T(8,128)(2,1)} %bitcast.33, bf16[1024,2048]{1,0:T(8,128)(2,1)} %refs_2_.1, bf16[1024,2048]{1,0:T(8,128)(2,1)} %refs_2_.1), custom_call_target="tpu_custom_call" | custom-call | flops 3221225472 | bytes 11010048 | tf_op jit(solution)/shard_map/gated/pallas_call | solution.py:87
  16.0 12.4 %convolved.1 = (f32[8,800,128]{2,1,0:T(8,128)}, bf16[8,64,128]{2,1,0:T(8,128)(2,1)}, f32[32,3,1024]{2,1,0:T(4,128)}) custom-call(s32[2]{0:T(128)} %pad_add_fusion.span_ref, bf16[48,1024]{1,0:T(8,128)(2,1)} %copy-done.9, bf16[48,1024]{1,0:T(8,128)(2,1)} %copy-done.10, bf16[1024,2048]{1,0:T(8,128)(2,1)} %refs_2_.1, bf16[1024,2048]{1,0:T(8,128)(2,1)} %refs_2_.1, ...), custom_call_target="tpu_custom_call" | custom-call | flops 3221225472 | bytes 11010048 | tf_op jit(solution)/shard_map/convolved/pallas_call | solution.py:162
  28.4 9.2 %all-to-all-start = ((f32[32,3,1024]{2,1,0:T(4,128)}), f32[32,3,1024]{2,1,0:T(4,128)S(1)}, u32[]{:S(2)}, u32[]{:S(2)}) async-start(f32[32,3,1024]{2,1,0:T(4,128)} %get-tuple-element.56), calls=%async_computation | async-start | bytes 1048576 | tf_op jit(solution)/shard_map/all_to_all | solution.py:670
  37.6 3.1 %flipped.1 = (bf16[512,768]{1,0:T(8,128)(2,1)}, bf16[512,768]{1,0:T(8,128)(2,1)}) custom-call(s32[1]{0:T(128)} %bitcast.8.core_ref, bf16[768,1024]{1,0:T(8,128)(2,1)} %bitcast.34), custom_call_target="tpu_custom_call" | custom-call | flops 3145728 | bytes 3145728 | tf_op jit(solution)/shard_map/flipped/pallas_call | solution.py:508
  40.7 5.6 %back_projected.1.back_ref = bf16[8,800,128]{2,1,0:T(8,128)(2,1)} custom-call(bf16[48,1024]{1,0:T(8,128)(2,1)} %copy-done.9, bf16[768,1024]{1,0:T(8,128)(2,1)} %bitcast.46, bf16[48,1024]{1,0:T(8,128)(2,1)} %copy-done.10, bf16[1024,1024]{1,0:T(8,128)(2,1)} %w_ref.1), custom_call_target="tpu_custom_call" | custom-call | flops 1610612736 | bytes 6291456 | tf_op jit(solution)/shard_map/back_projected/pallas_call | solution.py:211
  46.3 6.8 %all-to-all-done.sums_ref = f32[32,3,1024]{2,1,0:T(4,128)S(1)} async-done(((f32[32,3,1024]{2,1,0:T(4,128)}), f32[32,3,1024]{2,1,0:T(4,128)S(1)}, u32[]{:S(2)}, u32[]{:S(2)}) %all-to-all-start) | async-done | bytes 393248 | tf_op jit(solution)/shard_map/all_to_all | solution.py:670
  54.0 7.0 %swish.1 = (bf16[768,1024]{1,0:T(8,128)(2,1)}, bf16[8,800,128]{2,1,0:T(8,128)(2,1)}, f32[32,2,1024]{2,1,0:T(2,128)}) custom-call(s32[2]{0:T(128)} %pad_add_fusion.span_ref, f32[32,3,1024]{2,1,0:T(4,128)} %copy-done, f32[1,1024]{1,0:T(1,128)} %bitcast.40, f32[1,1024]{1,0:T(1,128)} %bitcast.45, f32[8,800,128]{2,1,0:T(8,128)} %get-tuple-element.59.conv_ref, ...), custom_call_target="tpu_custom_call" | custom-call | flops 23592960 | bytes 11010048 | tf_op jit(solution)/shard_map/swish/pallas_call | solution.py:284
  60.9 5.0 %weight_term.1 = (bf16[512,1024]{1,0:T(8,128)(2,1)}, bf16[512,1024]{1,0:T(8,128)(2,1)}) custom-call(s32[1]{0:T(128)} %bitcast.8.core_ref, bf16[768,1024]{1,0:T(8,128)(2,1)} %get-tuple-element.61.left_ref, bf16[1,768,1024]{2,1,0:T(8,128)(2,1)} %right_ref.1), custom_call_target="tpu_custom_call" | custom-call | flops 1610612736 | bytes 4718592 | tf_op jit(solution)/shard_map/weight_term/pallas_call | solution.py:570
  66.5 3.1 %all-to-all-start.1 = ((f32[32,2,1024]{2,1,0:T(2,128)}), f32[32,2,1024]{2,1,0:T(2,128)S(1)}, u32[]{:S(2)}, u32[]{:S(2)}) async-start(f32[32,2,1024]{2,1,0:T(2,128)} %get-tuple-element.60), calls=%async_computation.1 | async-start | bytes 524288 | tf_op jit(solution)/shard_map/all_to_all | solution.py:670
  69.6 4.3 %convolution_convert_fusion = bf16[768,1024]{1,0:T(8,128)(2,1)} fusion(bf16[768,1024]{1,0:T(8,128)(2,1)} %get-tuple-element.61.left_ref, bf16[1024,1024]{1,0:T(8,128)(2,1)S(1)} %copy-done.7), kind=kOutput, calls=%fused_computation.1 | convolution fusion | flops 1611399168 | bytes 5242880 | tf_op jit(solution)/shard_map/dot_general | solution.py:22
  74.9 2.4 %combine.1 = (bf16[256,1024]{1,0:T(8,128)(2,1)}, bf16[256,1024]{1,0:T(8,128)(2,1)}) custom-call(s32[1]{0:T(128)} %bitcast.12.half_ref, bf16[512,1024]{1,0:T(8,128)(2,1)} %get-tuple-element.62.keep_other.keep_mine, bf16[512,1024]{1,0:T(8,128)(2,1)} %copy-done.1, bf16[512,1024]{1,0:T(8,128)(2,1)} %get-tuple-element.62.keep_other.keep_mine, ...), custom_call_target="tpu_custom_call" | custom-call | flops 524288 | bytes 3145728 | tf_op jit(solution)/shard_map/combine/pallas_call | solution.py:623
  77.3 2.9 %all-to-all-done.1.terms_ref = f32[32,2,1024]{2,1,0:T(2,128)S(1)} async-done(((f32[32,2,1024]{2,1,0:T(2,128)}), f32[32,2,1024]{2,1,0:T(2,128)S(1)}, u32[]{:S(2)}, u32[]{:S(2)}) %all-to-all-start.1) | async-done | bytes 262176 | tf_op jit(solution)/shard_map/all_to_all | solution.py:670
  80.9 8.2 %norm_grad.2 = (bf16[2,768,512]{2,1,0:T(8,128)(2,1)}, bf16[4,768,128]{2,1,0:T(8,128)(2,1)}) custom-call(s32[2]{0:T(128)} %pad_add_fusion.span_ref, f32[32,3,1024]{2,1,0:T(4,128)} %copy-done, f32[32,2,1024]{2,1,0:T(2,128)} %copy-done.2, f32[1,1024]{1,0:T(1,128)} %bitcast.41, f32[31,1024]{1,0:T(8,128)} %taps_ref.5, f32[8,800,128]{2,1,0:T(8,128)} %get-tuple-element.59.conv_ref, ...), custom_call_target="tpu_custom_call" | custom-call | flops 27525120 | bytes 6291456 | tf_op jit(solution)/shard_map/norm_grad/pallas_call | solution.py:360
  89.8 8.1 %norm_grad.3 = (bf16[2,768,512]{2,1,0:T(8,128)(2,1)}, bf16[4,768,128]{2,1,0:T(8,128)(2,1)}) custom-call(s32[2]{0:T(128)} %pad_add_fusion.span_ref, f32[32,3,1024]{2,1,0:T(4,128)} %copy-done, f32[32,2,1024]{2,1,0:T(2,128)} %copy-done.2, f32[1,1024]{1,0:T(1,128)} %bitcast.42, f32[31,1024]{1,0:T(8,128)} %taps_ref.5, f32[8,800,128]{2,1,0:T(8,128)} %get-tuple-element.59.conv_ref, ...), custom_call_target="tpu_custom_call" | custom-call | flops 27525120 | bytes 6291456 | tf_op jit(solution)/shard_map/norm_grad/pallas_call | solution.py:360
  100.3 4.7 %pair_term.2 = (bf16[256,1024]{1,0:T(8,128)(2,1)}, bf16[256,1024]{1,0:T(8,128)(2,1)}) custom-call(s32[1]{0:T(128)} %bitcast.12.half_ref, bf16[512,768]{1,0:T(8,128)(2,1)} %get-tuple-element.67.left_own, bf16[512,768]{1,0:T(8,128)(2,1)} %collective-permute-done.3.left_got, bf16[2,768,512]{2,1,0:T(8,128)(2,1)} %get-tuple-element.94.own_ref.refs_0_, ...), custom_call_target="tpu_custom_call" | custom-call | flops 1610612736 | bytes 6291456 | tf_op jit(solution)/shard_map/pair_term/pallas_call | solution.py:535
  106.1 4.7 %pair_term.3 = (bf16[256,1024]{1,0:T(8,128)(2,1)}, bf16[256,1024]{1,0:T(8,128)(2,1)}) custom-call(s32[1]{0:T(128)} %bitcast.12.half_ref, bf16[512,768]{1,0:T(8,128)(2,1)} %get-tuple-element.67.left_own, bf16[512,768]{1,0:T(8,128)(2,1)} %collective-permute-done.3.left_got, bf16[2,768,512]{2,1,0:T(8,128)(2,1)} %get-tuple-element.95.own_ref.refs_1_, ...), custom_call_target="tpu_custom_call" | custom-call | flops 1610612736 | bytes 6291456 | tf_op jit(solution)/shard_map/pair_term/pallas_call | solution.py:535
  112.6 11.1 %tap_grad.1 = f32[8,32,128]{2,1,0:T(8,128)} custom-call(bf16[8,64,128]{2,1,0:T(8,128)(2,1)} %get-tuple-element.75.edge_ref, bf16[8,768,128]{2,1,0:T(8,128)(2,1)} %get-tuple-element.83.glu_ref, bf16[4,768,128]{2,1,0:T(8,128)(2,1)} %get-tuple-element.84.refs_0_, bf16[4,768,128]{2,1,0:T(8,128)(2,1)} %get-tuple-element.85.refs_1_), custom_call_target="tpu_custom_call" | custom-call | flops 48758784 | bytes 3145728 | tf_op jit(solution)/shard_map/tap_grad/pallas_call | solution.py:440
  127.8 3.7 %all-to-all-start.2 = ((f32[32,8,128]{2,1,0:T(8,128)}), f32[32,8,128]{2,1,0:T(8,128)S(1)}, u32[]{:S(2)}, u32[]{:S(2)}) async-start(f32[32,8,128]{2,1,0:T(8,128)} %bitcast.14), calls=%async_computation.2 | async-start | bytes 262144 | tf_op jit(solution)/shard_map/all_to_all | solution.py:670
  131.4 2.1 %collective-permute-done.11 = bf16[128,2048]{1,0:T(8,128)(2,1)S(1)} collective-permute-done((bf16[128,2048]{1,0:T(8,128)(2,1)S(1)}, bf16[128,2048]{1,0:T(8,128)(2,1)S(1)}, u32[]{:S(2)}, u32[]{:S(2)}) %collective-permute-start.11) | collective-permute-done | bytes 524320 | tf_op jit(solution)/shard_map/ppermute | solution.py:645
  135.4 7.5 %frames_grad.1 = bf16[768,1024]{1,0:T(8,128)(2,1)} custom-call(bf16[2,768,512]{2,1,0:T(8,128)(2,1)} %get-tuple-element.94.own_ref.refs_0_, bf16[2,768,512]{2,1,0:T(8,128)(2,1)} %get-tuple-element.95.own_ref.refs_1_, bf16[1024,2048]{1,0:T(8,128)(2,1)} %refs_2_.1), custom_call_target="tpu_custom_call" | custom-call | flops 3221225472 | bytes 7864320 | tf_op jit(solution)/shard_map/frames_grad/pallas_call | solution.py:478
  143.7 3.7 %all-to-all-start.3 = ((f32[32,8,128]{2,1,0:T(8,128)}), f32[32,8,128]{2,1,0:T(8,128)S(1)}, u32[]{:S(2)}, u32[]{:S(2)}) async-start(f32[32,8,128]{2,1,0:T(8,128)} %broadcast_in_dim.22), calls=%async_computation.3 | async-start | bytes 262144 | tf_op jit(solution)/shard_map/all_to_all | solution.py:670
  147.5 2.7 %collective-permute-start.14 = (bf16[32,2048]{1,0:T(8,128)(2,1)S(1)}, bf16[32,2048]{1,0:T(8,128)(2,1)S(1)}, u32[]{:S(2)}, u32[]{:S(2)}) collective-permute-start(bf16[32,2048]{1,0:T(8,128)(2,1)S(1)} %broadcast_select_fusion.3), channel_id=1, source_target_pairs={{0,16},{1,17},{2,18},{3,19},{4,20},{5,21},{6,22},{7,23},{8,24},{9,... | collective-permute-start | bytes 393224 | tf_op jit(solution)/shard_map/ppermute | solution.py:645
  150.9 8.8 %collective-permute-done.14 = bf16[32,2048]{1,0:T(8,128)(2,1)S(1)} collective-permute-done((bf16[32,2048]{1,0:T(8,128)(2,1)S(1)}, bf16[32,2048]{1,0:T(8,128)(2,1)S(1)}, u32[]{:S(2)}, u32[]{:S(2)}) %collective-permute-start.14) | collective-permute-done | bytes 131104 | tf_op jit(solution)/shard_map/ppermute | solution.py:645
  (81 shorter events, 22.6 us)
Async XLA Ops:
  2.3 13.0 %collective-permute-start = (bf16[48,1024]{1,0:T(8,128)(2,1)S(1)}, bf16[48,1024]{1,0:T(8,128)(2,1)S(1)}, u32[]{:S(2)}, u32[]{:S(2)}) collective-permute-start(bf16[48,1024]{1,0:T(8,128)(2,1)S(1)} %pad_maximum_fusion), channel_id=1, source_target_pairs={{0,1},{1,2},{2,3},{4,5},{5,6},{6,7},{8,9},{9,10},{10,11},{12,13},{... | collective-permute-start | bytes 294920 | tf_op jit(solution)/shard_map/ppermute | solution.py:694
  4.7 10.7 %collective-permute-start.1 = (bf16[48,1024]{1,0:T(8,128)(2,1)S(1)}, bf16[48,1024]{1,0:T(8,128)(2,1)S(1)}, u32[]{:S(2)}, u32[]{:S(2)}) collective-permute-start(bf16[48,1024]{1,0:T(8,128)(2,1)S(1)} %pad_maximum_fusion.1), channel_id=1, source_target_pairs={{1,0},{2,1},{3,2},{5,4},{6,5},{7,6},{9,8},{10,9},{11,10},{13,12},{... | collective-permute-start | bytes 294920 | tf_op jit(solution)/shard_map/ppermute | solution.py:695
  28.4 24.8 %all-to-all-start = ((f32[32,3,1024]{2,1,0:T(4,128)}), f32[32,3,1024]{2,1,0:T(4,128)S(1)}, u32[]{:S(2)}, u32[]{:S(2)}) async-start(f32[32,3,1024]{2,1,0:T(4,128)} %get-tuple-element.56), calls=%async_computation | async-start | bytes 1048576 | tf_op jit(solution)/shard_map/all_to_all | solution.py:670
  60.9 8.6 %copy-start.7 = (bf16[1024,1024]{1,0:T(8,128)(2,1)S(1)}, bf16[1024,1024]{1,0:T(8,128)(2,1)}, u32[]{:S(2)}) copy-start(bf16[1024,1024]{1,0:T(8,128)(2,1)} %w_ref.1) | copy-start | bytes 6291460
  66.0 8.0 %collective-permute-start.2 = (bf16[512,1024]{1,0:T(8,128)(2,1)}, bf16[512,1024]{1,0:T(8,128)(2,1)S(1)}, u32[]{:S(2)}, u32[]{:S(2)}) collective-permute-start(bf16[512,1024]{1,0:T(8,128)(2,1)} %get-tuple-element.63), channel_id=1, source_target_pairs={{0,1},{1,0},{2,3},{3,2},{4,5},{5,4},{6,7},{7,6},{8,9},{9,8},{10,11... | collective-permute-start | bytes 3145736 | tf_op jit(solution)/shard_map/ppermute | solution.py:709
  66.0 14.2 %collective-permute-start.3 = (bf16[512,768]{1,0:T(8,128)(2,1)}, bf16[512,768]{1,0:T(8,128)(2,1)}, u32[]{:S(2)}, u32[]{:S(2)}) collective-permute-start(bf16[512,768]{1,0:T(8,128)(2,1)} %get-tuple-element.65), channel_id=1, source_target_pairs={{0,1},{1,0},{2,3},{3,2},{4,5},{5,4},{6,7},{7,6},{8,9},{9,8},{10,11... | collective-permute-start | bytes 2359304 | tf_op jit(solution)/shard_map/ppermute | solution.py:703
  66.5 13.7 %all-to-all-start.1 = ((f32[32,2,1024]{2,1,0:T(2,128)}), f32[32,2,1024]{2,1,0:T(2,128)S(1)}, u32[]{:S(2)}, u32[]{:S(2)}) async-start(f32[32,2,1024]{2,1,0:T(2,128)} %get-tuple-element.60), calls=%async_computation.1 | async-start | bytes 524288 | tf_op jit(solution)/shard_map/all_to_all | solution.py:670
  80.2 9.4 %collective-permute-start.5 = (bf16[256,1024]{1,0:T(8,128)(2,1)}, bf16[256,1024]{1,0:T(8,128)(2,1)S(1)}, u32[]{:S(2)}, u32[]{:S(2)}) collective-permute-start(bf16[256,1024]{1,0:T(8,128)(2,1)} %get-tuple-element.77), channel_id=1, source_target_pairs={{0,2},{1,5},{2,0},{3,7},{4,6},{5,1},{6,4},{7,3},{8,10},{9,13},{10,... | collective-permute-start | bytes 1572872 | tf_op jit(solution)/shard_map/ppermute | solution.py:645
  80.9 8.7 %copy-start.4 = (bf16[256,1024]{1,0:T(8,128)(2,1)S(1)}, bf16[256,1024]{1,0:T(8,128)(2,1)}, u32[]{:S(2)}) copy-start(bf16[256,1024]{1,0:T(8,128)(2,1)} %get-tuple-element.76) | copy-start | bytes 1572868
  89.1 10.0 %collective-permute-start.4 = (bf16[2,768,512]{2,1,0:T(8,128)(2,1)}, bf16[2,768,512]{2,1,0:T(8,128)(2,1)S(1)}, u32[]{:S(2)}, u32[]{:S(2)}) collective-permute-start(bf16[2,768,512]{2,1,0:T(8,128)(2,1)} %get-tuple-element.94.own_ref.refs_0_), channel_id=1, source_target_pairs={{0,1},{1,0},{2,3},{3,2},{4,5},{5,4},{6,7},{7,6},{8,9},{9,8},{10,11... | collective-permute-start | bytes 4718600 | tf_op jit(solution)/shard_map/ppermute | solution.py:721
  97.9 8.2 %collective-permute-start.7 = (bf16[2,768,512]{2,1,0:T(8,128)(2,1)}, bf16[2,768,512]{2,1,0:T(8,128)(2,1)}, u32[]{:S(2)}, u32[]{:S(2)}) collective-permute-start(bf16[2,768,512]{2,1,0:T(8,128)(2,1)} %get-tuple-element.95.own_ref.refs_1_), channel_id=1, source_target_pairs={{0,1},{1,0},{2,3},{3,2},{4,5},{5,4},{6,7},{7,6},{8,9},{9,8},{10,11... | collective-permute-start | bytes 4718600 | tf_op jit(solution)/shard_map/ppermute | solution.py:721
  98.0 13.7 %collective-permute-start.6 = (bf16[128,1024]{1,0:T(8,128)(2,1)S(1)}, bf16[128,1024]{1,0:T(8,128)(2,1)S(1)}, u32[]{:S(2)}, u32[]{:S(2)}) collective-permute-start(bf16[128,1024]{1,0:T(8,128)(2,1)S(1)} %broadcast_select_fusion.1), channel_id=1, source_target_pairs={{0,4},{1,3},{2,6},{3,1},{4,0},{5,7},{6,2},{7,5},{8,12},{9,11},{10,... | collective-permute-start | bytes 786440 | tf_op jit(solution)/shard_map/ppermute | solution.py:645
  105.0 18.8 %collective-permute-start.8 = (bf16[256,1024]{1,0:T(8,128)(2,1)}, bf16[256,1024]{1,0:T(8,128)(2,1)S(1)}, u32[]{:S(2)}, u32[]{:S(2)}) collective-permute-start(bf16[256,1024]{1,0:T(8,128)(2,1)} %get-tuple-element.79), channel_id=1, source_target_pairs={{0,2},{1,5},{2,0},{3,7},{4,6},{5,1},{6,4},{7,3},{8,10},{9,13},{10,... | collective-permute-start | bytes 1572872 | tf_op jit(solution)/shard_map/ppermute | solution.py:645
  110.9 1.6 copy-start.3
  110.9 12.9 %collective-permute-start.9 = (bf16[256,1024]{1,0:T(8,128)(2,1)}, bf16[256,1024]{1,0:T(8,128)(2,1)S(1)}, u32[]{:S(2)}, u32[]{:S(2)}) collective-permute-start(bf16[256,1024]{1,0:T(8,128)(2,1)} %get-tuple-element.82), channel_id=1, source_target_pairs={{0,2},{1,5},{2,0},{3,7},{4,6},{5,1},{6,4},{7,3},{8,10},{9,13},{10,... | collective-permute-start | bytes 1572872 | tf_op jit(solution)/shard_map/ppermute | solution.py:645
  111.9 11.9 %collective-permute-start.10 = (bf16[64,1024]{1,0:T(8,128)(2,1)S(1)}, bf16[64,1024]{1,0:T(8,128)(2,1)S(1)}, u32[]{:S(2)}, u32[]{:S(2)}) collective-permute-start(bf16[64,1024]{1,0:T(8,128)(2,1)S(1)} %broadcast_select_fusion.4), channel_id=1, source_target_pairs={{0,8},{1,9},{2,10},{3,11},{4,12},{5,13},{6,14},{7,15},{8,0},{9,1},... | collective-permute-start | bytes 393224 | tf_op jit(solution)/shard_map/ppermute | solution.py:645
  112.6 11.2 %copy-start.5 = (bf16[256,1024]{1,0:T(8,128)(2,1)S(1)}, bf16[256,1024]{1,0:T(8,128)(2,1)}, u32[]{:S(2)}) copy-start(bf16[256,1024]{1,0:T(8,128)(2,1)} %get-tuple-element.74) | copy-start | bytes 1572868
  112.6 11.2 %copy-start.6 = (bf16[256,1024]{1,0:T(8,128)(2,1)S(1)}, bf16[256,1024]{1,0:T(8,128)(2,1)}, u32[]{:S(2)}) copy-start(bf16[256,1024]{1,0:T(8,128)(2,1)} %get-tuple-element.88) | copy-start | bytes 1572868
  124.3 9.2 %collective-permute-start.11 = (bf16[128,2048]{1,0:T(8,128)(2,1)S(1)}, bf16[128,2048]{1,0:T(8,128)(2,1)S(1)}, u32[]{:S(2)}, u32[]{:S(2)}) collective-permute-start(bf16[128,2048]{1,0:T(8,128)(2,1)S(1)} %broadcast_select_fusion), channel_id=1, source_target_pairs={{0,4},{1,3},{2,6},{3,1},{4,0},{5,7},{6,2},{7,5},{8,12},{9,11},{10,... | collective-permute-start | bytes 1572872 | tf_op jit(solution)/shard_map/ppermute | solution.py:645
  126.4 16.4 %collective-permute-start.13 = (bf16[32,1024]{1,0:T(8,128)(2,1)S(1)}, bf16[32,1024]{1,0:T(8,128)(2,1)S(1)}, u32[]{:S(2)}, u32[]{:S(2)}) collective-permute-start(bf16[32,1024]{1,0:T(8,128)(2,1)S(1)} %broadcast_select_fusion.5), channel_id=1, source_target_pairs={{0,16},{1,17},{2,18},{3,19},{4,20},{5,21},{6,22},{7,23},{8,24},{9,... | collective-permute-start | bytes 196616 | tf_op jit(solution)/shard_map/ppermute | solution.py:645
  127.8 15.1 %all-to-all-start.2 = ((f32[32,8,128]{2,1,0:T(8,128)}), f32[32,8,128]{2,1,0:T(8,128)S(1)}, u32[]{:S(2)}, u32[]{:S(2)}) async-start(f32[32,8,128]{2,1,0:T(8,128)} %bitcast.14), calls=%async_computation.2 | async-start | bytes 262144 | tf_op jit(solution)/shard_map/all_to_all | solution.py:670
  133.8 9.0 %collective-permute-start.12 = (bf16[64,2048]{1,0:T(8,128)(2,1)S(1)}, bf16[64,2048]{1,0:T(8,128)(2,1)S(1)}, u32[]{:S(2)}, u32[]{:S(2)}) collective-permute-start(bf16[64,2048]{1,0:T(8,128)(2,1)S(1)} %broadcast_select_fusion.2), channel_id=1, source_target_pairs={{0,8},{1,9},{2,10},{3,11},{4,12},{5,13},{6,14},{7,15},{8,0},{9,1},... | collective-permute-start | bytes 786440 | tf_op jit(solution)/shard_map/ppermute | solution.py:645
  143.7 17.3 %all-to-all-start.3 = ((f32[32,8,128]{2,1,0:T(8,128)}), f32[32,8,128]{2,1,0:T(8,128)S(1)}, u32[]{:S(2)}, u32[]{:S(2)}) async-start(f32[32,8,128]{2,1,0:T(8,128)} %broadcast_in_dim.22), calls=%async_computation.3 | async-start | bytes 262144 | tf_op jit(solution)/shard_map/all_to_all | solution.py:670
  147.5 12.2 %collective-permute-start.14 = (bf16[32,2048]{1,0:T(8,128)(2,1)S(1)}, bf16[32,2048]{1,0:T(8,128)(2,1)S(1)}, u32[]{:S(2)}, u32[]{:S(2)}) collective-permute-start(bf16[32,2048]{1,0:T(8,128)(2,1)S(1)} %broadcast_select_fusion.3), channel_id=1, source_target_pairs={{0,16},{1,17},{2,18},{3,19},{4,20},{5,21},{6,22},{7,23},{8,24},{9,... | collective-permute-start | bytes 393224 | tf_op jit(solution)/shard_map/ppermute | solution.py:645
  (6 other events, 5.0 us)

commit v5 on v4

--- a/solution.py
+++ b/solution.py
@@ -15,7 +15,15 @@
 SUB = BLOCK // LANES
 WIDE = 32
 NEAR = 16
-VMEM_LIMIT = 56 << 20
+VMEM_LIMIT = 30 << 20
+
+
+def in_hbm(*arrays):
+    return [pltpu.with_memory_space_constraint(x, pltpu.HBM) for x in arrays]
+
+
+def in_vmem(*arrays):
+    return [pltpu.with_memory_space_constraint(x, pltpu.VMEM) for x in arrays]
 
 
 def dot_nn(a, b):
@@ -66,7 +74,7 @@
 
 def gate_kernel(span_ref, feats_ref, lin_w_ref, gate_w_ref, glu_ref, first_ref, second_ref):
     rows = feats_ref.shape[0]
-    step = 256 if rows % 256 == 0 else rows
+    step = 128 if rows % 128 == 0 else rows
     for r in range(0, rows, step):
         lin = dot_nn(feats_ref[r : r + step, :], lin_w_ref[...])
         sig = logistic(dot_nn(feats_ref[r : r + step, :], gate_w_ref[...]))
@@ -99,16 +107,16 @@
             pl.BlockSpec((rows, BLOCK), lambda j: (0, j)),
         ],
         out_shape=[
-            jax.ShapeDtypeStruct((channels // LANES, rows, LANES), BF16),
-            jax.ShapeDtypeStruct((rows, channels), BF16),
-            jax.ShapeDtypeStruct((rows, channels), BF16),
+            pltpu.HBM((channels // LANES, rows, LANES), BF16),
+            pltpu.HBM((rows, channels), BF16),
+            pltpu.HBM((rows, channels), BF16),
         ],
         compiler_params=pltpu.CompilerParams(vmem_limit_bytes=VMEM_LIMIT),
         cost_estimate=pl.CostEstimate(
             flops=4 * rows * depth * channels, bytes_accessed=14 * rows * channels, transcendentals=rows * channels
         ),
         name="gated",
-    )(span, feats, w_in, w_in)
+    )(span, *in_hbm(feats, w_in, w_in))
 
 
 def conv_kernel(span_ref, before_ref, after_ref, lin_w_ref, gate_w_ref, taps_ref, glu_ref, conv_ref, edge_ref, sums_ref, ext):
@@ -177,9 +185,9 @@
             pl.BlockSpec((devices, 3, BLOCK), lambda j: (0, 0, j)),
         ],
         out_shape=[
-            jax.ShapeDtypeStruct((groups, full, LANES), F32),
-            jax.ShapeDtypeStruct((groups, 2 * WIDE, LANES), BF16),
-            jax.ShapeDtypeStruct((devices, 3, channels), F32),
+            pltpu.VMEM((groups, full, LANES), F32),
+            pltpu.HBM((groups, 2 * WIDE, LANES), BF16),
+            pltpu.HBM((devices, 3, channels), F32),
         ],
         scratch_shapes=[pltpu.VMEM((SUB, rows + 2 * WIDE, LANES), F32)],
         compiler_params=pltpu.CompilerParams(vmem_limit_bytes=VMEM_LIMIT),
@@ -187,7 +195,7 @@
             flops=4 * rows * depth * channels, bytes_accessed=14 * rows * channels, transcendentals=rows * channels
         ),
         name="convolved",
-    )(span, before, after, w_in, w_in, w_dw, glu)
+    )(span, *in_hbm(before, after, w_in, w_in, w_dw, glu))
 
 
 def back_kernel(before_ref, own_ref, after_ref, w_ref, out_ref, left):
@@ -218,14 +226,14 @@
             pl.BlockSpec((BLOCK, features), lambda j: (j, 0)),
         ],
         out_specs=pl.BlockSpec((SUB, full, LANES), lambda j: (j, 0, 0)),
-        out_shape=jax.ShapeDtypeStruct((channels // LANES, full, LANES), BF16),
+        out_shape=pltpu.HBM((channels // LANES, full, LANES), BF16),
         scratch_shapes=[pltpu.VMEM((full, features), BF16)],
         compiler_params=pltpu.CompilerParams(vmem_limit_bytes=VMEM_LIMIT),
         cost_estimate=pl.CostEstimate(
             flops=2 * rows * features * channels, bytes_accessed=8 * rows * channels, transcendentals=0
         ),
         name="back_projected",
-    )(before, cot, after, w_out)
+    )(*in_hbm(before, cot, after, w_out))
 
 
 def moments(sums_ref, c):
@@ -239,7 +247,7 @@
 def swish_kernel(span_ref, sums_ref, gain_ref, bias_ref, conv_ref, back_ref, swished_ref, dshift_ref, terms_ref):
     rows = swished_ref.shape[0]
     low, high = span_ref[0], span_ref[1]
-    count = 128 if rows % 128 == 0 else NEAR
+    count = 384 if rows % 384 == 0 else NEAR
     for c in range(SUB):
         mean, inv_std, _ = moments(sums_ref, c)
         gain, bias = gain_ref[:, lanes_of(c)], bias_ref[:, lanes_of(c)]
@@ -298,16 +306,16 @@
             pl.BlockSpec((devices, 2, BLOCK), lambda j: (0, 0, j)),
         ],
         out_shape=[
-            jax.ShapeDtypeStruct((rows, channels), BF16),
-            jax.ShapeDtypeStruct((groups, full, LANES), BF16),
-            jax.ShapeDtypeStruct((devices, 2, channels), F32),
+            pltpu.HBM((rows, channels), BF16),
+            pltpu.HBM((groups, full, LANES), BF16),
+            pltpu.HBM((devices, 2, channels), F32),
         ],
         compiler_params=pltpu.CompilerParams(vmem_limit_bytes=VMEM_LIMIT),
         cost_estimate=pl.CostEstimate(
             flops=30 * rows * channels, bytes_accessed=14 * rows * channels, transcendentals=rows * channels
         ),
         name="swish",
-    )(span, sums, gain, bias, conv, back)
+    )(span, *in_hbm(sums, gain, bias), *in_vmem(conv), *in_hbm(back))
 
 
 def grad_kernel(
@@ -342,9 +350,11 @@
         def _(i):
             r = pl.multiple_of(i * count, count)
             tiles = taps_chunk(ext, c, r + shift, count, lambda k: taps_ref[taps - 1 - k : taps - k, at], taps)
-            dglu = jnp.concatenate(tiles, axis=0)
-            dpre_ref[0, pl.ds(r, count), at] = (dglu * first_ref[pl.ds(r, count), at].astype(F32)).astype(BF16)
-            dpre_ref[1, pl.ds(r, count), at] = (dglu * second_ref[pl.ds(r, count), at].astype(F32)).astype(BF16)
+            for u in range(0, count // 8, 2):
+                dglu = jnp.concatenate(tiles[u : u + 2], axis=0)
+                own = pl.ds(r + 8 * u, 16)
+                dpre_ref[0, own, at] = (dglu * first_ref[own, at].astype(F32)).astype(BF16)
+                dpre_ref[1, own, at] = (dglu * second_ref[own, at].astype(F32)).astype(BF16)
 
 
 def norm_grad(span, sums, terms, gain, w_dw, conv, dshift, first, second, part, parts):
@@ -376,8 +386,8 @@
             pl.BlockSpec((SUB, rows, LANES), lambda j: (j, 0, 0)),
         ],
         out_shape=[
-            jax.ShapeDtypeStruct((2, rows, channels), BF16),
-            jax.ShapeDtypeStruct((channels // LANES, rows, LANES), BF16),
+            pltpu.HBM((2, rows, channels), BF16),
+            pltpu.HBM((channels // LANES, rows, LANES), BF16),
         ],
         scratch_shapes=[pltpu.VMEM((SUB, full, LANES), F32)],
         compiler_params=pltpu.CompilerParams(vmem_limit_bytes=VMEM_LIMIT),
@@ -385,14 +395,14 @@
             flops=70 * rows * channels, bytes_accessed=16 * rows * channels, transcendentals=0
         ),
         name="norm_grad",
-    )(span, sums, terms, gain, w_dw, conv, dshift, first, second)
+    )(span, *in_hbm(sums, terms, gain, w_dw), *in_vmem(conv), *in_hbm(dshift, first, second))
 
 
 def tap_grad_kernel(taps, edge_ref, glu_ref, *refs):
     *dconv_refs, out_ref, ext, own = refs
     rows = glu_ref.shape[1]
     shift = WIDE - (taps - 1) // 2
-    tiles = 4 if rows % 32 == 0 else 2
+    tiles = 16 if rows % 128 == 0 else 2
     per = pl.num_programs(0) // len(dconv_refs)
     for part, dconv_ref in enumerate(dconv_refs):
 
@@ -456,7 +466,7 @@
             flops=62 * rows * groups * LANES, bytes_accessed=4 * rows * groups * LANES, transcendentals=0
         ),
         name="tap_grad",
-    )(edge, glu, *dconv_parts)
+    )(*in_hbm(edge, glu), *in_hbm(*dconv_parts))
 
 
 def frames_grad_kernel(*refs):
@@ -486,7 +496,7 @@
             flops=2 * rows * depth * outputs, bytes_accessed=10 * rows * depth, transcendentals=0
         ),
         name="frames_grad",
-    )(*dpre_parts, w_in)
+    )(*in_hbm(*dpre_parts, w_in))
 
 
 def flip_kernel(owner_rows, orders, core_ref, left_ref, mine_ref, other_ref):
@@ -504,7 +514,7 @@
 def flipped(core, left, plan):
     rows, depth = left.shape
     owner_rows = depth // (2 * len(plan.blocks[0]))
-    shape = jax.ShapeDtypeStruct((depth // 2, rows), BF16)
+    shape = pltpu.HBM((depth // 2, rows), BF16)
     return pl.pallas_call(
         functools.partial(flip_kernel, owner_rows, plan.blocks),
         in_specs=[pl.BlockSpec(memory_space=pltpu.SMEM), pl.BlockSpec(memory_space=pltpu.VMEM)],
@@ -513,7 +523,7 @@
         compiler_params=pltpu.CompilerParams(vmem_limit_bytes=VMEM_LIMIT),
         cost_estimate=pl.CostEstimate(flops=4 * rows * depth, bytes_accessed=4 * rows * depth, transcendentals=0),
         name="flipped",
-    )(core, left)
+    )(core, *in_hbm(left))
 
 
 def pair_kernel(half_ref, left_own, left_got, own_ref, got_ref, send_ref, keep_ref):
@@ -543,7 +553,7 @@
             flops=4 * halves * rows * depth * width, bytes_accessed=8 * halves * rows * width, transcendentals=0
         ),
         name="pair_term",
-    )(half.reshape(1), left_own, left_got, right_own, right_got)
+    )(half.reshape(1), *in_hbm(left_own, left_got, right_own, right_got))
 
 
 def weight_kernel(owner_rows, orders, core_ref, left_ref, right_ref, send_ref, keep_ref):
@@ -578,11 +588,8 @@
         out_specs=[out, out],
         out_shape=[shape, shape],
         compiler_params=pltpu.CompilerParams(vmem_limit_bytes=VMEM_LIMIT),
-        cost_estimate=pl.CostEstimate(
-            flops=2 * halves * rows * depth * width, bytes_accessed=6 * halves * rows * width, transcendentals=0
-        ),
         name="weight_term",
-    )(core, left, right)
+    )(core, *in_hbm(left, right))
 
 
 class Halving:
@@ -630,9 +637,8 @@
         ),
         out_shape=[shape, shape],
         compiler_params=pltpu.CompilerParams(vmem_limit_bytes=VMEM_LIMIT),
-        cost_estimate=pl.CostEstimate(flops=rows * width, bytes_accessed=6 * rows * width, transcendentals=0),
         name="combine",
-    )(half.reshape(1), keep, got, keep, got)
+    )(half.reshape(1), *in_hbm(keep, got, keep, got))
 
 
 class Scatter:
@@ -737,16 +743,12 @@
     in_scatter.go(in_send)
     out_scatter.go(out_send)
     owned = from_all(tap_sums.reshape(device_count, -1, LANES))
+    in_scatter.go(in_scatter.ready())
+    in_scatter.got, out_scatter.got, owned = lax.optimization_barrier((in_scatter.got, out_scatter.got, owned))
+    kernel_sum = shared(jnp.sum(owned, axis=0)).reshape(tap_sums.shape).transpose(1, 0, 2).reshape(-1, depth)[:taps]
     in_send, *dpre_own = lax.optimization_barrier((in_scatter.ready(), *dpre_own))
     in_scatter.go(in_send)
     grad_rows = frames_grad(dpre_own, w_in)
-    in_scatter.got, out_scatter.got, grad_rows, owned = lax.optimization_barrier(
-        (in_scatter.got, out_scatter.got, grad_rows, owned)
-    )
-    owned = jnp.sum(owned, axis=0)
-    in_send, owned = lax.optimization_barrier((in_scatter.ready(), owned))
-    in_scatter.go(in_send)
-    kernel_sum = shared(owned).reshape(tap_sums.shape).transpose(1, 0, 2).reshape(-1, depth)[:taps]
     grad_w_out = out_scatter.done()
     grad_w_in = in_scatter.done()
     grad_w_in = grad_w_in.reshape(-1, parts, 2, depth // parts).swapaxes(1, 2).reshape(-1, 2 * depth)

time: 163 us -> 158 us (0.969)
  Pallas kernels: 87.9 us -> 80.3 us
    pallas_call x2, Pallas kernels: 16.3 us -> 14.6 us  [norm_grad(): pl.pallas_call(grad_kernel, grid=(blocks,), in_specs=[pl.BlockSpec(memory...]
    pallas_call x1, Pallas kernels: 11.1 us -> 9.45 us  [tap_grad(): pl.pallas_call(functools.partial(tap_grad_kernel, taps), grid=(steps,), i...]
  transfers between devices with their start and end apart: 19 -> 19, of which waited for: 5 -> 7; matrix products, arithmetic and copies ran while one was open for 5% -> 6% of each run, Pallas kernels for 39% -> 37%
where the time goes in v5:
time: 158 us; the launch traced here: 157 us
  Pallas kernels  80.3 us (51%)
  starting transfers between devices  34.2 us (22%)
  waiting for transfers between devices  21.4 us (14%)
  local copies, waits for them, and re-layouts  10 us (6%)
  matrix products  5.01 us (3%)
  other arithmetic  3.98 us (3%)
  between operations  1.63 us (1%)
    all_to_all x4, starting transfers between devices, from_all(): return lax.all_to_all(copies, ('dp', 'tm'), 0, 0, tiled=True)  19.6 us
    pallas_call x2, Pallas kernels, norm_grad(): pl.pallas_call(grad_kernel, grid=(blocks,), in_specs=[pl.BlockSpec(memory...  14.6 us
    ppermute x9, waiting for transfers between devices, swap(): return lax.ppermute(send, ('dp', 'tm'), self.plan.perm(self.step))  12.3 us
    pallas_call x1, Pallas kernels, convolved(): pl.pallas_call(conv_kernel, grid=(blocks,), in_specs=[pl.BlockSpec(memory...  12.1 us
    ppermute x9, starting transfers between devices, swap(): return lax.ppermute(send, ('dp', 'tm'), self.plan.perm(self.step))  10.5 us
    pallas_call x1, Pallas kernels, tap_grad(): pl.pallas_call(functools.partial(tap_grad_kernel, taps), grid=(steps,), i...  9.45 us
    all_to_all x4, waiting for transfers between devices, from_all(): return lax.all_to_all(copies, ('dp', 'tm'), 0, 0, tiled=True)  9.03 us
    pallas_call x2, Pallas kernels, pair_term(): pl.pallas_call(pair_kernel, grid=(halves,), in_specs=[pl.BlockSpec(memory...  7.84 us
  transfers between devices with their start and end apart: 19, of which 7 were waited for; matrix products, arithmetic and copies ran while one was open for 6% of the time, Pallas kernels for 37%

profile of v5, /device:TPU:0, one launch (start us, length us, event | category | flops | bytes accessed | tf_op | source)
XLA Modules:
  0.0 156.5 jit_solution(3292719053861773753)
XLA Ops:
  2.3 2.4 %collective-permute-start = (bf16[48,1024]{1,0:T(8,128)(2,1)S(1)}, bf16[48,1024]{1,0:T(8,128)(2,1)S(1)}, u32[]{:S(2)}, u32[]{:S(2)}) collective-permute-start(bf16[48,1024]{1,0:T(8,128)(2,1)S(1)} %pad_maximum_fusion), channel_id=1, source_target_pairs={{0,1},{1,2},{2,3},{4,5},{5,6},{6,7},{8,9},{9,10},{10,11},{12,13},{... | collective-permute-start | bytes 294920 | tf_op jit(solution)/shard_map/ppermute | solution.py:700
  6.7 7.7 %gated.1 = (bf16[8,768,128]{2,1,0:T(8,128)(2,1)}, bf16[768,1024]{1,0:T(8,128)(2,1)}, bf16[768,1024]{1,0:T(8,128)(2,1)}) custom-call(s32[2]{0:T(128)S(1)} %pad_add_fusion.span_ref, bf16[768,1024]{1,0:T(8,128)(2,1)} %bitcast.33, bf16[1024,2048]{1,0:T(8,128)(2,1)} %refs_2_.1, bf16[1024,2048]{1,0:T(8,128)(2,1)} %refs_2_.1), custom_call_target="tpu_custom_call" | custom-call | flops 3221225472 | bytes 11010048 | tf_op jit(solution)/shard_map/gated/pallas_call | solution.py:95
  15.1 12.1 %convolved.1 = (f32[8,800,128]{2,1,0:T(8,128)S(1)}, bf16[8,64,128]{2,1,0:T(8,128)(2,1)}, f32[32,3,1024]{2,1,0:T(4,128)}) custom-call(s32[2]{0:T(128)S(1)} %pad_add_fusion.span_ref, bf16[48,1024]{1,0:T(8,128)(2,1)} %copy-done.9, bf16[48,1024]{1,0:T(8,128)(2,1)} %copy-done.10, bf16[1024,2048]{1,0:T(8,128)(2,1)} %refs_2_.1, bf16[1024,2048]{1,0:T(8,128)(2,1)} %refs_2_.1, ...), custom_call_target="tpu_custom_call" | custom-call | flops 3221225472 | bytes 11010048 | tf_op jit(solution)/shard_map/convolved/pallas_call | solution.py:170
  27.2 9.3 %all-to-all-start = ((f32[32,3,1024]{2,1,0:T(4,128)}), f32[32,3,1024]{2,1,0:T(4,128)}, u32[]{:S(2)}, u32[]{:S(2)}) async-start(f32[32,3,1024]{2,1,0:T(4,128)} %get-tuple-element.53), calls=%async_computation | async-start | bytes 1048576 | tf_op jit(solution)/shard_map/all_to_all | solution.py:676
  36.6 3.1 %flipped.1 = (bf16[512,768]{1,0:T(8,128)(2,1)}, bf16[512,768]{1,0:T(8,128)(2,1)}) custom-call(s32[1]{0:T(128)} %bitcast.8.core_ref, bf16[768,1024]{1,0:T(8,128)(2,1)} %bitcast.34), custom_call_target="tpu_custom_call" | custom-call | flops 3145728 | bytes 3145728 | tf_op jit(solution)/shard_map/flipped/pallas_call | solution.py:518
  39.7 5.6 %back_projected.1.back_ref = bf16[8,800,128]{2,1,0:T(8,128)(2,1)} custom-call(bf16[48,1024]{1,0:T(8,128)(2,1)} %copy-done.9, bf16[768,1024]{1,0:T(8,128)(2,1)} %bitcast.35, bf16[48,1024]{1,0:T(8,128)(2,1)} %copy-done.10, bf16[1024,1024]{1,0:T(8,128)(2,1)} %w_ref.1), custom_call_target="tpu_custom_call" | custom-call | flops 1610612736 | bytes 6291456 | tf_op jit(solution)/shard_map/back_projected/pallas_call | solution.py:219
  45.3 6.8 %all-to-all-done.sums_ref = f32[32,3,1024]{2,1,0:T(4,128)} async-done(((f32[32,3,1024]{2,1,0:T(4,128)}), f32[32,3,1024]{2,1,0:T(4,128)}, u32[]{:S(2)}, u32[]{:S(2)}) %all-to-all-start) | async-done | bytes 393248 | tf_op jit(solution)/shard_map/all_to_all | solution.py:676
  52.1 6.0 %swish.1 = (bf16[768,1024]{1,0:T(8,128)(2,1)}, bf16[8,800,128]{2,1,0:T(8,128)(2,1)}, f32[32,2,1024]{2,1,0:T(2,128)}) custom-call(s32[2]{0:T(128)S(1)} %pad_add_fusion.span_ref, f32[32,3,1024]{2,1,0:T(4,128)} %all-to-all-done.sums_ref, f32[1,1024]{1,0:T(1,128)} %bitcast.41, f32[1,1024]{1,0:T(1,128)} %bitcast.46, ...), custom_call_target="tpu_custom_call" | custom-call | flops 23592960 | bytes 11010048 | tf_op jit(solution)/shard_map/swish/pallas_call | solution.py:292
  58.1 4.6 %weight_term.1 = (bf16[512,1024]{1,0:T(8,128)(2,1)}, bf16[512,1024]{1,0:T(8,128)(2,1)S(1)}) custom-call(s32[1]{0:T(128)} %bitcast.8.core_ref, bf16[768,1024]{1,0:T(8,128)(2,1)} %get-tuple-element.58.left_ref, bf16[1,768,1024]{2,1,0:T(8,128)(2,1)} %right_ref.1), custom_call_target="tpu_custom_call" | custom-call | tf_op jit(solution)/shard_map/weight_term/pallas_call | solution.py:580
  64.2 3.1 %all-to-all-start.1 = ((f32[32,2,1024]{2,1,0:T(2,128)}), f32[32,2,1024]{2,1,0:T(2,128)S(1)}, u32[]{:S(2)}, u32[]{:S(2)}) async-start(f32[32,2,1024]{2,1,0:T(2,128)} %get-tuple-element.57), calls=%async_computation.1 | async-start | bytes 524288 | tf_op jit(solution)/shard_map/all_to_all | solution.py:676
  67.3 5.0 %convolution_convert_fusion = bf16[768,1024]{1,0:T(8,128)(2,1)} fusion(bf16[768,1024]{1,0:T(8,128)(2,1)} %get-tuple-element.58.left_ref, bf16[1024,1024]{1,0:T(8,128)(2,1)} %w_ref.1), kind=kOutput, calls=%fused_computation.1 | convolution fusion | flops 1611399168 | bytes 5242880 | tf_op jit(solution)/shard_map/dot_general | solution.py:30
  72.3 1.7 %combine.1 = (bf16[256,1024]{1,0:T(8,128)(2,1)S(1)}, bf16[256,1024]{1,0:T(8,128)(2,1)S(1)}) custom-call(s32[1]{0:T(128)} %bitcast.12.half_ref, bf16[512,1024]{1,0:T(8,128)(2,1)} %copy-done, bf16[512,1024]{1,0:T(8,128)(2,1)} %collective-permute-done.2.got_other.got_mine, bf16[512,1024]{1,0:T(8,128)(2,1)} %copy-done, ...), custom_call_target="tpu_custom_call" | custom-call | tf_op jit(solution)/shard_map/combine/pallas_call | solution.py:630
  75.7 2.2 %all-to-all-done.1.terms_ref = f32[32,2,1024]{2,1,0:T(2,128)S(1)} async-done(((f32[32,2,1024]{2,1,0:T(2,128)}), f32[32,2,1024]{2,1,0:T(2,128)S(1)}, u32[]{:S(2)}, u32[]{:S(2)}) %all-to-all-start.1) | async-done | bytes 262176 | tf_op jit(solution)/shard_map/all_to_all | solution.py:676
  78.6 7.3 %norm_grad.2 = (bf16[2,768,512]{2,1,0:T(8,128)(2,1)}, bf16[4,768,128]{2,1,0:T(8,128)(2,1)}) custom-call(s32[2]{0:T(128)S(1)} %pad_add_fusion.span_ref, f32[32,3,1024]{2,1,0:T(4,128)} %all-to-all-done.sums_ref, f32[32,2,1024]{2,1,0:T(2,128)} %copy-done.6, f32[1,1024]{1,0:T(1,128)} %bitcast.42, f32[31,1024]{1,0:T(8,128)} %taps_ref.5, ...), custom_call_target="tpu_custom_call" | custom-call | flops 27525120 | bytes 6291456 | tf_op jit(solution)/shard_map/norm_grad/pallas_call | solution.py:370
  89.5 7.3 %norm_grad.3 = (bf16[2,768,512]{2,1,0:T(8,128)(2,1)}, bf16[4,768,128]{2,1,0:T(8,128)(2,1)}) custom-call(s32[2]{0:T(128)S(1)} %pad_add_fusion.span_ref, f32[32,3,1024]{2,1,0:T(4,128)} %all-to-all-done.sums_ref, f32[32,2,1024]{2,1,0:T(2,128)} %copy-done.6, f32[1,1024]{1,0:T(1,128)} %bitcast.43, f32[31,1024]{1,0:T(8,128)} %taps_ref.5, ...), custom_call_target="tpu_custom_call" | custom-call | flops 27525120 | bytes 6291456 | tf_op jit(solution)/shard_map/norm_grad/pallas_call | solution.py:370
  97.7 3.9 %pair_term.2 = (bf16[256,1024]{1,0:T(8,128)(2,1)S(1)}, bf16[256,1024]{1,0:T(8,128)(2,1)S(1)}) custom-call(s32[1]{0:T(128)} %bitcast.12.half_ref, bf16[512,768]{1,0:T(8,128)(2,1)} %get-tuple-element.64.left_own, bf16[512,768]{1,0:T(8,128)(2,1)} %collective-permute-done.3.left_got, bf16[2,768,512]{2,1,0:T(8,128)(2,1)} %get-tuple-element.92.own_ref.refs_0_, ...), custom_call_target="tpu_custom_call" | custom-call | flops 1610612736 | bytes 6291456 | tf_op jit(solution)/shard_map/pair_term/pallas_call | solution.py:545
  103.7 3.9 %pair_term.3 = (bf16[256,1024]{1,0:T(8,128)(2,1)S(1)}, bf16[256,1024]{1,0:T(8,128)(2,1)S(1)}) custom-call(s32[1]{0:T(128)} %bitcast.12.half_ref, bf16[512,768]{1,0:T(8,128)(2,1)} %get-tuple-element.64.left_own, bf16[512,768]{1,0:T(8,128)(2,1)} %collective-permute-done.3.left_got, bf16[2,768,512]{2,1,0:T(8,128)(2,1)} %get-tuple-element.93.own_ref.refs_1_, ...), custom_call_target="tpu_custom_call" | custom-call | flops 1610612736 | bytes 6291456 | tf_op jit(solution)/shard_map/pair_term/pallas_call | solution.py:545
  109.8 9.4 %tap_grad.1 = f32[8,32,128]{2,1,0:T(8,128)} custom-call(bf16[8,64,128]{2,1,0:T(8,128)(2,1)} %get-tuple-element.72.edge_ref, bf16[8,768,128]{2,1,0:T(8,128)(2,1)} %get-tuple-element.80.glu_ref, bf16[4,768,128]{2,1,0:T(8,128)(2,1)} %get-tuple-element.81.refs_0_, bf16[4,768,128]{2,1,0:T(8,128)(2,1)} %get-tuple-element.82.refs_1_), custom_call_target="tpu_custom_call" | custom-call | flops 48758784 | bytes 3145728 | tf_op jit(solution)/shard_map/tap_grad/pallas_call | solution.py:450
  121.4 3.5 %all-to-all-start.2 = ((f32[32,8,128]{2,1,0:T(8,128)}), f32[32,8,128]{2,1,0:T(8,128)S(1)}, u32[]{:S(2)}, u32[]{:S(2)}) async-start(f32[32,8,128]{2,1,0:T(8,128)} %bitcast.14), calls=%async_computation.2 | async-start | bytes 262144 | tf_op jit(solution)/shard_map/all_to_all | solution.py:676
  125.0 4.8 %collective-permute-done.11 = bf16[128,2048]{1,0:T(8,128)(2,1)S(1)} collective-permute-done((bf16[128,2048]{1,0:T(8,128)(2,1)S(1)}, bf16[128,2048]{1,0:T(8,128)(2,1)S(1)}, u32[]{:S(2)}, u32[]{:S(2)}) %collective-permute-start.11) | collective-permute-done | bytes 524320 | tf_op jit(solution)/shard_map/ppermute | solution.py:651
  132.9 4.2 %collective-permute-done.13 = bf16[32,1024]{1,0:T(8,128)(2,1)S(1)} collective-permute-done((bf16[32,1024]{1,0:T(8,128)(2,1)S(1)}, bf16[32,1024]{1,0:T(8,128)(2,1)S(1)}, u32[]{:S(2)}, u32[]{:S(2)}) %collective-permute-start.13) | collective-permute-done | bytes 65568 | tf_op jit(solution)/shard_map/ppermute | solution.py:651
  138.5 3.6 %all-to-all-start.3 = ((f32[32,8,128]{2,1,0:T(8,128)}), f32[32,8,128]{2,1,0:T(8,128)S(1)}, u32[]{:S(2)}, u32[]{:S(2)}) async-start(f32[32,8,128]{2,1,0:T(8,128)} %broadcast_in_dim.22), calls=%async_computation.3 | async-start | bytes 262144 | tf_op jit(solution)/shard_map/all_to_all | solution.py:676
  142.2 2.7 %collective-permute-start.14 = (bf16[32,2048]{1,0:T(8,128)(2,1)S(1)}, bf16[32,2048]{1,0:T(8,128)(2,1)S(1)}, u32[]{:S(2)}, u32[]{:S(2)}) collective-permute-start(bf16[32,2048]{1,0:T(8,128)(2,1)S(1)} %broadcast_select_fusion.4), channel_id=1, source_target_pairs={{0,16},{1,17},{2,18},{3,19},{4,20},{5,21},{6,22},{7,23},{8,24},{9,... | collective-permute-start | bytes 393224 | tf_op jit(solution)/shard_map/ppermute | solution.py:651
  144.9 7.5 %frames_grad.1 = bf16[768,1024]{1,0:T(8,128)(2,1)} custom-call(bf16[2,768,512]{2,1,0:T(8,128)(2,1)} %get-tuple-element.92.own_ref.refs_0_, bf16[2,768,512]{2,1,0:T(8,128)(2,1)} %get-tuple-element.93.own_ref.refs_1_, bf16[1024,2048]{1,0:T(8,128)(2,1)} %refs_2_.1), custom_call_target="tpu_custom_call" | custom-call | flops 3221225472 | bytes 7864320 | tf_op jit(solution)/shard_map/frames_grad/pallas_call | solution.py:488
  (81 shorter events, 26.9 us)
Async XLA Ops:
  2.3 12.1 %collective-permute-start = (bf16[48,1024]{1,0:T(8,128)(2,1)S(1)}, bf16[48,1024]{1,0:T(8,128)(2,1)S(1)}, u32[]{:S(2)}, u32[]{:S(2)}) collective-permute-start(bf16[48,1024]{1,0:T(8,128)(2,1)S(1)} %pad_maximum_fusion), channel_id=1, source_target_pairs={{0,1},{1,2},{2,3},{4,5},{5,6},{6,7},{8,9},{9,10},{10,11},{12,13},{... | collective-permute-start | bytes 294920 | tf_op jit(solution)/shard_map/ppermute | solution.py:700
  4.7 9.8 %collective-permute-start.1 = (bf16[48,1024]{1,0:T(8,128)(2,1)S(1)}, bf16[48,1024]{1,0:T(8,128)(2,1)S(1)}, u32[]{:S(2)}, u32[]{:S(2)}) collective-permute-start(bf16[48,1024]{1,0:T(8,128)(2,1)S(1)} %pad_maximum_fusion.1), channel_id=1, source_target_pairs={{1,0},{2,1},{3,2},{5,4},{6,5},{7,6},{9,8},{10,9},{11,10},{13,12},{... | collective-permute-start | bytes 294920 | tf_op jit(solution)/shard_map/ppermute | solution.py:701
  27.2 24.9 %all-to-all-start = ((f32[32,3,1024]{2,1,0:T(4,128)}), f32[32,3,1024]{2,1,0:T(4,128)}, u32[]{:S(2)}, u32[]{:S(2)}) async-start(f32[32,3,1024]{2,1,0:T(4,128)} %get-tuple-element.53), calls=%async_computation | async-start | bytes 1048576 | tf_op jit(solution)/shard_map/all_to_all | solution.py:676
  62.7 1.0 copy-start
  63.7 8.6 %collective-permute-start.2 = (bf16[512,1024]{1,0:T(8,128)(2,1)}, bf16[512,1024]{1,0:T(8,128)(2,1)}, u32[]{:S(2)}, u32[]{:S(2)}) collective-permute-start(bf16[512,1024]{1,0:T(8,128)(2,1)} %get-tuple-element.60), channel_id=1, source_target_pairs={{0,1},{1,0},{2,3},{3,2},{4,5},{5,4},{6,7},{7,6},{8,9},{9,8},{10,11... | collective-permute-start | bytes 3145736 | tf_op jit(solution)/shard_map/ppermute | solution.py:715
  63.7 14.2 %collective-permute-start.3 = (bf16[512,768]{1,0:T(8,128)(2,1)}, bf16[512,768]{1,0:T(8,128)(2,1)}, u32[]{:S(2)}, u32[]{:S(2)}) collective-permute-start(bf16[512,768]{1,0:T(8,128)(2,1)} %get-tuple-element.62), channel_id=1, source_target_pairs={{0,1},{1,0},{2,3},{3,2},{4,5},{5,4},{6,7},{7,6},{8,9},{9,8},{10,11... | collective-permute-start | bytes 2359304 | tf_op jit(solution)/shard_map/ppermute | solution.py:709
  64.2 13.7 %all-to-all-start.1 = ((f32[32,2,1024]{2,1,0:T(2,128)}), f32[32,2,1024]{2,1,0:T(2,128)S(1)}, u32[]{:S(2)}, u32[]{:S(2)}) async-start(f32[32,2,1024]{2,1,0:T(2,128)} %get-tuple-element.57), calls=%async_computation.1 | async-start | bytes 524288 | tf_op jit(solution)/shard_map/all_to_all | solution.py:676
  77.9 9.5 %collective-permute-start.5 = (bf16[256,1024]{1,0:T(8,128)(2,1)}, bf16[256,1024]{1,0:T(8,128)(2,1)}, u32[]{:S(2)}, u32[]{:S(2)}) collective-permute-start(bf16[256,1024]{1,0:T(8,128)(2,1)} %copy-done.3), channel_id=1, source_target_pairs={{0,2},{1,5},{2,0},{3,7},{4,6},{5,1},{6,4},{7,3},{8,10},{9,13},{10,... | collective-permute-start | bytes 1572872 | tf_op jit(solution)/shard_map/ppermute | solution.py:651
  78.6 8.8 %copy-start.2 = (bf16[256,1024]{1,0:T(8,128)(2,1)S(1)}, bf16[256,1024]{1,0:T(8,128)(2,1)}, u32[]{:S(2)}) copy-start(bf16[256,1024]{1,0:T(8,128)(2,1)} %copy-done.1) | copy-start | bytes 1572868
  85.9 11.8 %collective-permute-start.4 = (bf16[2,768,512]{2,1,0:T(8,128)(2,1)}, bf16[2,768,512]{2,1,0:T(8,128)(2,1)}, u32[]{:S(2)}, u32[]{:S(2)}) collective-permute-start(bf16[2,768,512]{2,1,0:T(8,128)(2,1)} %get-tuple-element.92.own_ref.refs_0_), channel_id=1, source_target_pairs={{0,1},{1,0},{2,3},{3,2},{4,5},{5,4},{6,7},{7,6},{8,9},{9,8},{10,11... | collective-permute-start | bytes 4718600 | tf_op jit(solution)/shard_map/ppermute | solution.py:727
  96.8 5.8 %collective-permute-start.7 = (bf16[2,768,512]{2,1,0:T(8,128)(2,1)}, bf16[2,768,512]{2,1,0:T(8,128)(2,1)S(1)}, u32[]{:S(2)}, u32[]{:S(2)}) collective-permute-start(bf16[2,768,512]{2,1,0:T(8,128)(2,1)} %get-tuple-element.93.own_ref.refs_1_), channel_id=1, source_target_pairs={{0,1},{1,0},{2,3},{3,2},{4,5},{5,4},{6,7},{7,6},{8,9},{9,8},{10,11... | collective-permute-start | bytes 4718600 | tf_op jit(solution)/shard_map/ppermute | solution.py:727
  96.8 12.1 %collective-permute-start.6 = (bf16[128,1024]{1,0:T(8,128)(2,1)S(1)}, bf16[128,1024]{1,0:T(8,128)(2,1)S(1)}, u32[]{:S(2)}, u32[]{:S(2)}) collective-permute-start(bf16[128,1024]{1,0:T(8,128)(2,1)S(1)} %broadcast_select_fusion.1), channel_id=1, source_target_pairs={{0,4},{1,3},{2,6},{3,1},{4,0},{5,7},{6,2},{7,5},{8,12},{9,11},{10,... | collective-permute-start | bytes 786440 | tf_op jit(solution)/shard_map/ppermute | solution.py:651
  101.7 7.2 %copy-start.5 = (bf16[256,1024]{1,0:T(8,128)(2,1)S(1)}, bf16[256,1024]{1,0:T(8,128)(2,1)}, u32[]{:S(2)}) copy-start(bf16[256,1024]{1,0:T(8,128)(2,1)} %copy-done.4) | copy-start | bytes 1572868
  101.7 17.6 %collective-permute-start.8 = (bf16[256,1024]{1,0:T(8,128)(2,1)S(1)}, bf16[256,1024]{1,0:T(8,128)(2,1)S(1)}, u32[]{:S(2)}, u32[]{:S(2)}) collective-permute-start(bf16[256,1024]{1,0:T(8,128)(2,1)S(1)} %get-tuple-element.76), channel_id=1, source_target_pairs={{0,2},{1,5},{2,0},{3,7},{4,6},{5,1},{6,4},{7,3},{8,10},{9,13},{10,... | collective-permute-start | bytes 1572872 | tf_op jit(solution)/shard_map/ppermute | solution.py:651
  102.6 1.1 copy-start.8
  107.7 11.6 %collective-permute-start.9 = (bf16[256,1024]{1,0:T(8,128)(2,1)S(1)}, bf16[256,1024]{1,0:T(8,128)(2,1)S(1)}, u32[]{:S(2)}, u32[]{:S(2)}) collective-permute-start(bf16[256,1024]{1,0:T(8,128)(2,1)S(1)} %get-tuple-element.79), channel_id=1, source_target_pairs={{0,2},{1,5},{2,0},{3,7},{4,6},{5,1},{6,4},{7,3},{8,10},{9,13},{10,... | collective-permute-start | bytes 1572872 | tf_op jit(solution)/shard_map/ppermute | solution.py:651
  109.1 10.2 %collective-permute-start.10 = (bf16[64,1024]{1,0:T(8,128)(2,1)S(1)}, bf16[64,1024]{1,0:T(8,128)(2,1)S(1)}, u32[]{:S(2)}, u32[]{:S(2)}) collective-permute-start(bf16[64,1024]{1,0:T(8,128)(2,1)S(1)} %broadcast_select_fusion.3), channel_id=1, source_target_pairs={{0,8},{1,9},{2,10},{3,11},{4,12},{5,13},{6,14},{7,15},{8,0},{9,1},... | collective-permute-start | bytes 393224 | tf_op jit(solution)/shard_map/ppermute | solution.py:651
  119.7 1.6 %copy-start.7 = (f32[32,2,1024]{2,1,0:T(2,128)S(1)}, f32[32,2,1024]{2,1,0:T(2,128)}, u32[]{:S(2)}) copy-start(f32[32,2,1024]{2,1,0:T(2,128)} %copy-done.6) | copy-start | bytes 786436
  119.8 9.9 %collective-permute-start.11 = (bf16[128,2048]{1,0:T(8,128)(2,1)S(1)}, bf16[128,2048]{1,0:T(8,128)(2,1)S(1)}, u32[]{:S(2)}, u32[]{:S(2)}) collective-permute-start(bf16[128,2048]{1,0:T(8,128)(2,1)S(1)} %broadcast_select_fusion), channel_id=1, source_target_pairs={{0,4},{1,3},{2,6},{3,1},{4,0},{5,7},{6,2},{7,5},{8,12},{9,11},{10,... | collective-permute-start | bytes 1572872 | tf_op jit(solution)/shard_map/ppermute | solution.py:651
  121.4 15.7 %all-to-all-start.2 = ((f32[32,8,128]{2,1,0:T(8,128)}), f32[32,8,128]{2,1,0:T(8,128)S(1)}, u32[]{:S(2)}, u32[]{:S(2)}) async-start(f32[32,8,128]{2,1,0:T(8,128)} %bitcast.14), calls=%async_computation.2 | async-start | bytes 262144 | tf_op jit(solution)/shard_map/all_to_all | solution.py:676
  130.0 7.7 %collective-permute-start.12 = (bf16[64,2048]{1,0:T(8,128)(2,1)S(1)}, bf16[64,2048]{1,0:T(8,128)(2,1)S(1)}, u32[]{:S(2)}, u32[]{:S(2)}) collective-permute-start(bf16[64,2048]{1,0:T(8,128)(2,1)S(1)} %broadcast_select_fusion.2), channel_id=1, source_target_pairs={{0,8},{1,9},{2,10},{3,11},{4,12},{5,13},{6,14},{7,15},{8,0},{9,1},... | collective-permute-start | bytes 786440 | tf_op jit(solution)/shard_map/ppermute | solution.py:651
  131.8 5.3 %collective-permute-start.13 = (bf16[32,1024]{1,0:T(8,128)(2,1)S(1)}, bf16[32,1024]{1,0:T(8,128)(2,1)S(1)}, u32[]{:S(2)}, u32[]{:S(2)}) collective-permute-start(bf16[32,1024]{1,0:T(8,128)(2,1)S(1)} %broadcast_select_fusion.5), channel_id=1, source_target_pairs={{0,16},{1,17},{2,18},{3,19},{4,20},{5,21},{6,22},{7,23},{8,24},{9,... | collective-permute-start | bytes 196616 | tf_op jit(solution)/shard_map/ppermute | solution.py:651
  138.5 17.2 %all-to-all-start.3 = ((f32[32,8,128]{2,1,0:T(8,128)}), f32[32,8,128]{2,1,0:T(8,128)S(1)}, u32[]{:S(2)}, u32[]{:S(2)}) async-start(f32[32,8,128]{2,1,0:T(8,128)} %broadcast_in_dim.22), calls=%async_computation.3 | async-start | bytes 262144 | tf_op jit(solution)/shard_map/all_to_all | solution.py:676
  142.2 12.2 %collective-permute-start.14 = (bf16[32,2048]{1,0:T(8,128)(2,1)S(1)}, bf16[32,2048]{1,0:T(8,128)(2,1)S(1)}, u32[]{:S(2)}, u32[]{:S(2)}) collective-permute-start(bf16[32,2048]{1,0:T(8,128)(2,1)S(1)} %broadcast_select_fusion.4), channel_id=1, source_target_pairs={{0,16},{1,17},{2,18},{3,19},{4,20},{5,21},{6,22},{7,23},{8,24},{9,... | collective-permute-start | bytes 393224 | tf_op jit(solution)/shard_map/ppermute | solution.py:651
  (6 other events, 4.4 us)

commit v6 on v5

--- a/solution.py
+++ b/solution.py
@@ -72,6 +72,33 @@
     copies_ref[:, :, lanes_of(c)] = jnp.broadcast_to(lines[None], (copies_ref.shape[0],) + lines.shape)
 
 
+def edges_kernel(last_ref, last_cot_ref, first_ref, first_cot_ref, tail_ref, head_ref):
+    tail_ref[:WIDE] = last_ref[...]
+    tail_ref[WIDE:] = last_cot_ref[...]
+    head_ref[:WIDE] = first_ref[...]
+    head_ref[WIDE:] = first_cot_ref[...]
+
+
+def edges(feats, cot):
+    rows, depth = feats.shape
+    shape = jax.ShapeDtypeStruct((WIDE + NEAR, depth), BF16)
+    return pl.pallas_call(
+        edges_kernel,
+        grid=(1,),
+        in_specs=[
+            pl.BlockSpec((WIDE, depth), lambda j: (rows // WIDE - 1, 0)),
+            pl.BlockSpec((NEAR, depth), lambda j: (rows // NEAR - 1, 0)),
+            pl.BlockSpec((WIDE, depth), lambda j: (0, 0)),
+            pl.BlockSpec((NEAR, depth), lambda j: (0, 0)),
+        ],
+        out_specs=[pl.BlockSpec((WIDE + NEAR, depth), lambda j: (0, 0))] * 2,
+        out_shape=[shape, shape],
+        compiler_params=pltpu.CompilerParams(vmem_limit_bytes=VMEM_LIMIT),
+        cost_estimate=pl.CostEstimate(flops=0, bytes_accessed=8 * WIDE * depth, transcendentals=0),
+        name="edges",
+    )(*in_hbm(feats, cot, feats, cot))
+
+
 def gate_kernel(span_ref, feats_ref, lin_w_ref, gate_w_ref, glu_ref, first_ref, second_ref):
     rows = feats_ref.shape[0]
     step = 128 if rows % 128 == 0 else rows
@@ -124,8 +151,8 @@
     taps = taps_ref.shape[0]
     full = rows + 2 * NEAR
     halo = jnp.concatenate([before_ref[...], after_ref[...]], axis=0)
-    lin = dot_nn(halo, lin_w_ref[...])
-    sig = logistic(dot_nn(halo, gate_w_ref[...]))
+    pre = dot_nn(halo, jnp.concatenate([lin_w_ref[...], gate_w_ref[...]], axis=1))
+    lin, sig = pre[:, :BLOCK], logistic(pre[:, BLOCK:])
     low, high = span_ref[0], span_ref[1]
     live = jnp.concatenate([row_mask(-WIDE, WIDE, low, high), row_mask(rows, WIDE, low, high)], axis=0)
     for c in range(SUB):
@@ -695,8 +722,7 @@
     gain, bias = bn_gain[None], bn_bias[None]
 
     everyone = ("dp", "tm")
-    tail = jnp.concatenate([feats[rows - WIDE :], cot[rows - NEAR :]], axis=0)
-    head = jnp.concatenate([feats[:WIDE], cot[:NEAR]], axis=0)
+    tail, head = edges(feats, cot)
     before = lax.ppermute(tail, "tm", [(i, i + 1) for i in range(tm_count - 1)])
     after = lax.ppermute(head, "tm", [(i + 1, i) for i in range(tm_count - 1)])
 

time: 158 us -> 157 us (level)
  local copies, waits for them, and re-layouts: 10 us -> 8.32 us
    slice x2 -> x0, local copies, waits for them, and re-layouts: 1.66 us -> none  [local(): head = jnp.concatenate([feats[:WIDE], cot[:NEAR]], axis=0)]
where the time goes in v6:
time: 157 us; the launch traced here: 156 us
  Pallas kernels  81.2 us (52%)
  starting transfers between devices  34.2 us (22%)
  waiting for transfers between devices  21.4 us (14%)
  local copies, waits for them, and re-layouts  8.32 us (5%)
  matrix products  5.01 us (3%)
  other arithmetic  3.97 us (3%)
  between operations  1.62 us (1%)
    all_to_all x4, starting transfers between devices, from_all(): return lax.all_to_all(copies, ('dp', 'tm'), 0, 0, tiled=True)  19.6 us
    pallas_call x2, Pallas kernels, norm_grad(): pl.pallas_call(grad_kernel, grid=(blocks,), in_specs=[pl.BlockSpec(memory...  14.6 us
    ppermute x9, waiting for transfers between devices, swap(): return lax.ppermute(send, ('dp', 'tm'), self.plan.perm(self.step))  12.3 us
    pallas_call x1, Pallas kernels, convolved(): pl.pallas_call(conv_kernel, grid=(blocks,), in_specs=[pl.BlockSpec(memory...  12.1 us
    ppermute x9, starting transfers between devices, swap(): return lax.ppermute(send, ('dp', 'tm'), self.plan.perm(self.step))  10.5 us
    pallas_call x1, Pallas kernels, tap_grad(): pl.pallas_call(functools.partial(tap_grad_kernel, taps), grid=(steps,), i...  9.45 us
    all_to_all x4, waiting for transfers between devices, from_all(): return lax.all_to_all(copies, ('dp', 'tm'), 0, 0, tiled=True)  9.05 us
    pallas_call x2, Pallas kernels, pair_term(): pl.pallas_call(pair_kernel, grid=(halves,), in_specs=[pl.BlockSpec(memory...  7.84 us
  transfers between devices with their start and end apart: 19, of which 7 were waited for; matrix products, arithmetic and copies ran while one was open for 6% of the time, Pallas kernels for 37%

profile of v6, /device:TPU:0, one launch (start us, length us, event | category | flops | bytes accessed | tf_op | source)
XLA Modules:
  0.0 155.7 jit_solution(11075705720600489774)
XLA Ops:
  1.5 2.4 %collective-permute-start = (bf16[48,1024]{1,0:T(8,128)(2,1)S(1)}, bf16[48,1024]{1,0:T(8,128)(2,1)S(1)}, u32[]{:S(2)}, u32[]{:S(2)}) collective-permute-start(bf16[48,1024]{1,0:T(8,128)(2,1)S(1)} %get-tuple-element.54), channel_id=1, source_target_pairs={{0,1},{1,2},{2,3},{4,5},{5,6},{6,7},{8,9},{9,10},{10,11},{12,13},{... | collective-permute-start | bytes 294920 | tf_op jit(solution)/shard_map/ppermute | solution.py:726
  5.9 7.7 %gated.1 = (bf16[8,768,128]{2,1,0:T(8,128)(2,1)}, bf16[768,1024]{1,0:T(8,128)(2,1)}, bf16[768,1024]{1,0:T(8,128)(2,1)}) custom-call(s32[2]{0:T(128)S(1)} %pad_add_fusion.span_ref, bf16[768,1024]{1,0:T(8,128)(2,1)} %bitcast.27, bf16[1024,2048]{1,0:T(8,128)(2,1)} %refs_2_.1, bf16[1024,2048]{1,0:T(8,128)(2,1)} %refs_2_.1), custom_call_target="tpu_custom_call" | custom-call | flops 3221225472 | bytes 11010048 | tf_op jit(solution)/shard_map/gated/pallas_call | solution.py:122
  14.3 12.1 %convolved.1 = (f32[8,800,128]{2,1,0:T(8,128)S(1)}, bf16[8,64,128]{2,1,0:T(8,128)(2,1)}, f32[32,3,1024]{2,1,0:T(4,128)}) custom-call(s32[2]{0:T(128)S(1)} %pad_add_fusion.span_ref, bf16[48,1024]{1,0:T(8,128)(2,1)} %copy-done.9, bf16[48,1024]{1,0:T(8,128)(2,1)} %copy-done.10, bf16[1024,2048]{1,0:T(8,128)(2,1)} %refs_2_.1, bf16[1024,2048]{1,0:T(8,128)(2,1)} %refs_2_.1, ...), custom_call_target="tpu_custom_call" | custom-call | flops 3221225472 | bytes 11010048 | tf_op jit(solution)/shard_map/convolved/pallas_call | solution.py:197
  26.4 9.3 %all-to-all-start = ((f32[32,3,1024]{2,1,0:T(4,128)}), f32[32,3,1024]{2,1,0:T(4,128)}, u32[]{:S(2)}, u32[]{:S(2)}) async-start(f32[32,3,1024]{2,1,0:T(4,128)} %get-tuple-element.57), calls=%async_computation | async-start | bytes 1048576 | tf_op jit(solution)/shard_map/all_to_all | solution.py:703
  35.8 3.1 %flipped.1 = (bf16[512,768]{1,0:T(8,128)(2,1)}, bf16[512,768]{1,0:T(8,128)(2,1)}) custom-call(s32[1]{0:T(128)} %bitcast.5.core_ref, bf16[768,1024]{1,0:T(8,128)(2,1)} %bitcast.28), custom_call_target="tpu_custom_call" | custom-call | flops 3145728 | bytes 3145728 | tf_op jit(solution)/shard_map/flipped/pallas_call | solution.py:545
  38.9 5.6 %back_projected.1.back_ref = bf16[8,800,128]{2,1,0:T(8,128)(2,1)} custom-call(bf16[48,1024]{1,0:T(8,128)(2,1)} %copy-done.9, bf16[768,1024]{1,0:T(8,128)(2,1)} %bitcast.31, bf16[48,1024]{1,0:T(8,128)(2,1)} %copy-done.10, bf16[1024,1024]{1,0:T(8,128)(2,1)} %w_ref.1), custom_call_target="tpu_custom_call" | custom-call | flops 1610612736 | bytes 6291456 | tf_op jit(solution)/shard_map/back_projected/pallas_call | solution.py:246
  44.5 6.8 %all-to-all-done.sums_ref = f32[32,3,1024]{2,1,0:T(4,128)} async-done(((f32[32,3,1024]{2,1,0:T(4,128)}), f32[32,3,1024]{2,1,0:T(4,128)}, u32[]{:S(2)}, u32[]{:S(2)}) %all-to-all-start) | async-done | bytes 393248 | tf_op jit(solution)/shard_map/all_to_all | solution.py:703
  51.3 6.0 %swish.1 = (bf16[768,1024]{1,0:T(8,128)(2,1)}, bf16[8,800,128]{2,1,0:T(8,128)(2,1)}, f32[32,2,1024]{2,1,0:T(2,128)}) custom-call(s32[2]{0:T(128)S(1)} %pad_add_fusion.span_ref, f32[32,3,1024]{2,1,0:T(4,128)} %all-to-all-done.sums_ref, f32[1,1024]{1,0:T(1,128)} %bitcast.37, f32[1,1024]{1,0:T(1,128)} %bitcast.42, ...), custom_call_target="tpu_custom_call" | custom-call | flops 23592960 | bytes 11010048 | tf_op jit(solution)/shard_map/swish/pallas_call | solution.py:319
  57.3 4.6 %weight_term.1 = (bf16[512,1024]{1,0:T(8,128)(2,1)}, bf16[512,1024]{1,0:T(8,128)(2,1)S(1)}) custom-call(s32[1]{0:T(128)} %bitcast.5.core_ref, bf16[768,1024]{1,0:T(8,128)(2,1)} %get-tuple-element.62.left_ref, bf16[1,768,1024]{2,1,0:T(8,128)(2,1)} %right_ref.1), custom_call_target="tpu_custom_call" | custom-call | tf_op jit(solution)/shard_map/weight_term/pallas_call | solution.py:607
  63.4 3.1 %all-to-all-start.1 = ((f32[32,2,1024]{2,1,0:T(2,128)}), f32[32,2,1024]{2,1,0:T(2,128)S(1)}, u32[]{:S(2)}, u32[]{:S(2)}) async-start(f32[32,2,1024]{2,1,0:T(2,128)} %get-tuple-element.61), calls=%async_computation.1 | async-start | bytes 524288 | tf_op jit(solution)/shard_map/all_to_all | solution.py:703
  66.5 5.0 %convolution_convert_fusion = bf16[768,1024]{1,0:T(8,128)(2,1)} fusion(bf16[768,1024]{1,0:T(8,128)(2,1)} %get-tuple-element.62.left_ref, bf16[1024,1024]{1,0:T(8,128)(2,1)} %w_ref.1), kind=kOutput, calls=%fused_computation.1 | convolution fusion | flops 1611399168 | bytes 5242880 | tf_op jit(solution)/shard_map/dot_general | solution.py:30
  71.5 1.7 %combine.1 = (bf16[256,1024]{1,0:T(8,128)(2,1)S(1)}, bf16[256,1024]{1,0:T(8,128)(2,1)S(1)}) custom-call(s32[1]{0:T(128)} %bitcast.8.half_ref, bf16[512,1024]{1,0:T(8,128)(2,1)} %copy-done, bf16[512,1024]{1,0:T(8,128)(2,1)} %collective-permute-done.2.got_other.got_mine, bf16[512,1024]{1,0:T(8,128)(2,1)} %copy-done, ...), custom_call_target="tpu_custom_call" | custom-call | tf_op jit(solution)/shard_map/combine/pallas_call | solution.py:657
  74.9 2.2 %all-to-all-done.1.terms_ref = f32[32,2,1024]{2,1,0:T(2,128)S(1)} async-done(((f32[32,2,1024]{2,1,0:T(2,128)}), f32[32,2,1024]{2,1,0:T(2,128)S(1)}, u32[]{:S(2)}, u32[]{:S(2)}) %all-to-all-start.1) | async-done | bytes 262176 | tf_op jit(solution)/shard_map/all_to_all | solution.py:703
  77.8 7.3 %norm_grad.2 = (bf16[2,768,512]{2,1,0:T(8,128)(2,1)}, bf16[4,768,128]{2,1,0:T(8,128)(2,1)}) custom-call(s32[2]{0:T(128)S(1)} %pad_add_fusion.span_ref, f32[32,3,1024]{2,1,0:T(4,128)} %all-to-all-done.sums_ref, f32[32,2,1024]{2,1,0:T(2,128)} %copy-done.6, f32[1,1024]{1,0:T(1,128)} %bitcast.38, f32[31,1024]{1,0:T(8,128)} %taps_ref.5, ...), custom_call_target="tpu_custom_call" | custom-call | flops 27525120 | bytes 6291456 | tf_op jit(solution)/shard_map/norm_grad/pallas_call | solution.py:397
  88.7 7.3 %norm_grad.3 = (bf16[2,768,512]{2,1,0:T(8,128)(2,1)}, bf16[4,768,128]{2,1,0:T(8,128)(2,1)}) custom-call(s32[2]{0:T(128)S(1)} %pad_add_fusion.span_ref, f32[32,3,1024]{2,1,0:T(4,128)} %all-to-all-done.sums_ref, f32[32,2,1024]{2,1,0:T(2,128)} %copy-done.6, f32[1,1024]{1,0:T(1,128)} %bitcast.39, f32[31,1024]{1,0:T(8,128)} %taps_ref.5, ...), custom_call_target="tpu_custom_call" | custom-call | flops 27525120 | bytes 6291456 | tf_op jit(solution)/shard_map/norm_grad/pallas_call | solution.py:397
  97.0 3.9 %pair_term.2 = (bf16[256,1024]{1,0:T(8,128)(2,1)S(1)}, bf16[256,1024]{1,0:T(8,128)(2,1)S(1)}) custom-call(s32[1]{0:T(128)} %bitcast.8.half_ref, bf16[512,768]{1,0:T(8,128)(2,1)} %get-tuple-element.68.left_own, bf16[512,768]{1,0:T(8,128)(2,1)} %collective-permute-done.3.left_got, bf16[2,768,512]{2,1,0:T(8,128)(2,1)} %get-tuple-element.96.own_ref.refs_0_, ...), custom_call_target="tpu_custom_call" | custom-call | flops 1610612736 | bytes 6291456 | tf_op jit(solution)/shard_map/pair_term/pallas_call | solution.py:572
  103.0 3.9 %pair_term.3 = (bf16[256,1024]{1,0:T(8,128)(2,1)S(1)}, bf16[256,1024]{1,0:T(8,128)(2,1)S(1)}) custom-call(s32[1]{0:T(128)} %bitcast.8.half_ref, bf16[512,768]{1,0:T(8,128)(2,1)} %get-tuple-element.68.left_own, bf16[512,768]{1,0:T(8,128)(2,1)} %collective-permute-done.3.left_got, bf16[2,768,512]{2,1,0:T(8,128)(2,1)} %get-tuple-element.97.own_ref.refs_1_, ...), custom_call_target="tpu_custom_call" | custom-call | flops 1610612736 | bytes 6291456 | tf_op jit(solution)/shard_map/pair_term/pallas_call | solution.py:572
  109.0 9.4 %tap_grad.1 = f32[8,32,128]{2,1,0:T(8,128)} custom-call(bf16[8,64,128]{2,1,0:T(8,128)(2,1)} %get-tuple-element.76.edge_ref, bf16[8,768,128]{2,1,0:T(8,128)(2,1)} %get-tuple-element.84.glu_ref, bf16[4,768,128]{2,1,0:T(8,128)(2,1)} %get-tuple-element.85.refs_0_, bf16[4,768,128]{2,1,0:T(8,128)(2,1)} %get-tuple-element.86.refs_1_), custom_call_target="tpu_custom_call" | custom-call | flops 48758784 | bytes 3145728 | tf_op jit(solution)/shard_map/tap_grad/pallas_call | solution.py:477
  120.6 3.5 %all-to-all-start.2 = ((f32[32,8,128]{2,1,0:T(8,128)}), f32[32,8,128]{2,1,0:T(8,128)S(1)}, u32[]{:S(2)}, u32[]{:S(2)}) async-start(f32[32,8,128]{2,1,0:T(8,128)} %bitcast.10), calls=%async_computation.2 | async-start | bytes 262144 | tf_op jit(solution)/shard_map/all_to_all | solution.py:703
  124.2 4.8 %collective-permute-done.11 = bf16[128,2048]{1,0:T(8,128)(2,1)S(1)} collective-permute-done((bf16[128,2048]{1,0:T(8,128)(2,1)S(1)}, bf16[128,2048]{1,0:T(8,128)(2,1)S(1)}, u32[]{:S(2)}, u32[]{:S(2)}) %collective-permute-start.11) | collective-permute-done | bytes 524320 | tf_op jit(solution)/shard_map/ppermute | solution.py:678
  132.1 4.2 %collective-permute-done.13 = bf16[32,1024]{1,0:T(8,128)(2,1)S(1)} collective-permute-done((bf16[32,1024]{1,0:T(8,128)(2,1)S(1)}, bf16[32,1024]{1,0:T(8,128)(2,1)S(1)}, u32[]{:S(2)}, u32[]{:S(2)}) %collective-permute-start.13) | collective-permute-done | bytes 65568 | tf_op jit(solution)/shard_map/ppermute | solution.py:678
  137.7 3.6 %all-to-all-start.3 = ((f32[32,8,128]{2,1,0:T(8,128)}), f32[32,8,128]{2,1,0:T(8,128)S(1)}, u32[]{:S(2)}, u32[]{:S(2)}) async-start(f32[32,8,128]{2,1,0:T(8,128)} %broadcast_in_dim.22), calls=%async_computation.3 | async-start | bytes 262144 | tf_op jit(solution)/shard_map/all_to_all | solution.py:703
  141.4 2.7 %collective-permute-start.14 = (bf16[32,2048]{1,0:T(8,128)(2,1)S(1)}, bf16[32,2048]{1,0:T(8,128)(2,1)S(1)}, u32[]{:S(2)}, u32[]{:S(2)}) collective-permute-start(bf16[32,2048]{1,0:T(8,128)(2,1)S(1)} %broadcast_select_fusion.4), channel_id=1, source_target_pairs={{0,16},{1,17},{2,18},{3,19},{4,20},{5,21},{6,22},{7,23},{8,24},{9,... | collective-permute-start | bytes 393224 | tf_op jit(solution)/shard_map/ppermute | solution.py:678
  144.2 7.5 %frames_grad.1 = bf16[768,1024]{1,0:T(8,128)(2,1)} custom-call(bf16[2,768,512]{2,1,0:T(8,128)(2,1)} %get-tuple-element.96.own_ref.refs_0_, bf16[2,768,512]{2,1,0:T(8,128)(2,1)} %get-tuple-element.97.own_ref.refs_1_, bf16[1024,2048]{1,0:T(8,128)(2,1)} %refs_2_.1), custom_call_target="tpu_custom_call" | custom-call | flops 3221225472 | bytes 7864320 | tf_op jit(solution)/shard_map/frames_grad/pallas_call | solution.py:515
  (78 shorter events, 26.1 us)
Async XLA Ops:
  1.5 12.1 %collective-permute-start = (bf16[48,1024]{1,0:T(8,128)(2,1)S(1)}, bf16[48,1024]{1,0:T(8,128)(2,1)S(1)}, u32[]{:S(2)}, u32[]{:S(2)}) collective-permute-start(bf16[48,1024]{1,0:T(8,128)(2,1)S(1)} %get-tuple-element.54), channel_id=1, source_target_pairs={{0,1},{1,2},{2,3},{4,5},{5,6},{6,7},{8,9},{9,10},{10,11},{12,13},{... | collective-permute-start | bytes 294920 | tf_op jit(solution)/shard_map/ppermute | solution.py:726
  3.9 9.8 %collective-permute-start.1 = (bf16[48,1024]{1,0:T(8,128)(2,1)S(1)}, bf16[48,1024]{1,0:T(8,128)(2,1)S(1)}, u32[]{:S(2)}, u32[]{:S(2)}) collective-permute-start(bf16[48,1024]{1,0:T(8,128)(2,1)S(1)} %get-tuple-element.55), channel_id=1, source_target_pairs={{1,0},{2,1},{3,2},{5,4},{6,5},{7,6},{9,8},{10,9},{11,10},{13,12},{... | collective-permute-start | bytes 294920 | tf_op jit(solution)/shard_map/ppermute | solution.py:727
  26.4 24.9 %all-to-all-start = ((f32[32,3,1024]{2,1,0:T(4,128)}), f32[32,3,1024]{2,1,0:T(4,128)}, u32[]{:S(2)}, u32[]{:S(2)}) async-start(f32[32,3,1024]{2,1,0:T(4,128)} %get-tuple-element.57), calls=%async_computation | async-start | bytes 1048576 | tf_op jit(solution)/shard_map/all_to_all | solution.py:703
  62.0 1.0 copy-start
  62.9 8.6 %collective-permute-start.2 = (bf16[512,1024]{1,0:T(8,128)(2,1)}, bf16[512,1024]{1,0:T(8,128)(2,1)}, u32[]{:S(2)}, u32[]{:S(2)}) collective-permute-start(bf16[512,1024]{1,0:T(8,128)(2,1)} %get-tuple-element.64), channel_id=1, source_target_pairs={{0,1},{1,0},{2,3},{3,2},{4,5},{5,4},{6,7},{7,6},{8,9},{9,8},{10,11... | collective-permute-start | bytes 3145736 | tf_op jit(solution)/shard_map/ppermute | solution.py:741
  62.9 14.2 %collective-permute-start.3 = (bf16[512,768]{1,0:T(8,128)(2,1)}, bf16[512,768]{1,0:T(8,128)(2,1)}, u32[]{:S(2)}, u32[]{:S(2)}) collective-permute-start(bf16[512,768]{1,0:T(8,128)(2,1)} %get-tuple-element.66), channel_id=1, source_target_pairs={{0,1},{1,0},{2,3},{3,2},{4,5},{5,4},{6,7},{7,6},{8,9},{9,8},{10,11... | collective-permute-start | bytes 2359304 | tf_op jit(solution)/shard_map/ppermute | solution.py:735
  63.4 13.7 %all-to-all-start.1 = ((f32[32,2,1024]{2,1,0:T(2,128)}), f32[32,2,1024]{2,1,0:T(2,128)S(1)}, u32[]{:S(2)}, u32[]{:S(2)}) async-start(f32[32,2,1024]{2,1,0:T(2,128)} %get-tuple-element.61), calls=%async_computation.1 | async-start | bytes 524288 | tf_op jit(solution)/shard_map/all_to_all | solution.py:703
  77.1 9.5 %collective-permute-start.5 = (bf16[256,1024]{1,0:T(8,128)(2,1)}, bf16[256,1024]{1,0:T(8,128)(2,1)}, u32[]{:S(2)}, u32[]{:S(2)}) collective-permute-start(bf16[256,1024]{1,0:T(8,128)(2,1)} %copy-done.3), channel_id=1, source_target_pairs={{0,2},{1,5},{2,0},{3,7},{4,6},{5,1},{6,4},{7,3},{8,10},{9,13},{10,... | collective-permute-start | bytes 1572872 | tf_op jit(solution)/shard_map/ppermute | solution.py:678
  77.8 8.8 %copy-start.2 = (bf16[256,1024]{1,0:T(8,128)(2,1)S(1)}, bf16[256,1024]{1,0:T(8,128)(2,1)}, u32[]{:S(2)}) copy-start(bf16[256,1024]{1,0:T(8,128)(2,1)} %copy-done.1) | copy-start | bytes 1572868
  85.2 11.8 %collective-permute-start.4 = (bf16[2,768,512]{2,1,0:T(8,128)(2,1)}, bf16[2,768,512]{2,1,0:T(8,128)(2,1)}, u32[]{:S(2)}, u32[]{:S(2)}) collective-permute-start(bf16[2,768,512]{2,1,0:T(8,128)(2,1)} %get-tuple-element.96.own_ref.refs_0_), channel_id=1, source_target_pairs={{0,1},{1,0},{2,3},{3,2},{4,5},{5,4},{6,7},{7,6},{8,9},{9,8},{10,11... | collective-permute-start | bytes 4718600 | tf_op jit(solution)/shard_map/ppermute | solution.py:753
  96.0 5.8 %collective-permute-start.7 = (bf16[2,768,512]{2,1,0:T(8,128)(2,1)}, bf16[2,768,512]{2,1,0:T(8,128)(2,1)S(1)}, u32[]{:S(2)}, u32[]{:S(2)}) collective-permute-start(bf16[2,768,512]{2,1,0:T(8,128)(2,1)} %get-tuple-element.97.own_ref.refs_1_), channel_id=1, source_target_pairs={{0,1},{1,0},{2,3},{3,2},{4,5},{5,4},{6,7},{7,6},{8,9},{9,8},{10,11... | collective-permute-start | bytes 4718600 | tf_op jit(solution)/shard_map/ppermute | solution.py:753
  96.0 12.1 %collective-permute-start.6 = (bf16[128,1024]{1,0:T(8,128)(2,1)S(1)}, bf16[128,1024]{1,0:T(8,128)(2,1)S(1)}, u32[]{:S(2)}, u32[]{:S(2)}) collective-permute-start(bf16[128,1024]{1,0:T(8,128)(2,1)S(1)} %broadcast_select_fusion.1), channel_id=1, source_target_pairs={{0,4},{1,3},{2,6},{3,1},{4,0},{5,7},{6,2},{7,5},{8,12},{9,11},{10,... | collective-permute-start | bytes 786440 | tf_op jit(solution)/shard_map/ppermute | solution.py:678
  100.9 7.2 %copy-start.5 = (bf16[256,1024]{1,0:T(8,128)(2,1)S(1)}, bf16[256,1024]{1,0:T(8,128)(2,1)}, u32[]{:S(2)}) copy-start(bf16[256,1024]{1,0:T(8,128)(2,1)} %copy-done.4) | copy-start | bytes 1572868
  100.9 17.6 %collective-permute-start.8 = (bf16[256,1024]{1,0:T(8,128)(2,1)S(1)}, bf16[256,1024]{1,0:T(8,128)(2,1)S(1)}, u32[]{:S(2)}, u32[]{:S(2)}) collective-permute-start(bf16[256,1024]{1,0:T(8,128)(2,1)S(1)} %get-tuple-element.80), channel_id=1, source_target_pairs={{0,2},{1,5},{2,0},{3,7},{4,6},{5,1},{6,4},{7,3},{8,10},{9,13},{10,... | collective-permute-start | bytes 1572872 | tf_op jit(solution)/shard_map/ppermute | solution.py:678
  101.8 1.1 copy-start.8
  106.9 11.6 %collective-permute-start.9 = (bf16[256,1024]{1,0:T(8,128)(2,1)S(1)}, bf16[256,1024]{1,0:T(8,128)(2,1)S(1)}, u32[]{:S(2)}, u32[]{:S(2)}) collective-permute-start(bf16[256,1024]{1,0:T(8,128)(2,1)S(1)} %get-tuple-element.83), channel_id=1, source_target_pairs={{0,2},{1,5},{2,0},{3,7},{4,6},{5,1},{6,4},{7,3},{8,10},{9,13},{10,... | collective-permute-start | bytes 1572872 | tf_op jit(solution)/shard_map/ppermute | solution.py:678
  108.3 10.2 %collective-permute-start.10 = (bf16[64,1024]{1,0:T(8,128)(2,1)S(1)}, bf16[64,1024]{1,0:T(8,128)(2,1)S(1)}, u32[]{:S(2)}, u32[]{:S(2)}) collective-permute-start(bf16[64,1024]{1,0:T(8,128)(2,1)S(1)} %broadcast_select_fusion.3), channel_id=1, source_target_pairs={{0,8},{1,9},{2,10},{3,11},{4,12},{5,13},{6,14},{7,15},{8,0},{9,1},... | collective-permute-start | bytes 393224 | tf_op jit(solution)/shard_map/ppermute | solution.py:678
  118.9 1.6 %copy-start.7 = (f32[32,2,1024]{2,1,0:T(2,128)S(1)}, f32[32,2,1024]{2,1,0:T(2,128)}, u32[]{:S(2)}) copy-start(f32[32,2,1024]{2,1,0:T(2,128)} %copy-done.6) | copy-start | bytes 786436
  119.1 9.9 %collective-permute-start.11 = (bf16[128,2048]{1,0:T(8,128)(2,1)S(1)}, bf16[128,2048]{1,0:T(8,128)(2,1)S(1)}, u32[]{:S(2)}, u32[]{:S(2)}) collective-permute-start(bf16[128,2048]{1,0:T(8,128)(2,1)S(1)} %broadcast_select_fusion), channel_id=1, source_target_pairs={{0,4},{1,3},{2,6},{3,1},{4,0},{5,7},{6,2},{7,5},{8,12},{9,11},{10,... | collective-permute-start | bytes 1572872 | tf_op jit(solution)/shard_map/ppermute | solution.py:678
  120.6 15.7 %all-to-all-start.2 = ((f32[32,8,128]{2,1,0:T(8,128)}), f32[32,8,128]{2,1,0:T(8,128)S(1)}, u32[]{:S(2)}, u32[]{:S(2)}) async-start(f32[32,8,128]{2,1,0:T(8,128)} %bitcast.10), calls=%async_computation.2 | async-start | bytes 262144 | tf_op jit(solution)/shard_map/all_to_all | solution.py:703
  129.3 7.7 %collective-permute-start.12 = (bf16[64,2048]{1,0:T(8,128)(2,1)S(1)}, bf16[64,2048]{1,0:T(8,128)(2,1)S(1)}, u32[]{:S(2)}, u32[]{:S(2)}) collective-permute-start(bf16[64,2048]{1,0:T(8,128)(2,1)S(1)} %broadcast_select_fusion.2), channel_id=1, source_target_pairs={{0,8},{1,9},{2,10},{3,11},{4,12},{5,13},{6,14},{7,15},{8,0},{9,1},... | collective-permute-start | bytes 786440 | tf_op jit(solution)/shard_map/ppermute | solution.py:678
  131.0 5.3 %collective-permute-start.13 = (bf16[32,1024]{1,0:T(8,128)(2,1)S(1)}, bf16[32,1024]{1,0:T(8,128)(2,1)S(1)}, u32[]{:S(2)}, u32[]{:S(2)}) collective-permute-start(bf16[32,1024]{1,0:T(8,128)(2,1)S(1)} %broadcast_select_fusion.5), channel_id=1, source_target_pairs={{0,16},{1,17},{2,18},{3,19},{4,20},{5,21},{6,22},{7,23},{8,24},{9,... | collective-permute-start | bytes 196616 | tf_op jit(solution)/shard_map/ppermute | solution.py:678
  137.7 17.2 %all-to-all-start.3 = ((f32[32,8,128]{2,1,0:T(8,128)}), f32[32,8,128]{2,1,0:T(8,128)S(1)}, u32[]{:S(2)}, u32[]{:S(2)}) async-start(f32[32,8,128]{2,1,0:T(8,128)} %broadcast_in_dim.22), calls=%async_computation.3 | async-start | bytes 262144 | tf_op jit(solution)/shard_map/all_to_all | solution.py:703
  141.4 12.2 %collective-permute-start.14 = (bf16[32,2048]{1,0:T(8,128)(2,1)S(1)}, bf16[32,2048]{1,0:T(8,128)(2,1)S(1)}, u32[]{:S(2)}, u32[]{:S(2)}) collective-permute-start(bf16[32,2048]{1,0:T(8,128)(2,1)S(1)} %broadcast_select_fusion.4), channel_id=1, source_target_pairs={{0,16},{1,17},{2,18},{3,19},{4,20},{5,21},{6,22},{7,23},{8,24},{9,... | collective-permute-start | bytes 393224 | tf_op jit(solution)/shard_map/ppermute | solution.py:678
  (6 other events, 4.4 us)

commit v7 on v6

--- a/solution.py
+++ b/solution.py
@@ -274,7 +274,7 @@
 def swish_kernel(span_ref, sums_ref, gain_ref, bias_ref, conv_ref, back_ref, swished_ref, dshift_ref, terms_ref):
     rows = swished_ref.shape[0]
     low, high = span_ref[0], span_ref[1]
-    count = 384 if rows % 384 == 0 else NEAR
+    count = 768 if rows % 768 == 0 else NEAR
     for c in range(SUB):
         mean, inv_std, _ = moments(sums_ref, c)
         gain, bias = gain_ref[:, lanes_of(c)], bias_ref[:, lanes_of(c)]
@@ -352,7 +352,7 @@
     taps = taps_ref.shape[0]
     full = rows + 2 * NEAR
     low, high = span_ref[0], span_ref[1]
-    span = 160 if full % 160 == 0 else NEAR
+    span = 400 if full % 400 == 0 else NEAR
     count = 128 if rows % 128 == 0 else NEAR
     shift = NEAR - (taps - 1) // 2
     for c in range(SUB):

time: 157 us -> 156 us (level)
  no operation moved by 1% of the time
where the time goes in v7:
time: 156 us; the launch traced here: 155 us
  Pallas kernels  80.9 us (52%)
  starting transfers between devices  34 us (22%)
  waiting for transfers between devices  21.7 us (14%)
  local copies, waits for them, and re-layouts  8.32 us (5%)
  matrix products  5.01 us (3%)
  other arithmetic  3.97 us (3%)
  between operations  1.62 us (1%)
    all_to_all x4, starting transfers between devices, from_all(): return lax.all_to_all(copies, ('dp', 'tm'), 0, 0, tiled=True)  19.4 us
    pallas_call x2, Pallas kernels, norm_grad(): pl.pallas_call(grad_kernel, grid=(blocks,), in_specs=[pl.BlockSpec(memory...  14.5 us
    ppermute x9, waiting for transfers between devices, swap(): return lax.ppermute(send, ('dp', 'tm'), self.plan.perm(self.step))  12.6 us
    pallas_call x1, Pallas kernels, convolved(): pl.pallas_call(conv_kernel, grid=(blocks,), in_specs=[pl.BlockSpec(memory...  12.1 us
    ppermute x9, starting transfers between devices, swap(): return lax.ppermute(send, ('dp', 'tm'), self.plan.perm(self.step))  10.5 us
    pallas_call x1, Pallas kernels, tap_grad(): pl.pallas_call(functools.partial(tap_grad_kernel, taps), grid=(steps,), i...  9.45 us
    all_to_all x4, waiting for transfers between devices, from_all(): return lax.all_to_all(copies, ('dp', 'tm'), 0, 0, tiled=True)  9.05 us
    pallas_call x2, Pallas kernels, pair_term(): pl.pallas_call(pair_kernel, grid=(halves,), in_specs=[pl.BlockSpec(memory...  7.84 us
  transfers between devices with their start and end apart: 19, of which 7 were waited for; matrix products, arithmetic and copies ran while one was open for 6% of the time, Pallas kernels for 37%

profile of v7, /device:TPU:0, one launch (start us, length us, event | category | flops | bytes accessed | tf_op | source)
XLA Modules:
  0.0 155.5 jit_solution(16464896790543756747)
XLA Ops:
  1.5 2.4 %collective-permute-start = (bf16[48,1024]{1,0:T(8,128)(2,1)S(1)}, bf16[48,1024]{1,0:T(8,128)(2,1)S(1)}, u32[]{:S(2)}, u32[]{:S(2)}) collective-permute-start(bf16[48,1024]{1,0:T(8,128)(2,1)S(1)} %get-tuple-element.54), channel_id=1, source_target_pairs={{0,1},{1,2},{2,3},{4,5},{5,6},{6,7},{8,9},{9,10},{10,11},{12,13},{... | collective-permute-start | bytes 294920 | tf_op jit(solution)/shard_map/ppermute | solution.py:726
  5.9 7.7 %gated.1 = (bf16[8,768,128]{2,1,0:T(8,128)(2,1)}, bf16[768,1024]{1,0:T(8,128)(2,1)}, bf16[768,1024]{1,0:T(8,128)(2,1)}) custom-call(s32[2]{0:T(128)S(1)} %pad_add_fusion.span_ref, bf16[768,1024]{1,0:T(8,128)(2,1)} %bitcast.27, bf16[1024,2048]{1,0:T(8,128)(2,1)} %refs_2_.1, bf16[1024,2048]{1,0:T(8,128)(2,1)} %refs_2_.1), custom_call_target="tpu_custom_call" | custom-call | flops 3221225472 | bytes 11010048 | tf_op jit(solution)/shard_map/gated/pallas_call | solution.py:122
  14.3 12.1 %convolved.1 = (f32[8,800,128]{2,1,0:T(8,128)S(1)}, bf16[8,64,128]{2,1,0:T(8,128)(2,1)}, f32[32,3,1024]{2,1,0:T(4,128)}) custom-call(s32[2]{0:T(128)S(1)} %pad_add_fusion.span_ref, bf16[48,1024]{1,0:T(8,128)(2,1)} %copy-done.9, bf16[48,1024]{1,0:T(8,128)(2,1)} %copy-done.10, bf16[1024,2048]{1,0:T(8,128)(2,1)} %refs_2_.1, bf16[1024,2048]{1,0:T(8,128)(2,1)} %refs_2_.1, ...), custom_call_target="tpu_custom_call" | custom-call | flops 3221225472 | bytes 11010048 | tf_op jit(solution)/shard_map/convolved/pallas_call | solution.py:197
  26.4 9.3 %all-to-all-start = ((f32[32,3,1024]{2,1,0:T(4,128)}), f32[32,3,1024]{2,1,0:T(4,128)}, u32[]{:S(2)}, u32[]{:S(2)}) async-start(f32[32,3,1024]{2,1,0:T(4,128)} %get-tuple-element.57), calls=%async_computation | async-start | bytes 1048576 | tf_op jit(solution)/shard_map/all_to_all | solution.py:703
  35.8 3.1 %flipped.1 = (bf16[512,768]{1,0:T(8,128)(2,1)}, bf16[512,768]{1,0:T(8,128)(2,1)}) custom-call(s32[1]{0:T(128)} %bitcast.5.core_ref, bf16[768,1024]{1,0:T(8,128)(2,1)} %bitcast.28), custom_call_target="tpu_custom_call" | custom-call | flops 3145728 | bytes 3145728 | tf_op jit(solution)/shard_map/flipped/pallas_call | solution.py:545
  38.9 5.6 %back_projected.1.back_ref = bf16[8,800,128]{2,1,0:T(8,128)(2,1)} custom-call(bf16[48,1024]{1,0:T(8,128)(2,1)} %copy-done.9, bf16[768,1024]{1,0:T(8,128)(2,1)} %bitcast.31, bf16[48,1024]{1,0:T(8,128)(2,1)} %copy-done.10, bf16[1024,1024]{1,0:T(8,128)(2,1)} %w_ref.1), custom_call_target="tpu_custom_call" | custom-call | flops 1610612736 | bytes 6291456 | tf_op jit(solution)/shard_map/back_projected/pallas_call | solution.py:246
  44.5 6.8 %all-to-all-done.sums_ref = f32[32,3,1024]{2,1,0:T(4,128)} async-done(((f32[32,3,1024]{2,1,0:T(4,128)}), f32[32,3,1024]{2,1,0:T(4,128)}, u32[]{:S(2)}, u32[]{:S(2)}) %all-to-all-start) | async-done | bytes 393248 | tf_op jit(solution)/shard_map/all_to_all | solution.py:703
  51.3 5.8 %swish.1 = (bf16[768,1024]{1,0:T(8,128)(2,1)}, bf16[8,800,128]{2,1,0:T(8,128)(2,1)}, f32[32,2,1024]{2,1,0:T(2,128)}) custom-call(s32[2]{0:T(128)S(1)} %pad_add_fusion.span_ref, f32[32,3,1024]{2,1,0:T(4,128)} %all-to-all-done.sums_ref, f32[1,1024]{1,0:T(1,128)} %bitcast.37, f32[1,1024]{1,0:T(1,128)} %bitcast.42, ...), custom_call_target="tpu_custom_call" | custom-call | flops 23592960 | bytes 11010048 | tf_op jit(solution)/shard_map/swish/pallas_call | solution.py:319
  57.1 4.6 %weight_term.1 = (bf16[512,1024]{1,0:T(8,128)(2,1)}, bf16[512,1024]{1,0:T(8,128)(2,1)S(1)}) custom-call(s32[1]{0:T(128)} %bitcast.5.core_ref, bf16[768,1024]{1,0:T(8,128)(2,1)} %get-tuple-element.62.left_ref, bf16[1,768,1024]{2,1,0:T(8,128)(2,1)} %right_ref.1), custom_call_target="tpu_custom_call" | custom-call | tf_op jit(solution)/shard_map/weight_term/pallas_call | solution.py:607
  63.2 3.1 %all-to-all-start.1 = ((f32[32,2,1024]{2,1,0:T(2,128)}), f32[32,2,1024]{2,1,0:T(2,128)S(1)}, u32[]{:S(2)}, u32[]{:S(2)}) async-start(f32[32,2,1024]{2,1,0:T(2,128)} %get-tuple-element.61), calls=%async_computation.1 | async-start | bytes 524288 | tf_op jit(solution)/shard_map/all_to_all | solution.py:703
  66.3 5.0 %convolution_convert_fusion = bf16[768,1024]{1,0:T(8,128)(2,1)} fusion(bf16[768,1024]{1,0:T(8,128)(2,1)} %get-tuple-element.62.left_ref, bf16[1024,1024]{1,0:T(8,128)(2,1)} %w_ref.1), kind=kOutput, calls=%fused_computation.1 | convolution fusion | flops 1611399168 | bytes 5242880 | tf_op jit(solution)/shard_map/dot_general | solution.py:30
  71.3 1.7 %combine.1 = (bf16[256,1024]{1,0:T(8,128)(2,1)S(1)}, bf16[256,1024]{1,0:T(8,128)(2,1)S(1)}) custom-call(s32[1]{0:T(128)} %bitcast.8.half_ref, bf16[512,1024]{1,0:T(8,128)(2,1)} %copy-done, bf16[512,1024]{1,0:T(8,128)(2,1)} %collective-permute-done.2.got_other.got_mine, bf16[512,1024]{1,0:T(8,128)(2,1)} %copy-done, ...), custom_call_target="tpu_custom_call" | custom-call | tf_op jit(solution)/shard_map/combine/pallas_call | solution.py:657
  74.7 2.2 %all-to-all-done.1.terms_ref = f32[32,2,1024]{2,1,0:T(2,128)S(1)} async-done(((f32[32,2,1024]{2,1,0:T(2,128)}), f32[32,2,1024]{2,1,0:T(2,128)S(1)}, u32[]{:S(2)}, u32[]{:S(2)}) %all-to-all-start.1) | async-done | bytes 262176 | tf_op jit(solution)/shard_map/all_to_all | solution.py:703
  77.6 7.3 %norm_grad.2 = (bf16[2,768,512]{2,1,0:T(8,128)(2,1)}, bf16[4,768,128]{2,1,0:T(8,128)(2,1)}) custom-call(s32[2]{0:T(128)S(1)} %pad_add_fusion.span_ref, f32[32,3,1024]{2,1,0:T(4,128)} %all-to-all-done.sums_ref, f32[32,2,1024]{2,1,0:T(2,128)} %copy-done.6, f32[1,1024]{1,0:T(1,128)} %bitcast.38, f32[31,1024]{1,0:T(8,128)} %taps_ref.5, ...), custom_call_target="tpu_custom_call" | custom-call | flops 27525120 | bytes 6291456 | tf_op jit(solution)/shard_map/norm_grad/pallas_call | solution.py:397
  88.5 7.2 %norm_grad.3 = (bf16[2,768,512]{2,1,0:T(8,128)(2,1)}, bf16[4,768,128]{2,1,0:T(8,128)(2,1)}) custom-call(s32[2]{0:T(128)S(1)} %pad_add_fusion.span_ref, f32[32,3,1024]{2,1,0:T(4,128)} %all-to-all-done.sums_ref, f32[32,2,1024]{2,1,0:T(2,128)} %copy-done.6, f32[1,1024]{1,0:T(1,128)} %bitcast.39, f32[31,1024]{1,0:T(8,128)} %taps_ref.5, ...), custom_call_target="tpu_custom_call" | custom-call | flops 27525120 | bytes 6291456 | tf_op jit(solution)/shard_map/norm_grad/pallas_call | solution.py:397
  96.7 3.9 %pair_term.2 = (bf16[256,1024]{1,0:T(8,128)(2,1)S(1)}, bf16[256,1024]{1,0:T(8,128)(2,1)S(1)}) custom-call(s32[1]{0:T(128)} %bitcast.8.half_ref, bf16[512,768]{1,0:T(8,128)(2,1)} %get-tuple-element.68.left_own, bf16[512,768]{1,0:T(8,128)(2,1)} %collective-permute-done.3.left_got, bf16[2,768,512]{2,1,0:T(8,128)(2,1)} %get-tuple-element.96.own_ref.refs_0_, ...), custom_call_target="tpu_custom_call" | custom-call | flops 1610612736 | bytes 6291456 | tf_op jit(solution)/shard_map/pair_term/pallas_call | solution.py:572
  102.7 3.9 %pair_term.3 = (bf16[256,1024]{1,0:T(8,128)(2,1)S(1)}, bf16[256,1024]{1,0:T(8,128)(2,1)S(1)}) custom-call(s32[1]{0:T(128)} %bitcast.8.half_ref, bf16[512,768]{1,0:T(8,128)(2,1)} %get-tuple-element.68.left_own, bf16[512,768]{1,0:T(8,128)(2,1)} %collective-permute-done.3.left_got, bf16[2,768,512]{2,1,0:T(8,128)(2,1)} %get-tuple-element.97.own_ref.refs_1_, ...), custom_call_target="tpu_custom_call" | custom-call | flops 1610612736 | bytes 6291456 | tf_op jit(solution)/shard_map/pair_term/pallas_call | solution.py:572
  108.8 9.4 %tap_grad.1 = f32[8,32,128]{2,1,0:T(8,128)} custom-call(bf16[8,64,128]{2,1,0:T(8,128)(2,1)} %get-tuple-element.76.edge_ref, bf16[8,768,128]{2,1,0:T(8,128)(2,1)} %get-tuple-element.84.glu_ref, bf16[4,768,128]{2,1,0:T(8,128)(2,1)} %get-tuple-element.85.refs_0_, bf16[4,768,128]{2,1,0:T(8,128)(2,1)} %get-tuple-element.86.refs_1_), custom_call_target="tpu_custom_call" | custom-call | flops 48758784 | bytes 3145728 | tf_op jit(solution)/shard_map/tap_grad/pallas_call | solution.py:477
  120.4 3.3 %all-to-all-start.2 = ((f32[32,8,128]{2,1,0:T(8,128)}), f32[32,8,128]{2,1,0:T(8,128)S(1)}, u32[]{:S(2)}, u32[]{:S(2)}) async-start(f32[32,8,128]{2,1,0:T(8,128)} %bitcast.10), calls=%async_computation.2 | async-start | bytes 262144 | tf_op jit(solution)/shard_map/all_to_all | solution.py:703
  123.8 5.0 %collective-permute-done.11 = bf16[128,2048]{1,0:T(8,128)(2,1)S(1)} collective-permute-done((bf16[128,2048]{1,0:T(8,128)(2,1)S(1)}, bf16[128,2048]{1,0:T(8,128)(2,1)S(1)}, u32[]{:S(2)}, u32[]{:S(2)}) %collective-permute-start.11) | collective-permute-done | bytes 524320 | tf_op jit(solution)/shard_map/ppermute | solution.py:678
  131.8 4.2 %collective-permute-done.13 = bf16[32,1024]{1,0:T(8,128)(2,1)S(1)} collective-permute-done((bf16[32,1024]{1,0:T(8,128)(2,1)S(1)}, bf16[32,1024]{1,0:T(8,128)(2,1)S(1)}, u32[]{:S(2)}, u32[]{:S(2)}) %collective-permute-start.13) | collective-permute-done | bytes 65568 | tf_op jit(solution)/shard_map/ppermute | solution.py:678
  137.5 3.6 %all-to-all-start.3 = ((f32[32,8,128]{2,1,0:T(8,128)}), f32[32,8,128]{2,1,0:T(8,128)S(1)}, u32[]{:S(2)}, u32[]{:S(2)}) async-start(f32[32,8,128]{2,1,0:T(8,128)} %broadcast_in_dim.22), calls=%async_computation.3 | async-start | bytes 262144 | tf_op jit(solution)/shard_map/all_to_all | solution.py:703
  141.2 2.7 %collective-permute-start.14 = (bf16[32,2048]{1,0:T(8,128)(2,1)S(1)}, bf16[32,2048]{1,0:T(8,128)(2,1)S(1)}, u32[]{:S(2)}, u32[]{:S(2)}) collective-permute-start(bf16[32,2048]{1,0:T(8,128)(2,1)S(1)} %broadcast_select_fusion.4), channel_id=1, source_target_pairs={{0,16},{1,17},{2,18},{3,19},{4,20},{5,21},{6,22},{7,23},{8,24},{9,... | collective-permute-start | bytes 393224 | tf_op jit(solution)/shard_map/ppermute | solution.py:678
  143.9 7.5 %frames_grad.1 = bf16[768,1024]{1,0:T(8,128)(2,1)} custom-call(bf16[2,768,512]{2,1,0:T(8,128)(2,1)} %get-tuple-element.96.own_ref.refs_0_, bf16[2,768,512]{2,1,0:T(8,128)(2,1)} %get-tuple-element.97.own_ref.refs_1_, bf16[1024,2048]{1,0:T(8,128)(2,1)} %refs_2_.1), custom_call_target="tpu_custom_call" | custom-call | flops 3221225472 | bytes 7864320 | tf_op jit(solution)/shard_map/frames_grad/pallas_call | solution.py:515
  (78 shorter events, 26.2 us)
Async XLA Ops:
  1.5 12.1 %collective-permute-start = (bf16[48,1024]{1,0:T(8,128)(2,1)S(1)}, bf16[48,1024]{1,0:T(8,128)(2,1)S(1)}, u32[]{:S(2)}, u32[]{:S(2)}) collective-permute-start(bf16[48,1024]{1,0:T(8,128)(2,1)S(1)} %get-tuple-element.54), channel_id=1, source_target_pairs={{0,1},{1,2},{2,3},{4,5},{5,6},{6,7},{8,9},{9,10},{10,11},{12,13},{... | collective-permute-start | bytes 294920 | tf_op jit(solution)/shard_map/ppermute | solution.py:726
  3.9 9.8 %collective-permute-start.1 = (bf16[48,1024]{1,0:T(8,128)(2,1)S(1)}, bf16[48,1024]{1,0:T(8,128)(2,1)S(1)}, u32[]{:S(2)}, u32[]{:S(2)}) collective-permute-start(bf16[48,1024]{1,0:T(8,128)(2,1)S(1)} %get-tuple-element.55), channel_id=1, source_target_pairs={{1,0},{2,1},{3,2},{5,4},{6,5},{7,6},{9,8},{10,9},{11,10},{13,12},{... | collective-permute-start | bytes 294920 | tf_op jit(solution)/shard_map/ppermute | solution.py:727
  26.4 24.9 %all-to-all-start = ((f32[32,3,1024]{2,1,0:T(4,128)}), f32[32,3,1024]{2,1,0:T(4,128)}, u32[]{:S(2)}, u32[]{:S(2)}) async-start(f32[32,3,1024]{2,1,0:T(4,128)} %get-tuple-element.57), calls=%async_computation | async-start | bytes 1048576 | tf_op jit(solution)/shard_map/all_to_all | solution.py:703
  61.8 1.0 copy-start
  62.7 8.6 %collective-permute-start.2 = (bf16[512,1024]{1,0:T(8,128)(2,1)}, bf16[512,1024]{1,0:T(8,128)(2,1)}, u32[]{:S(2)}, u32[]{:S(2)}) collective-permute-start(bf16[512,1024]{1,0:T(8,128)(2,1)} %get-tuple-element.64), channel_id=1, source_target_pairs={{0,1},{1,0},{2,3},{3,2},{4,5},{5,4},{6,7},{7,6},{8,9},{9,8},{10,11... | collective-permute-start | bytes 3145736 | tf_op jit(solution)/shard_map/ppermute | solution.py:741
  62.7 14.2 %collective-permute-start.3 = (bf16[512,768]{1,0:T(8,128)(2,1)}, bf16[512,768]{1,0:T(8,128)(2,1)}, u32[]{:S(2)}, u32[]{:S(2)}) collective-permute-start(bf16[512,768]{1,0:T(8,128)(2,1)} %get-tuple-element.66), channel_id=1, source_target_pairs={{0,1},{1,0},{2,3},{3,2},{4,5},{5,4},{6,7},{7,6},{8,9},{9,8},{10,11... | collective-permute-start | bytes 2359304 | tf_op jit(solution)/shard_map/ppermute | solution.py:735
  63.2 13.7 %all-to-all-start.1 = ((f32[32,2,1024]{2,1,0:T(2,128)}), f32[32,2,1024]{2,1,0:T(2,128)S(1)}, u32[]{:S(2)}, u32[]{:S(2)}) async-start(f32[32,2,1024]{2,1,0:T(2,128)} %get-tuple-element.61), calls=%async_computation.1 | async-start | bytes 524288 | tf_op jit(solution)/shard_map/all_to_all | solution.py:703
  76.9 9.5 %collective-permute-start.5 = (bf16[256,1024]{1,0:T(8,128)(2,1)}, bf16[256,1024]{1,0:T(8,128)(2,1)}, u32[]{:S(2)}, u32[]{:S(2)}) collective-permute-start(bf16[256,1024]{1,0:T(8,128)(2,1)} %copy-done.3), channel_id=1, source_target_pairs={{0,2},{1,5},{2,0},{3,7},{4,6},{5,1},{6,4},{7,3},{8,10},{9,13},{10,... | collective-permute-start | bytes 1572872 | tf_op jit(solution)/shard_map/ppermute | solution.py:678
  77.6 8.8 %copy-start.2 = (bf16[256,1024]{1,0:T(8,128)(2,1)S(1)}, bf16[256,1024]{1,0:T(8,128)(2,1)}, u32[]{:S(2)}) copy-start(bf16[256,1024]{1,0:T(8,128)(2,1)} %copy-done.1) | copy-start | bytes 1572868
  84.9 11.8 %collective-permute-start.4 = (bf16[2,768,512]{2,1,0:T(8,128)(2,1)}, bf16[2,768,512]{2,1,0:T(8,128)(2,1)}, u32[]{:S(2)}, u32[]{:S(2)}) collective-permute-start(bf16[2,768,512]{2,1,0:T(8,128)(2,1)} %get-tuple-element.96.own_ref.refs_0_), channel_id=1, source_target_pairs={{0,1},{1,0},{2,3},{3,2},{4,5},{5,4},{6,7},{7,6},{8,9},{9,8},{10,11... | collective-permute-start | bytes 4718600 | tf_op jit(solution)/shard_map/ppermute | solution.py:753
  95.7 5.8 %collective-permute-start.7 = (bf16[2,768,512]{2,1,0:T(8,128)(2,1)}, bf16[2,768,512]{2,1,0:T(8,128)(2,1)S(1)}, u32[]{:S(2)}, u32[]{:S(2)}) collective-permute-start(bf16[2,768,512]{2,1,0:T(8,128)(2,1)} %get-tuple-element.97.own_ref.refs_1_), channel_id=1, source_target_pairs={{0,1},{1,0},{2,3},{3,2},{4,5},{5,4},{6,7},{7,6},{8,9},{9,8},{10,11... | collective-permute-start | bytes 4718600 | tf_op jit(solution)/shard_map/ppermute | solution.py:753
  95.8 12.1 %collective-permute-start.6 = (bf16[128,1024]{1,0:T(8,128)(2,1)S(1)}, bf16[128,1024]{1,0:T(8,128)(2,1)S(1)}, u32[]{:S(2)}, u32[]{:S(2)}) collective-permute-start(bf16[128,1024]{1,0:T(8,128)(2,1)S(1)} %broadcast_select_fusion.1), channel_id=1, source_target_pairs={{0,4},{1,3},{2,6},{3,1},{4,0},{5,7},{6,2},{7,5},{8,12},{9,11},{10,... | collective-permute-start | bytes 786440 | tf_op jit(solution)/shard_map/ppermute | solution.py:678
  100.7 7.2 %copy-start.5 = (bf16[256,1024]{1,0:T(8,128)(2,1)S(1)}, bf16[256,1024]{1,0:T(8,128)(2,1)}, u32[]{:S(2)}) copy-start(bf16[256,1024]{1,0:T(8,128)(2,1)} %copy-done.4) | copy-start | bytes 1572868
  100.7 17.6 %collective-permute-start.8 = (bf16[256,1024]{1,0:T(8,128)(2,1)S(1)}, bf16[256,1024]{1,0:T(8,128)(2,1)S(1)}, u32[]{:S(2)}, u32[]{:S(2)}) collective-permute-start(bf16[256,1024]{1,0:T(8,128)(2,1)S(1)} %get-tuple-element.80), channel_id=1, source_target_pairs={{0,2},{1,5},{2,0},{3,7},{4,6},{5,1},{6,4},{7,3},{8,10},{9,13},{10,... | collective-permute-start | bytes 1572872 | tf_op jit(solution)/shard_map/ppermute | solution.py:678
  101.6 1.1 copy-start.8
  106.6 11.6 %collective-permute-start.9 = (bf16[256,1024]{1,0:T(8,128)(2,1)S(1)}, bf16[256,1024]{1,0:T(8,128)(2,1)S(1)}, u32[]{:S(2)}, u32[]{:S(2)}) collective-permute-start(bf16[256,1024]{1,0:T(8,128)(2,1)S(1)} %get-tuple-element.83), channel_id=1, source_target_pairs={{0,2},{1,5},{2,0},{3,7},{4,6},{5,1},{6,4},{7,3},{8,10},{9,13},{10,... | collective-permute-start | bytes 1572872 | tf_op jit(solution)/shard_map/ppermute | solution.py:678
  108.0 10.2 %collective-permute-start.10 = (bf16[64,1024]{1,0:T(8,128)(2,1)S(1)}, bf16[64,1024]{1,0:T(8,128)(2,1)S(1)}, u32[]{:S(2)}, u32[]{:S(2)}) collective-permute-start(bf16[64,1024]{1,0:T(8,128)(2,1)S(1)} %broadcast_select_fusion.3), channel_id=1, source_target_pairs={{0,8},{1,9},{2,10},{3,11},{4,12},{5,13},{6,14},{7,15},{8,0},{9,1},... | collective-permute-start | bytes 393224 | tf_op jit(solution)/shard_map/ppermute | solution.py:678
  118.6 1.6 %copy-start.7 = (f32[32,2,1024]{2,1,0:T(2,128)S(1)}, f32[32,2,1024]{2,1,0:T(2,128)}, u32[]{:S(2)}) copy-start(f32[32,2,1024]{2,1,0:T(2,128)} %copy-done.6) | copy-start | bytes 786436
  118.8 9.9 %collective-permute-start.11 = (bf16[128,2048]{1,0:T(8,128)(2,1)S(1)}, bf16[128,2048]{1,0:T(8,128)(2,1)S(1)}, u32[]{:S(2)}, u32[]{:S(2)}) collective-permute-start(bf16[128,2048]{1,0:T(8,128)(2,1)S(1)} %broadcast_select_fusion), channel_id=1, source_target_pairs={{0,4},{1,3},{2,6},{3,1},{4,0},{5,7},{6,2},{7,5},{8,12},{9,11},{10,... | collective-permute-start | bytes 1572872 | tf_op jit(solution)/shard_map/ppermute | solution.py:678
  120.4 15.7 %all-to-all-start.2 = ((f32[32,8,128]{2,1,0:T(8,128)}), f32[32,8,128]{2,1,0:T(8,128)S(1)}, u32[]{:S(2)}, u32[]{:S(2)}) async-start(f32[32,8,128]{2,1,0:T(8,128)} %bitcast.10), calls=%async_computation.2 | async-start | bytes 262144 | tf_op jit(solution)/shard_map/all_to_all | solution.py:703
  129.0 7.7 %collective-permute-start.12 = (bf16[64,2048]{1,0:T(8,128)(2,1)S(1)}, bf16[64,2048]{1,0:T(8,128)(2,1)S(1)}, u32[]{:S(2)}, u32[]{:S(2)}) collective-permute-start(bf16[64,2048]{1,0:T(8,128)(2,1)S(1)} %broadcast_select_fusion.2), channel_id=1, source_target_pairs={{0,8},{1,9},{2,10},{3,11},{4,12},{5,13},{6,14},{7,15},{8,0},{9,1},... | collective-permute-start | bytes 786440 | tf_op jit(solution)/shard_map/ppermute | solution.py:678
  130.7 5.3 %collective-permute-start.13 = (bf16[32,1024]{1,0:T(8,128)(2,1)S(1)}, bf16[32,1024]{1,0:T(8,128)(2,1)S(1)}, u32[]{:S(2)}, u32[]{:S(2)}) collective-permute-start(bf16[32,1024]{1,0:T(8,128)(2,1)S(1)} %broadcast_select_fusion.5), channel_id=1, source_target_pairs={{0,16},{1,17},{2,18},{3,19},{4,20},{5,21},{6,22},{7,23},{8,24},{9,... | collective-permute-start | bytes 196616 | tf_op jit(solution)/shard_map/ppermute | solution.py:678
  137.5 17.2 %all-to-all-start.3 = ((f32[32,8,128]{2,1,0:T(8,128)}), f32[32,8,128]{2,1,0:T(8,128)S(1)}, u32[]{:S(2)}, u32[]{:S(2)}) async-start(f32[32,8,128]{2,1,0:T(8,128)} %broadcast_in_dim.22), calls=%async_computation.3 | async-start | bytes 262144 | tf_op jit(solution)/shard_map/all_to_all | solution.py:703
  141.2 12.2 %collective-permute-start.14 = (bf16[32,2048]{1,0:T(8,128)(2,1)S(1)}, bf16[32,2048]{1,0:T(8,128)(2,1)S(1)}, u32[]{:S(2)}, u32[]{:S(2)}) collective-permute-start(bf16[32,2048]{1,0:T(8,128)(2,1)S(1)} %broadcast_select_fusion.4), channel_id=1, source_target_pairs={{0,16},{1,17},{2,18},{3,19},{4,20},{5,21},{6,22},{7,23},{8,24},{9,... | collective-permute-start | bytes 393224 | tf_op jit(solution)/shard_map/ppermute | solution.py:678
  (6 other events, 4.4 us)
